TPU v7x, 512 devices: a whole 4x8x8 slice. The times are simulated.
512 devices in a mesh: len: 16 (over x_lo, y), height: 32 (over x_hi, z, core).
Axes of the slice: x: 4 (x_hi: 2, x_lo: 2; x = x_hi * 2 + x_lo), y: 8, z: 8, core: 2. Of those that a mesh axis runs over, the one named last changes fastest.
Arguments:
- position: float32 [3, 262144], P(None, ('len', 'height')), may hold values from -6 to 6
- velocity: float32 [3, 262144], P(None, ('len', 'height')), may hold values from -4 to 4
- tangent_pos: float32 [3, 32, 262144], P(None, None, ('len', 'height')), may hold values from -6 to 6
- tangent_vel: float32 [3, 32, 262144], P(None, None, ('len', 'height')), may hold values from -6 to 6
- mass: float32 [262144], P(('len', 'height')), may hold values from 0.5 to 2
- load_basis: float32 [3, 32, 262144], P(None, None, ('len', 'height')), may hold values from -2 to 2
- params: float32 [32], replicated, may hold values from -4 to 4
- stiffness: float32 [12, 262144], P(None, ('len', 'height')), may hold values from 0.5 to 2
- rest_length: float32 [12, 262144], P(None, ('len', 'height')), may hold values from 0.5 to 1.5
- neighbours: int32 [12, 262144], P(None, ('len', 'height')), may hold values from 0 to 1599, as said below
- intact: int32 [12, 262144], P(None, ('len', 'height')), may hold values 0 or 1
- face_lists: int32 [4, 131072], P(None, ('len', 'height')), may hold values from 0 to 511, as said below
- corner_lists: int32 [4, 8192], P(None, ('len', 'height')), may hold values from 0 to 511, as said below
- owned: int32 [512], P(('len', 'height')), may hold values from 256 to 512, as said below
Outputs:
- position_out: float32 [3, 262144], P(None, ('len', 'height'))
- velocity_out: float32 [3, 262144], P(None, ('len', 'height'))
- tangent_pos_out: float32 [3, 32, 262144], P(None, None, ('len', 'height'))
- tangent_vel_out: float32 [3, 32, 262144], P(None, None, ('len', 'height'))
Inputs may be any that keep to these rules, and one draw needn't show every extreme that they name: `owned`: debris makes particle counts differ up to twofold between devices; at least one device is full. `neighbours`: an entry below 512 names a live particle of the same device; an entry 512 + f * 256 + g names row g of face block f, and an entry 1536 + c * 16 + g row g of diagonal block c; a ghost entry occurs only where the device it comes from exists. `face_lists`: every entry names a live particle of the sending device. `corner_lists`: every entry names a live particle of the sending device.
All inputs are finite; a program needn't handle non-finite values. No bound on the sum of `intact` on one device may be relied on, other than what follows from the above.
Results may differ from a plain program's by a relative error of at most 0.0001.
Values sent between devices are 32-bit elements; how exact they have to be, the bound alone decides.
No kernel may reach another device: no remote copies, remote signals or barrier semaphores. Data moves between devices by JAX's collectives and lax.ppermute only.
A program may use at most 64 MiB of HBM per device.

v0:
```python
import jax
import jax.numpy as jnp
from jax import lax
from jax.sharding import PartitionSpec as P

STEPS = 2


face_dirs = ((-1, 0), (0, -1), (0, 1), (1, 0))
corner_dirs = ((-1, -1), (-1, 1), (1, -1), (1, 1))


def extended(cells, sides, width):
    for axis, dim in sides:
        count = lax.axis_size(axis)
        ends = count - 1
        head = lax.slice_in_dim(cells, 0, width, axis=dim)
        tail = lax.slice_in_dim(cells, cells.shape[dim] - width, cells.shape[dim], axis=dim)
        cells = jnp.concatenate(
            [
                lax.ppermute(tail, axis, [(i, (i + 1) % count) for i in range(ends)]),
                cells,
                lax.ppermute(head, axis, [((i + 1) % count, i) for i in range(ends)]),
            ],
            axis=dim,
        )
    return cells


def bond_terms(rows, state, weights, stiffness, rest_length):
    columns = state.shape[1] // 3
    own = state.reshape(1, state.shape[0], 3, columns)
    rows = rows.reshape(rows.shape[0], rows.shape[1], 3, columns)
    delta = rows[:, :, :, 0] - own[:, :, :, 0]
    dtang = rows[:, :, :, 1:] - own[:, :, :, 1:]
    radius = jnp.sqrt(jnp.sum(delta * delta, axis=2) + 0.25)
    scaled = stiffness * (1.0 - rest_length / radius)
    curved = stiffness * rest_length / (radius * radius * radius)
    along_dir = jnp.sum(delta[:, :, :, None] * dtang, axis=2)
    force = jnp.sum((weights * scaled)[:, :, None] * delta, axis=0)
    dforce = jnp.sum(
        weights[:, :, None, None]
        * (
            scaled[:, :, None, None] * dtang
            + (curved[:, :, None] * along_dir)[:, :, None, :] * delta[:, :, :, None]
        ),
        axis=0,
    )
    return (force, dforce)


def route_rows(state, face_lists, corner_lists):
    width = face_lists.shape[1]
    small = corner_lists.shape[1]
    blocks = {}
    for index, pair in enumerate(face_dirs):
        blocks[pair] = jnp.take(state, face_lists[index], axis=0)
    for index, pair in enumerate(corner_dirs):
        blocks[pair] = jnp.take(state, corner_lists[index], axis=0)
    arrived = {}
    center = jnp.zeros_like(blocks[face_dirs[0]])
    layout = [[center, center, center], [center, center, center], [center, center, center]]
    for pair in face_dirs:
        layout[1 + pair[0]][1 + pair[1]] = blocks[pair]
    for pair in corner_dirs:
        layout[1 + pair[0]][1 + pair[1]] = jnp.pad(blocks[pair], ((0, width - small), (0, 0)))
    stacked = jnp.stack([jnp.stack(column) for column in layout])
    padded = extended(stacked, (("len", 0), ("height", 1)), 1)
    for pair in face_dirs:
        arrived[pair] = padded[2 - 2 * pair[0], 2 - 2 * pair[1]]
    for pair in corner_dirs:
        arrived[pair] = padded[2 - 2 * pair[0], 2 - 2 * pair[1]][:small]
    return [arrived[pair] for pair in face_dirs] + [arrived[pair] for pair in corner_dirs]


def on_device(
    position,
    velocity,
    tangent_pos,
    tangent_vel,
    mass,
    load_basis,
    params,
    stiffness,
    rest_length,
    neighbours,
    intact,
    face_lists,
    corner_lists,
    owned,
):
    count = position.shape[1]
    bonds = neighbours.shape[0]
    tang = tangent_pos.shape[1]
    live = (lax.iota(jnp.int32, count) < owned[0]).astype(jnp.float32)
    weights = intact.astype(jnp.float32) * live[None, :]
    external = jnp.einsum("cpn,p->cn", load_basis, params, precision=lax.Precision.HIGHEST)
    flat_index = neighbours.reshape(-1)
    for step in range(STEPS):
        joined = jnp.concatenate([position[:, None, :], tangent_pos], axis=1)
        state = jnp.transpose(joined, (2, 0, 1)).reshape(count, 3 * (tang + 1))
        received = route_rows(state, face_lists, corner_lists)
        table = jnp.concatenate([state] + received, axis=0)
        rows = jnp.take(table, flat_index, axis=0)
        rows = rows.reshape(bonds, count, 3 * (tang + 1))
        force, dforce = bond_terms(rows, state, weights, stiffness, rest_length)
        force = jnp.transpose(force, (1, 0))
        dforce = jnp.transpose(dforce, (1, 2, 0))
        velocity = velocity + 0.05 * ((force + external) / mass[None, :])
        position = position + 0.05 * velocity
        tangent_vel = tangent_vel + 0.05 * ((dforce + load_basis) / mass[None, None, :])
        tangent_pos = tangent_pos + 0.05 * tangent_vel
    return (position, velocity, tangent_pos, tangent_vel)


def solution(mesh):
    placed = (
        P(None, ("len", "height")),
        P(None, ("len", "height")),
        P(None, None, ("len", "height")),
        P(None, None, ("len", "height")),
        P(("len", "height")),
        P(None, None, ("len", "height")),
        P(),
        P(None, ("len", "height")),
        P(None, ("len", "height")),
        P(None, ("len", "height")),
        P(None, ("len", "height")),
        P(None, ("len", "height")),
        P(None, ("len", "height")),
        P(("len", "height")),
    )
    return jax.shard_map(
        on_device,
        mesh=mesh,
        in_specs=placed,
        out_specs=(
            P(None, ("len", "height")),
            P(None, ("len", "height")),
            P(None, None, ("len", "height")),
            P(None, None, ("len", "height")),
        ),
        check_vma=False,
    )
```

profile of v0, /device:TPU:22, one launch (start us, length us, event | category | flops | bytes accessed | tf_op | source)
XLA Modules:
  0.0 172.0 jit_solution(8039930849525902098)
XLA Ops:
  0.6 0.8 fusion.34
  1.5 0.8 compare_and_fusion.5
  2.4 0.7 copy.48
  3.1 1.0 fusion.4
  5.7 0.7 gather_fusion.4
  6.5 0.8 maximum_bitcast_fusion.1
  7.3 3.5 %collective-permute-start.1 = (f32[1,3,256,99]{3,2,1,0:T(8,128)}, f32[1,3,256,99]{3,2,1,0:T(8,128)S(1)}, u32[]{:S(2)}, u32[]{:S(2)}) collective-permute-start(f32[1,3,256,99]{3,2,1,0:T(8,128)} %maximum_bitcast_fusion.1), channel_id=1, source_target_pairs={{0,32},{32,64},{64,96},{96,128},{128,160},{160,192},{192,224},{224... | collective-permute-start | bytes 912392 | tf_op jit(solution)/shard_map/ppermute | solution.py:21
  12.2 0.7 gather_fusion.1
  13.1 0.8 maximum_bitcast_fusion
  13.9 2.4 %collective-permute-start = (f32[1,3,256,99]{3,2,1,0:T(8,128)}, f32[1,3,256,99]{3,2,1,0:T(8,128)S(1)}, u32[]{:S(2)}, u32[]{:S(2)}) collective-permute-start(f32[1,3,256,99]{3,2,1,0:T(8,128)} %maximum_bitcast_fusion), channel_id=1, source_target_pairs={{32,0},{64,32},{96,64},{128,96},{160,128},{192,160},{224,192},{256... | collective-permute-start | bytes 912392 | tf_op jit(solution)/shard_map/ppermute | solution.py:23
  16.4 0.7 gather_fusion.7
  17.1 0.7 gather_fusion.6
  18.7 0.8 fusion.23
  19.7 0.6 collective-permute-done.1
  20.5 7.1 %collective-permute-done = f32[1,3,256,99]{3,2,1,0:T(8,128)S(1)} collective-permute-done((f32[1,3,256,99]{3,2,1,0:T(8,128)}, f32[1,3,256,99]{3,2,1,0:T(8,128)S(1)}, u32[]{:S(2)}, u32[]{:S(2)}) %collective-permute-start) | collective-permute-done | bytes 304160 | tf_op jit(solution)/shard_map/ppermute | solution.py:23
  27.6 0.7 copy-done.11
  28.5 1.1 copy.57
  29.6 10.3 %collective-permute-start.2 = (f32[5,1,256,99]{2,1,3,0:T(1,128)}, f32[5,1,256,99]{2,1,3,0:T(1,128)}, u32[]{:S(2)}, u32[]{:S(2)}) collective-permute-start(f32[5,1,256,99]{2,1,3,0:T(1,128)} %copy.57), channel_id=1, source_target_pairs={{1,0},{2,1},{3,2},{4,3},{5,4},{6,5},{7,6},{8,7},{9,8},{10,9},{11,1... | collective-permute-start | bytes 1520648 | tf_op jit(solution)/shard_map/ppermute | solution.py:23
  40.0 0.6 copy.59
  40.6 1.9 %collective-permute-start.3 = (f32[5,1,256,99]{2,1,3,0:T(1,128)S(1)}, f32[5,1,256,99]{2,1,3,0:T(1,128)S(1)}, u32[]{:S(2)}, u32[]{:S(2)}) collective-permute-start(f32[5,1,256,99]{2,1,3,0:T(1,128)S(1)} %copy.59), channel_id=1, source_target_pairs={{0,1},{1,2},{2,3},{3,4},{4,5},{5,6},{6,7},{7,8},{8,9},{9,10},{10,1... | collective-permute-start | bytes 1520648 | tf_op jit(solution)/shard_map/ppermute | solution.py:21
  42.5 0.6 fusion.22
  43.1 0.9 fusion.15
  44.0 2.7 %collective-permute-done.2 = f32[5,1,256,99]{2,1,3,0:T(1,128)} collective-permute-done((f32[5,1,256,99]{2,1,3,0:T(1,128)}, f32[5,1,256,99]{2,1,3,0:T(1,128)}, u32[]{:S(2)}, u32[]{:S(2)}) %collective-permute-start.2) | collective-permute-done | bytes 506912 | tf_op jit(solution)/shard_map/ppermute | solution.py:23
  46.8 0.9 slice.238
  47.8 6.7 %collective-permute-done.3 = f32[5,1,256,99]{2,1,3,0:T(1,128)S(1)} collective-permute-done((f32[5,1,256,99]{2,1,3,0:T(1,128)S(1)}, f32[5,1,256,99]{2,1,3,0:T(1,128)S(1)}, u32[]{:S(2)}, u32[]{:S(2)}) %collective-permute-start.3) | collective-permute-done | bytes 506912 | tf_op jit(solution)/shard_map/ppermute | solution.py:21
  54.6 0.8 fusion.33
  55.9 20.9 %gather_fusion.8 = f32[6144,99]{1,0:T(8,128)} fusion(f32[1600,99]{1,0:T(8,128)S(1)} %constant_dynamic-update-slice_fusion.4, s32[6144]{0:T(1024)S(1)} %fusion.18), kind=kCustom, calls=%fused_computation.2.clone | custom fusion | bytes 4890624 | tf_op jit(solution)/shard_map/jit(_take)/gather | solution.py:104
  76.9 4.7 %broadcast_select_fusion.1 = f32[6144,99]{1,0:T(8,128)S(1)} fusion(f32[6144,99]{1,0:T(8,128)} %gather_fusion.8, pred[6144]{0:T(1024)(128)(4,1)S(1)} %compare_and_fusion), kind=kLoop, calls=%fused_computation.25 | loop fusion | flops 608256 | bytes 4872192 | tf_op jit(solution)/shard_map/jit(_take)/select_n | solution.py:104
  81.5 2.3 %copy.66 = f32[6144,99]{0,1:T(8,128)} copy(f32[6144,99]{1,0:T(8,128)S(1)} %broadcast_select_fusion.1) | data formatting | bytes 4866048 | tf_op jit(solution)/shard_map/jit(_take)/select_n | solution.py:104
  83.9 2.8 %reshape_reshape.12 = f32[12,512,3,33]{1,0,3,2:T(8,128)S(1)} reshape(f32[6144,99]{0,1:T(8,128)} %copy.66) | data formatting | bytes 4866048 | tf_op jit(solution)/shard_map/reshape;reshape | solution.py:33
  86.7 1.4 fusion.16
  88.2 1.3 fusion.21
  90.2 1.2 multiply_reduce_fusion.2
  91.5 0.7 copy-done.1
  92.3 0.7 copy-done.6
  93.2 0.9 gather_fusion.13
  94.1 0.7 gather_fusion.14
  94.8 0.7 gather_fusion.12
  95.5 0.9 gather_fusion.10
  96.4 0.7 gather_fusion.11
  97.0 0.7 gather_fusion.9
  97.7 0.9 gather_fusion.16
  98.6 0.9 gather_fusion.15
  99.8 4.5 %collective-permute-start.5 = (f32[1,3,256,99]{3,2,1,0:T(8,128)S(1)}, f32[1,3,256,99]{3,2,1,0:T(8,128)S(1)}, u32[]{:S(2)}, u32[]{:S(2)}) collective-permute-start(f32[1,3,256,99]{3,2,1,0:T(8,128)S(1)} %maximum_bitcast_fusion.4), channel_id=1, source_target_pairs={{0,32},{32,64},{64,96},{96,128},{128,160},{160,192},{192,224},{224... | collective-permute-start | bytes 912392 | tf_op jit(solution)/shard_map/ppermute | solution.py:21
  104.8 1.9 %collective-permute-start.4 = (f32[1,3,256,99]{3,2,1,0:T(8,128)S(1)}, f32[1,3,256,99]{3,2,1,0:T(8,128)S(1)}, u32[]{:S(2)}, u32[]{:S(2)}) collective-permute-start(f32[1,3,256,99]{3,2,1,0:T(8,128)S(1)} %maximum_bitcast_fusion.3), channel_id=1, source_target_pairs={{32,0},{64,32},{96,64},{128,96},{160,128},{192,160},{224,192},{256... | collective-permute-start | bytes 912392 | tf_op jit(solution)/shard_map/ppermute | solution.py:23
  106.9 2.8 %collective-permute-done.5 = f32[1,3,256,99]{3,2,1,0:T(8,128)S(1)} collective-permute-done((f32[1,3,256,99]{3,2,1,0:T(8,128)S(1)}, f32[1,3,256,99]{3,2,1,0:T(8,128)S(1)}, u32[]{:S(2)}, u32[]{:S(2)}) %collective-permute-start.5) | collective-permute-done | bytes 304160 | tf_op jit(solution)/shard_map/ppermute | solution.py:21
  109.8 4.7 %collective-permute-done.4 = f32[1,3,256,99]{3,2,1,0:T(8,128)S(1)} collective-permute-done((f32[1,3,256,99]{3,2,1,0:T(8,128)S(1)}, f32[1,3,256,99]{3,2,1,0:T(8,128)S(1)}, u32[]{:S(2)}, u32[]{:S(2)}) %collective-permute-start.4) | collective-permute-done | bytes 304160 | tf_op jit(solution)/shard_map/ppermute | solution.py:23
  114.6 0.6 copy.76
  115.3 3.7 %collective-permute-start.6 = (f32[5,1,256,99]{2,1,3,0:T(1,128)S(1)}, f32[5,1,256,99]{2,1,3,0:T(1,128)}, u32[]{:S(2)}, u32[]{:S(2)}) collective-permute-start(f32[5,1,256,99]{2,1,3,0:T(1,128)S(1)} %copy.76), channel_id=1, source_target_pairs={{1,0},{2,1},{3,2},{4,3},{5,4},{6,5},{7,6},{8,7},{9,8},{10,9},{11,1... | collective-permute-start | bytes 1520648 | tf_op jit(solution)/shard_map/ppermute | solution.py:23
  119.0 1.1 copy.78
  120.1 2.1 %collective-permute-start.7 = (f32[5,1,256,99]{2,1,3,0:T(1,128)}, f32[5,1,256,99]{2,1,3,0:T(1,128)}, u32[]{:S(2)}, u32[]{:S(2)}) collective-permute-start(f32[5,1,256,99]{2,1,3,0:T(1,128)} %copy.78), channel_id=1, source_target_pairs={{0,1},{1,2},{2,3},{3,4},{4,5},{5,6},{6,7},{7,8},{8,9},{9,10},{10,1... | collective-permute-start | bytes 1520648 | tf_op jit(solution)/shard_map/ppermute | solution.py:21
  122.3 3.2 %collective-permute-done.6 = f32[5,1,256,99]{2,1,3,0:T(1,128)} collective-permute-done((f32[5,1,256,99]{2,1,3,0:T(1,128)S(1)}, f32[5,1,256,99]{2,1,3,0:T(1,128)}, u32[]{:S(2)}, u32[]{:S(2)}) %collective-permute-start.6) | collective-permute-done | bytes 506912 | tf_op jit(solution)/shard_map/ppermute | solution.py:23
  125.5 0.9 slice.252
  126.5 7.9 %collective-permute-done.7 = f32[5,1,256,99]{2,1,3,0:T(1,128)} collective-permute-done((f32[5,1,256,99]{2,1,3,0:T(1,128)}, f32[5,1,256,99]{2,1,3,0:T(1,128)}, u32[]{:S(2)}, u32[]{:S(2)}) %collective-permute-start.7) | collective-permute-done | bytes 506912 | tf_op jit(solution)/shard_map/ppermute | solution.py:21
  134.4 0.9 slice.254
  135.4 0.8 fusion.31
  136.3 0.8 fusion.30
  137.5 20.9 %gather_fusion.17 = f32[6144,99]{1,0:T(8,128)} fusion(f32[1600,99]{1,0:T(8,128)S(1)} %constant_dynamic-update-slice_fusion.13, s32[6144]{0:T(1024)S(1)} %fusion.18), kind=kCustom, calls=%fused_computation.17.clone | custom fusion | bytes 4890624 | tf_op jit(solution)/shard_map/jit(_take)/gather | solution.py:104
  158.4 4.7 %broadcast_select_fusion = f32[6144,99]{1,0:T(8,128)S(1)} fusion(f32[6144,99]{1,0:T(8,128)} %gather_fusion.17, pred[6144]{0:T(1024)(128)(4,1)S(1)} %copy-done.17), kind=kLoop, calls=%fused_computation.24 | loop fusion | flops 608256 | bytes 4872192 | tf_op jit(solution)/shard_map/jit(_take)/select_n | solution.py:104
  163.1 2.3 %copy.85 = f32[6144,99]{0,1:T(8,128)} copy(f32[6144,99]{1,0:T(8,128)S(1)} %broadcast_select_fusion) | data formatting | bytes 4866048 | tf_op jit(solution)/shard_map/jit(_take)/select_n | solution.py:104
  165.4 2.8 %reshape_reshape.14 = f32[12,512,3,33]{1,0,3,2:T(8,128)S(1)} reshape(f32[6144,99]{0,1:T(8,128)} %copy.85) | data formatting | bytes 4866048 | tf_op jit(solution)/shard_map/reshape;reshape | solution.py:33
  169.2 1.2 multiply_reduce_fusion
  170.4 0.8 multiply_add_fusion
  171.3 0.6 multiply_add_fusion.2
  (206 shorter events, 8.1 us)
Async XLA Ops:
  0.6 18.1 %copy-start = (f32[32]{0:T(128)S(1)}, f32[32]{0:T(128)}, u32[]{:S(2)}) copy-start(f32[32]{0:T(128)} %param.26) | copy-start | bytes 388
  1.5 11.5 %copy-start.38 = (pred[256]{0:T(512)(128)(4,1)}, pred[256]{0:T(512)(128)(4,1)S(1)}, u32[]{:S(2)}) copy-start(pred[256]{0:T(512)(128)(4,1)S(1)} %compare_and_fusion.4) | copy-start | bytes 772
  2.4 8.4 %copy-start.34 = (pred[16]{0:T(512)(128)(4,1)}, pred[16]{0:T(512)(128)(4,1)S(1)}, u32[]{:S(2)}) copy-start(pred[16]{0:T(512)(128)(4,1)S(1)} %get-tuple-element.20) | copy-start | bytes 52
  2.4 10.7 %copy-start.30 = (pred[16]{0:T(512)(128)(4,1)}, pred[16]{0:T(512)(128)(4,1)S(1)}, u32[]{:S(2)}) copy-start(pred[16]{0:T(512)(128)(4,1)S(1)} %get-tuple-element.54) | copy-start | bytes 52
  2.4 10.7 %copy-start.32 = (pred[16]{0:T(512)(128)(4,1)}, pred[16]{0:T(512)(128)(4,1)S(1)}, u32[]{:S(2)}) copy-start(pred[16]{0:T(512)(128)(4,1)S(1)} %get-tuple-element.52) | copy-start | bytes 52
  2.4 10.7 %copy-start.36 = (pred[16]{0:T(512)(128)(4,1)}, pred[16]{0:T(512)(128)(4,1)S(1)}, u32[]{:S(2)}) copy-start(pred[16]{0:T(512)(128)(4,1)S(1)} %get-tuple-element.56) | copy-start | bytes 52
  4.1 12.2 %copy-start.20 = (s32[12,512]{1,0:T(8,128)S(1)}, s32[12,512]{1,0:T(8,128)}, u32[]{:S(2)}) copy-start(s32[12,512]{1,0:T(8,128)} %param.29) | copy-start | bytes 73732
  4.3 0.6 copy-start.27
  4.3 1.3 copy-start.26
  5.7 5.8 %copy-start.23 = (s32[1024]{0:T(1024)}, s32[1024]{0:T(1024)S(1)}, u32[]{:S(2)}) copy-start(s32[1024]{0:T(1024)S(1)} %get-tuple-element.64) | copy-start | bytes 12292
  5.7 11.5 %copy-start.22 = (s32[1024]{0:T(1024)}, s32[1024]{0:T(1024)S(1)}, u32[]{:S(2)}) copy-start(s32[1024]{0:T(1024)S(1)} %get-tuple-element.65) | copy-start | bytes 12292
  6.5 12.2 %copy-start.3 = (f32[3,32,512]{2,1,0:T(8,128)S(1)}, f32[3,32,512]{2,1,0:T(8,128)}, u32[]{:S(2)}) copy-start(f32[3,32,512]{2,1,0:T(8,128)} %param.25) | copy-start | bytes 589828
  7.3 12.9 %collective-permute-start.1 = (f32[1,3,256,99]{3,2,1,0:T(8,128)}, f32[1,3,256,99]{3,2,1,0:T(8,128)S(1)}, u32[]{:S(2)}, u32[]{:S(2)}) collective-permute-start(f32[1,3,256,99]{3,2,1,0:T(8,128)} %maximum_bitcast_fusion.1), channel_id=1, source_target_pairs={{0,32},{32,64},{64,96},{96,128},{128,160},{160,192},{192,224},{224... | collective-permute-start | bytes 912392 | tf_op jit(solution)/shard_map/ppermute | solution.py:21
  10.8 5.5 %copy-start.40 = (pred[256]{0:T(512)(128)(4,1)}, pred[256]{0:T(512)(128)(4,1)S(1)}, u32[]{:S(2)}) copy-start(pred[256]{0:T(512)(128)(4,1)S(1)} %compare_and_fusion.7) | copy-start | bytes 772
  10.8 0.6 copy-start.29
  10.8 5.5 %copy-start.28 = (s32[1024]{0:T(1024)}, s32[1024]{0:T(1024)S(1)}, u32[]{:S(2)}) copy-start(s32[1024]{0:T(1024)S(1)} %get-tuple-element.61) | copy-start | bytes 12292
  13.9 13.7 %collective-permute-start = (f32[1,3,256,99]{3,2,1,0:T(8,128)}, f32[1,3,256,99]{3,2,1,0:T(8,128)S(1)}, u32[]{:S(2)}, u32[]{:S(2)}) collective-permute-start(f32[1,3,256,99]{3,2,1,0:T(8,128)} %maximum_bitcast_fusion), channel_id=1, source_target_pairs={{32,0},{64,32},{96,64},{128,96},{160,128},{192,160},{224,192},{256... | collective-permute-start | bytes 912392 | tf_op jit(solution)/shard_map/ppermute | solution.py:23
  16.2 4.2 %copy-start.44 = (pred[256]{0:T(512)(128)(4,1)}, pred[256]{0:T(512)(128)(4,1)S(1)}, u32[]{:S(2)}) copy-start(pred[256]{0:T(512)(128)(4,1)S(1)} %compare_and_fusion.1) | copy-start | bytes 772
  16.3 4.2 %copy-start.42 = (pred[256]{0:T(512)(128)(4,1)}, pred[256]{0:T(512)(128)(4,1)S(1)}, u32[]{:S(2)}) copy-start(pred[256]{0:T(512)(128)(4,1)S(1)} %compare_and_fusion.2) | copy-start | bytes 772
  16.4 60.5 %copy-start.16 = (pred[6144]{0:T(1024)(128)(4,1)}, pred[6144]{0:T(1024)(128)(4,1)S(1)}, u32[]{:S(2)}) copy-start(pred[6144]{0:T(1024)(128)(4,1)S(1)} %compare_and_fusion) | copy-start | bytes 18436
  16.4 1.5 copy-start.24
  16.4 1.5 copy-start.25
  18.7 9.7 %copy-start.46 = (f32[3]{0:T(128)}, f32[3]{0:T(128)S(1)}, u32[]{:S(2)}) copy-start(f32[3]{0:T(128)S(1)} %pad.45.clone) | copy-start | bytes 40
  27.6 0.7 copy-start.11
  29.6 17.2 %collective-permute-start.2 = (f32[5,1,256,99]{2,1,3,0:T(1,128)}, f32[5,1,256,99]{2,1,3,0:T(1,128)}, u32[]{:S(2)}, u32[]{:S(2)}) collective-permute-start(f32[5,1,256,99]{2,1,3,0:T(1,128)} %copy.57), channel_id=1, source_target_pairs={{1,0},{2,1},{3,2},{4,3},{5,4},{6,5},{7,6},{8,7},{9,8},{10,9},{11,1... | collective-permute-start | bytes 1520648 | tf_op jit(solution)/shard_map/ppermute | solution.py:23
  40.6 13.9 %collective-permute-start.3 = (f32[5,1,256,99]{2,1,3,0:T(1,128)S(1)}, f32[5,1,256,99]{2,1,3,0:T(1,128)S(1)}, u32[]{:S(2)}, u32[]{:S(2)}) collective-permute-start(f32[5,1,256,99]{2,1,3,0:T(1,128)S(1)} %copy.59), channel_id=1, source_target_pairs={{0,1},{1,2},{2,3},{3,4},{4,5},{5,6},{6,7},{7,8},{8,9},{9,10},{10,1... | collective-permute-start | bytes 1520648 | tf_op jit(solution)/shard_map/ppermute | solution.py:21
  83.9 2.9 %copy-start.12 = (f32[12,512]{1,0:T(8,128)S(1)}, f32[12,512]{1,0:T(8,128)}, u32[]{:S(2)}) copy-start(f32[12,512]{1,0:T(8,128)} %param.27) | copy-start | bytes 73732
  83.9 4.3 %copy-start.15 = (f32[3,512]{1,0:T(4,128)S(1)}, f32[3,512]{1,0:T(4,128)}, u32[]{:S(2)}) copy-start(f32[3,512]{1,0:T(4,128)} %param.20) | copy-start | bytes 18436
  83.9 4.3 %copy-start.19 = (f32[512]{0:T(512)S(1)}, f32[512]{0:T(512)}, u32[]{:S(2)}) copy-start(f32[512]{0:T(512)} %param.24) | copy-start | bytes 6148
  90.1 2.1 %copy-start.4 = (f32[3,32,512]{2,1,0:T(8,128)S(1)}, f32[3,32,512]{2,1,0:T(8,128)}, u32[]{:S(2)}) copy-start(f32[3,32,512]{2,1,0:T(8,128)} %param.25) | copy-start | bytes 589828
  90.1 2.1 %copy-start.8 = (f32[3,32,512]{2,1,0:T(8,128)S(1)}, f32[3,32,512]{2,1,0:T(8,128)}, u32[]{:S(2)}) copy-start(f32[3,32,512]{2,1,0:T(8,128)} %param.22) | copy-start | bytes 589828
  90.1 2.1 %copy-start.9 = (f32[3,32,512]{2,1,0:T(8,128)S(1)}, f32[3,32,512]{2,1,0:T(8,128)}, u32[]{:S(2)}) copy-start(f32[3,32,512]{2,1,0:T(8,128)} %param.23) | copy-start | bytes 589828
  91.5 0.7 copy-start.1
  92.3 0.7 copy-start.6
  93.0 6.5 %copy-start.39 = (pred[256]{0:T(512)(128)(4,1)S(1)}, pred[256]{0:T(512)(128)(4,1)}, u32[]{:S(2)}) copy-start(pred[256]{0:T(512)(128)(4,1)} %copy-done.38) | copy-start | bytes 772
  93.0 6.6 %copy-start.37 = (pred[16]{0:T(512)(128)(4,1)S(1)}, pred[16]{0:T(512)(128)(4,1)}, u32[]{:S(2)}) copy-start(pred[16]{0:T(512)(128)(4,1)} %copy-done.36) | copy-start | bytes 52
  93.0 6.7 %copy-start.35 = (pred[16]{0:T(512)(128)(4,1)S(1)}, pred[16]{0:T(512)(128)(4,1)}, u32[]{:S(2)}) copy-start(pred[16]{0:T(512)(128)(4,1)} %copy-done.34) | copy-start | bytes 52
  93.2 11.2 %copy-start.41 = (pred[256]{0:T(512)(128)(4,1)S(1)}, pred[256]{0:T(512)(128)(4,1)}, u32[]{:S(2)}) copy-start(pred[256]{0:T(512)(128)(4,1)} %copy-done.40) | copy-start | bytes 772
  93.2 11.3 %copy-start.33 = (pred[16]{0:T(512)(128)(4,1)S(1)}, pred[16]{0:T(512)(128)(4,1)}, u32[]{:S(2)}) copy-start(pred[16]{0:T(512)(128)(4,1)} %copy-done.32) | copy-start | bytes 52
  93.2 11.4 %copy-start.31 = (pred[16]{0:T(512)(128)(4,1)S(1)}, pred[16]{0:T(512)(128)(4,1)}, u32[]{:S(2)}) copy-start(pred[16]{0:T(512)(128)(4,1)} %copy-done.30) | copy-start | bytes 52
  94.1 10.6 %copy-start.45 = (pred[256]{0:T(512)(128)(4,1)S(1)}, pred[256]{0:T(512)(128)(4,1)}, u32[]{:S(2)}) copy-start(pred[256]{0:T(512)(128)(4,1)} %copy-done.44) | copy-start | bytes 772
  95.5 11.3 %copy-start.43 = (pred[256]{0:T(512)(128)(4,1)S(1)}, pred[256]{0:T(512)(128)(4,1)}, u32[]{:S(2)}) copy-start(pred[256]{0:T(512)(128)(4,1)} %copy-done.42) | copy-start | bytes 772
  98.6 11.1 %copy-start.47 = (f32[3]{0:T(128)S(1)}, f32[3]{0:T(128)}, u32[]{:S(2)}) copy-start(f32[3]{0:T(128)} %copy-done.46) | copy-start | bytes 40
  99.8 9.8 %collective-permute-start.5 = (f32[1,3,256,99]{3,2,1,0:T(8,128)S(1)}, f32[1,3,256,99]{3,2,1,0:T(8,128)S(1)}, u32[]{:S(2)}, u32[]{:S(2)}) collective-permute-start(f32[1,3,256,99]{3,2,1,0:T(8,128)S(1)} %maximum_bitcast_fusion.4), channel_id=1, source_target_pairs={{0,32},{32,64},{64,96},{96,128},{128,160},{160,192},{192,224},{224... | collective-permute-start | bytes 912392 | tf_op jit(solution)/shard_map/ppermute | solution.py:21
  104.8 9.7 %collective-permute-start.4 = (f32[1,3,256,99]{3,2,1,0:T(8,128)S(1)}, f32[1,3,256,99]{3,2,1,0:T(8,128)S(1)}, u32[]{:S(2)}, u32[]{:S(2)}) collective-permute-start(f32[1,3,256,99]{3,2,1,0:T(8,128)S(1)} %maximum_bitcast_fusion.3), channel_id=1, source_target_pairs={{32,0},{64,32},{96,64},{128,96},{160,128},{192,160},{224,192},{256... | collective-permute-start | bytes 912392 | tf_op jit(solution)/shard_map/ppermute | solution.py:23
  115.3 10.2 %collective-permute-start.6 = (f32[5,1,256,99]{2,1,3,0:T(1,128)S(1)}, f32[5,1,256,99]{2,1,3,0:T(1,128)}, u32[]{:S(2)}, u32[]{:S(2)}) collective-permute-start(f32[5,1,256,99]{2,1,3,0:T(1,128)S(1)} %copy.76), channel_id=1, source_target_pairs={{1,0},{2,1},{3,2},{4,3},{5,4},{6,5},{7,6},{8,7},{9,8},{10,9},{11,1... | collective-permute-start | bytes 1520648 | tf_op jit(solution)/shard_map/ppermute | solution.py:23
  120.1 14.2 %collective-permute-start.7 = (f32[5,1,256,99]{2,1,3,0:T(1,128)}, f32[5,1,256,99]{2,1,3,0:T(1,128)}, u32[]{:S(2)}, u32[]{:S(2)}) collective-permute-start(f32[5,1,256,99]{2,1,3,0:T(1,128)} %copy.78), channel_id=1, source_target_pairs={{0,1},{1,2},{2,3},{3,4},{4,5},{5,6},{6,7},{7,8},{8,9},{9,10},{10,1... | collective-permute-start | bytes 1520648 | tf_op jit(solution)/shard_map/ppermute | solution.py:21
  137.5 20.9 %copy-start.17 = (pred[6144]{0:T(1024)(128)(4,1)S(1)}, pred[6144]{0:T(1024)(128)(4,1)}, u32[]{:S(2)}) copy-start(pred[6144]{0:T(1024)(128)(4,1)} %copy-done.16) | copy-start | bytes 18436
  168.2 0.8 copy-start.13
  168.2 0.8 copy-start.14
  169.0 1.4 copy-start.2
  169.0 1.4 copy-start.5
  169.0 1.4 copy-start.7
  169.0 1.4 copy-start.10
  169.1 2.2 %copy-start.18 = (f32[1,3,512]{2,0,1:T(1,128)S(1)}, f32[1,3,512]{2,0,1:T(1,128)}, u32[]{:S(2)}) copy-start(f32[1,3,512]{2,0,1:T(1,128)} %fusion.23) | copy-start | bytes 18436
  169.1 2.2 %copy-start.21 = (f32[3,512]{1,0:T(4,128)S(1)}, f32[3,512]{1,0:T(4,128)}, u32[]{:S(2)}) copy-start(f32[3,512]{1,0:T(4,128)} %get-tuple-element.14) | copy-start | bytes 18436
where the time goes:
time: 173 us; the launch traced here: 172 us
  local copies, waits for them, and re-layouts  79.2 us (46%)
  waiting for transfers between devices  35.6 us (21%)
  starting transfers between devices  30.4 us (18%)
  other arithmetic  23.5 us (14%)
  between operations  2.59 us (1%)
    gather x2, local copies, waits for them, and re-layouts, on_device(): rows = jnp.take(table, flat_index, axis=0)  41.8 us
    ppermute x4, starting transfers between devices, extended(): lax.ppermute(head, axis, [((i + 1) % count, i) for i in range(ends)])  18.3 us
    ppermute x4, waiting for transfers between devices, extended(): lax.ppermute(tail, axis, [(i, (i + 1) % count) for i in range(ends)])  17.9 us
    ppermute x4, waiting for transfers between devices, extended(): lax.ppermute(head, axis, [((i + 1) % count, i) for i in range(ends)])  17.6 us
    ppermute x4, starting transfers between devices, extended(): lax.ppermute(tail, axis, [(i, (i + 1) % count) for i in range(ends)])  12 us
    select_n x2, other arithmetic, on_device(): rows = jnp.take(table, flat_index, axis=0)  9.32 us
    gather x8, local copies, waits for them, and re-layouts, route_rows(): blocks[pair] = jnp.take(state, face_lists[index], axis=0)  6.39 us
    another operation x2, local copies, waits for them, and re-layouts, bond_terms(): rows = rows.reshape(rows.shape[0], rows.shape[1], 3, columns)  5.55 us
  transfers between devices with their start and end apart: 8, of which 8 were waited for; matrix products, arithmetic and copies ran while one was open for 7% of the time, Pallas kernels for 0%

commit v1 on v0

v1 whole, which is shorter than its diff:
```python
import jax
import jax.numpy as jnp
from jax import lax
from jax.experimental import pallas as pl
from jax.experimental.pallas import tpu as pltpu
from jax.sharding import PartitionSpec as P

STEPS = 2
DT = 0.05
FACE = 256
CORNER = 16
MESSAGE = FACE + 128
ROWS = 104
AXES = ("len", "height")
PARAMS = pltpu.CompilerParams(vmem_limit_bytes=16 * 2**20)


def matching(strips, levels, along, odd):
    pairs = []
    for l in range(strips):
        for h in range(levels):
            place, size = (l, strips) if along == 0 else (h, levels)
            other = place + 1 if place % 2 == odd else place - 1
            if 0 <= other < size:
                pairs.append((l * levels + h, other * levels + h if along == 0 else l * levels + other))
    return pairs


def halves(table):
    high = table.astype(jnp.bfloat16).astype(jnp.float32)
    return jnp.concatenate([high, table - high], axis=0).astype(jnp.bfloat16)


def one_hot(index, rows):
    lanes = index.shape[1]
    wanted = jnp.broadcast_to(index, (16, lanes)).astype(jnp.int16)
    base = lax.broadcasted_iota(jnp.int16, (16, lanes), 0)
    one = jnp.ones((16, lanes), jnp.bfloat16)
    zero = jnp.zeros((16, lanes), jnp.bfloat16)
    parts = [jnp.where(wanted == base + jnp.int16(first), one, zero) for first in range(0, rows, 16)]
    return jnp.concatenate(parts, axis=0)


def pick(table, index):
    both = jnp.dot(table, one_hot(index, table.shape[1]), preferred_element_type=jnp.float32)
    return both[:ROWS] + both[ROWS:]


def stacked(tangent, position):
    lanes = position.shape[1]
    tang = tangent.shape[0] * tangent.shape[1]
    flat = tangent.reshape(tang, lanes)
    return jnp.concatenate([flat, position, jnp.zeros((ROWS - tang - 3, lanes), jnp.float32)], axis=0)


def pack(table, sends, first, second, third, fourth):
    first[...] = pick(table, sends[0:1, :])
    second[...] = pick(table, sends[1:2, :])
    third[...] = pick(table, sends[2:3, :FACE])
    fourth[...] = pick(table, sends[3:4, :FACE])


def bonds_into(total, table, index, inside, tangent, position, stiffness, rest_length, intact, owned):
    count = position.shape[1]
    tang = tangent.shape[1]
    slot = lax.broadcasted_iota(jnp.int32, (1, count), 1)
    live = slot < owned
    own = [tangent[c] for c in range(3)]
    force = [total[3 * tang + c : 3 * tang + c + 1, :] for c in range(3)]
    for bond in range(index.shape[0]):
        rows = pick(table, index[bond : bond + 1, :])
        weight = jnp.where(live & inside[bond : bond + 1, :], intact[bond : bond + 1, :].astype(jnp.float32), 0.0)
        stiff = stiffness[bond : bond + 1, :] * weight
        rest = rest_length[bond : bond + 1, :]
        delta = [rows[3 * tang + c : 3 * tang + c + 1, :] - position[c : c + 1, :] for c in range(3)]
        inverse = lax.rsqrt(delta[0] * delta[0] + delta[1] * delta[1] + delta[2] * delta[2] + 0.25)
        scaled = stiff * (1.0 - rest * inverse)
        curved = stiff * rest * (inverse * inverse * inverse)
        dtang = [rows[c * tang : (c + 1) * tang, :] - own[c] for c in range(3)]
        along = delta[0] * dtang[0] + delta[1] * dtang[1] + delta[2] * dtang[2]
        for c in range(3):
            force[c] = force[c] + scaled * delta[c]
            total[c * tang : (c + 1) * tang, :] += scaled * dtang[c] + (curved * delta[c]) * along
    for c in range(3):
        total[3 * tang + c : 3 * tang + c + 1, :] = force[c]


def place_of(index, odd):
    own = index < 512
    face = (index - 512) >> 8
    is_corner = index >= 1536
    corner = (index - 1536) >> 4
    upward = jnp.where(is_corner, corner & 1, (face >> 1) & 1)
    forward = jnp.where(is_corner, corner >> 1, (face >> 1) & 1)
    second_l = jnp.where(forward == odd[0], 1, 0)
    second_h = jnp.where(upward == odd[1], 1, 0)
    on_l = (face == 0) | (face == 3)
    at_face = jnp.where(on_l, 512 + 256 * second_l, 1024 + 256 * second_h) + (index & 255)
    at_corner = 1536 + 32 * second_h + 16 * second_l + (index & 15)
    return jnp.where(own, index, jnp.where(is_corner, at_corner, at_face))


def pack_kernel(tangent, position, sends, first, second, third, fourth):
    table = halves(stacked(tangent[...], position[...]))
    pack(table, sends, first, second, third, fourth)


def own_kernel(odd, owned, params, tangent, position, basis, stiffness, rest_length, neighbours, intact, total):
    tang = tangent.shape[1]
    count = position.shape[1]
    for c in range(3):
        total[c * tang : (c + 1) * tang, :] = basis[c]
        outer = jnp.zeros((1, count), jnp.float32)
        for p in range(tang):
            outer = outer + params[p] * basis[c, p : p + 1, :]
        total[3 * tang + c : 3 * tang + c + 1, :] = outer
    total[3 * tang + 3 : ROWS, :] = jnp.zeros((ROWS - 3 * tang - 3, count), jnp.float32)
    table = halves(stacked(tangent[...], position[...]))
    index = neighbours[...]
    inside = index < 512
    bonds_into(total, table, index, inside, tangent, position, stiffness, rest_length, intact, owned[0])


def len_kernel(odd, owned, before, first, second, tangent, position, stiffness, rest_length, neighbours, intact, total):
    total[...] = before[...]
    table = halves(jnp.concatenate([first[:, :FACE], second[:, :FACE]], axis=1))
    index = place_of(neighbours[...], odd) - 512
    inside = (index >= 0) & (index < 512)
    bonds_into(total, table, index, inside, tangent, position, stiffness, rest_length, intact, owned[0])


def height_kernel(last):
    def body(odd, owned, before, third, fourth, tangent, position, tangent_vel, velocity, mass, stiffness, rest_length, neighbours, intact, sends, *outs):
        new_tangent, new_position, new_tangent_vel, new_velocity = outs[:4]
        total = outs[-1]
        tang = tangent.shape[1]
        total[...] = before[...]
        lane = lax.broadcasted_iota(jnp.int32, (ROWS, 128), 1)
        corners = jnp.where(lane < 32, third[:, FACE:], fourth[:, FACE:])
        table = halves(jnp.concatenate([third[:, :FACE], fourth[:, :FACE], corners], axis=1))
        index = place_of(neighbours[...], odd) - 1024
        inside = index >= 0
        bonds_into(total, table, index, inside, tangent, position, stiffness, rest_length, intact, owned[0])
        pace = DT / mass[...]
        for c in range(3):
            speed = tangent_vel[c] + pace * total[c * tang : (c + 1) * tang, :]
            new_tangent_vel[c] = speed
            new_tangent[c] = tangent[c] + DT * speed
        speed = velocity[...] + pace * total[3 * tang : 3 * tang + 3, :]
        new_velocity[...] = speed
        new_position[...] = position[...] + DT * speed
        if not last:
            table = halves(stacked(new_tangent[...], new_position[...]))
            pack(table, sends, *outs[4:8])

    return body


def cost(columns, bonds, moved):
    return pl.CostEstimate(flops=2 * 2 * ROWS * columns * bonds * 512, bytes_accessed=moved, transcendentals=0)


def f32(*shape):
    return jax.ShapeDtypeStruct(shape, jnp.float32)


VMEM = pl.BlockSpec(memory_space=pltpu.VMEM)
SMEM = pl.BlockSpec(memory_space=pltpu.SMEM)


def on_device(
    position,
    velocity,
    tangent_pos,
    tangent_vel,
    mass,
    load_basis,
    params,
    stiffness,
    rest_length,
    neighbours,
    intact,
    face_lists,
    corner_lists,
    owned,
):
    count = position.shape[1]
    bonds = neighbours.shape[0]
    strips, levels = lax.axis_size("len"), lax.axis_size("height")
    odd_l = lax.axis_index("len") % 2
    odd_h = lax.axis_index("height") % 2
    odd = jnp.stack([odd_l, odd_h]).astype(jnp.int32)
    mass = mass.reshape(1, count)

    def either(flag, yes, no):
        return jnp.where(flag == 1, yes, no)

    blank = jnp.full((CORNER,), -1, jnp.int32)
    rest_blank = jnp.full((64,), -1, jnp.int32)
    up = [either(odd_h, corner_lists[2 * a + 1], corner_lists[2 * a]) for a in range(2)]
    down = [either(odd_h, corner_lists[2 * a], corner_lists[2 * a + 1]) for a in range(2)]
    sends = jnp.stack(
        [
            jnp.concatenate([either(odd_l, face_lists[3], face_lists[0]), either(odd_l, up[1], up[0]), blank, either(odd_l, down[1], down[0]), blank, rest_blank]),
            jnp.concatenate([either(odd_l, face_lists[0], face_lists[3]), blank, either(odd_l, up[0], up[1]), blank, either(odd_l, down[0], down[1]), rest_blank]),
            jnp.concatenate([either(odd_h, face_lists[2], face_lists[1]), blank, blank, blank, blank, rest_blank]),
            jnp.concatenate([either(odd_h, face_lists[1], face_lists[2]), blank, blank, blank, blank, rest_blank]),
        ]
    )
    packed = (f32(ROWS, MESSAGE), f32(ROWS, MESSAGE), f32(ROWS, FACE), f32(ROWS, FACE))
    messages = pl.pallas_call(
        pack_kernel,
        out_shape=packed,
        compiler_params=PARAMS,
        cost_estimate=cost(512, 3, 700000),
        name="pack",
    )(tangent_pos, position, sends)
    for step in range(STEPS):
        last = step == STEPS - 1
        first = lax.ppermute(messages[0], AXES, matching(strips, levels, 0, 1))
        second = lax.ppermute(messages[1], AXES, matching(strips, levels, 0, 0))
        total = pl.pallas_call(
            own_kernel,
            out_shape=f32(ROWS, count),
            in_specs=[SMEM] * 3 + [VMEM] * 7,
            compiler_params=PARAMS,
            cost_estimate=cost(512, bonds, 1000000),
            name="own_bonds",
        )(odd, owned, params, tangent_pos, position, load_basis, stiffness, rest_length, neighbours, intact)
        corners = first[:, FACE:] + second[:, FACE:]
        third = lax.ppermute(jnp.concatenate([messages[2], corners], axis=1), AXES, matching(strips, levels, 1, 1))
        fourth = lax.ppermute(jnp.concatenate([messages[3], corners], axis=1), AXES, matching(strips, levels, 1, 0))
        total = pl.pallas_call(
            len_kernel,
            out_shape=f32(ROWS, count),
            in_specs=[SMEM] * 2 + [VMEM] * 9,
            compiler_params=PARAMS,
            cost_estimate=cost(512, bonds, 1000000),
            name="len_bonds",
        )(odd, owned, total, first, second, tangent_pos, position, stiffness, rest_length, neighbours, intact)
        state = (f32(*tangent_pos.shape), f32(*position.shape), f32(*tangent_pos.shape), f32(*position.shape))
        out = pl.pallas_call(
            height_kernel(last),
            out_shape=state if last else state + packed,
            in_specs=[SMEM] * 2 + [VMEM] * 13,
            scratch_shapes=[pltpu.VMEM((ROWS, count), jnp.float32)],
            compiler_params=PARAMS,
            cost_estimate=cost(640, bonds, 1500000),
            name="height_bonds",
        )(odd, owned, total, third, fourth, tangent_pos, position, tangent_vel, velocity, mass, stiffness, rest_length, neighbours, intact, sends)
        tangent_pos, position, tangent_vel, velocity = out[:4]
        messages = out[4:]
    return (position, velocity, tangent_pos, tangent_vel)


def solution(mesh):
    placed = (
        P(None, ("len", "height")),
        P(None, ("len", "height")),
        P(None, None, ("len", "height")),
        P(None, None, ("len", "height")),
        P(("len", "height")),
        P(None, None, ("len", "height")),
        P(),
        P(None, ("len", "height")),
        P(None, ("len", "height")),
        P(None, ("len", "height")),
        P(None, ("len", "height")),
        P(None, ("len", "height")),
        P(None, ("len", "height")),
        P(("len", "height")),
    )
    return jax.shard_map(
        on_device,
        mesh=mesh,
        in_specs=placed,
        out_specs=(
            P(None, ("len", "height")),
            P(None, ("len", "height")),
            P(None, None, ("len", "height")),
            P(None, None, ("len", "height")),
        ),
        check_vma=False,
    )
```

time: 173 us -> 65.2 us (0.38)
  the two profiles are of different devices: /device:TPU:22 before, /device:TPU:14 now
where the time goes in v1:
time: 65.2 us; the launch traced here: 64.8 us
  starting transfers between devices  33.6 us (52%)
  Pallas kernels  17.1 us (26%)
  waiting for transfers between devices  9.73 us (15%)
  local copies, waits for them, and re-layouts  2.52 us (4%)
  between operations  1.68 us (3%)
    ppermute x2, starting transfers between devices, on_device(): lax.ppermute(jnp.concatenate([messages[2], corners], axis=1), AXES, match...  15.7 us
    ppermute x2, starting transfers between devices, on_device(): first = lax.ppermute(messages[0], AXES, matching(strips, levels, 0, 1))  7.44 us
    pallas_call x2, Pallas kernels, on_device(): pl.pallas_call(height_kernel(last), out_shape=state if last else state +...  7.26 us
    ppermute x2, waiting for transfers between devices, on_device(): second = lax.ppermute(messages[1], AXES, matching(strips, levels, 0, 0))  7.02 us
    ppermute x2, starting transfers between devices, on_device(): second = lax.ppermute(messages[1], AXES, matching(strips, levels, 0, 0))  6.47 us
    pallas_call x2, Pallas kernels, on_device(): pl.pallas_call(own_kernel, out_shape=f32(ROWS, count), in_specs=[SMEM] *...  4.7 us
    pallas_call x2, Pallas kernels, on_device(): pl.pallas_call(len_kernel, out_shape=f32(ROWS, count), in_specs=[SMEM] *...  4.68 us
    ppermute x2, starting transfers between devices, on_device(): lax.ppermute(jnp.concatenate([messages[3], corners], axis=1), AXES, match...  3.97 us
  transfers between devices with their start and end apart: 8, of which 4 were waited for; matrix products, arithmetic and copies ran while one was open for 0% of the time, Pallas kernels for 14%

profile of v1, /device:TPU:14, one launch (start us, length us, event | category | flops | bytes accessed | tf_op | source)
XLA Modules:
  0.0 64.8 jit_solution(56660128301617173)
XLA Ops:
  0.6 0.0 copy-start.13
  0.7 0.0 copy-start.12
  0.7 0.7 %copy-done.13 = s32[4,16]{1,0:T(4,128)S(1)} copy-done((s32[4,16]{1,0:T(4,128)S(1)}, s32[4,16]{1,0:T(4,128)}, u32[]{:S(2)}) %copy-start.13) | copy-done | bytes 280
  1.3 0.0 copy-done.12
  1.4 0.1 concatenate.25
  1.5 0.1 concatenate.24
  1.6 0.0 copy-start.8
  1.6 0.7 %copy-done.8 = f32[3,512]{1,0:T(4,128)S(1)} copy-done((f32[3,512]{1,0:T(4,128)S(1)}, f32[3,512]{1,0:T(4,128)}, u32[]{:S(2)}) %copy-start.8) | copy-done | bytes 6168
  2.3 0.0 copy-start
  2.3 0.9 %copy-done = f32[3,32,512]{2,1,0:T(8,128)S(1)} copy-done((f32[3,32,512]{2,1,0:T(8,128)S(1)}, f32[3,32,512]{2,1,0:T(8,128)}, u32[]{:S(2)}) %copy-start) | copy-done | bytes 196632
  3.2 0.5 pack.1
  3.7 3.5 %collective-permute-start = (f32[104,384]{1,0:T(8,128)S(1)}, f32[104,384]{1,0:T(8,128)S(1)}, u32[]{:S(2)}, u32[]{:S(2)}) collective-permute-start(f32[104,384]{1,0:T(8,128)S(1)} %get-tuple-element.20), channel_id=1, source_target_pairs={{32,64},{33,65},{34,66},{35,67},{36,68},{37,69},{38,70},{39,71},{4... | collective-permute-start | bytes 479240 | tf_op jit(solution)/shard_map/ppermute | solution.py:220
  7.2 4.5 %collective-permute-start.1 = (f32[104,384]{1,0:T(8,128)S(1)}, f32[104,384]{1,0:T(8,128)S(1)}, u32[]{:S(2)}, u32[]{:S(2)}) collective-permute-start(f32[104,384]{1,0:T(8,128)S(1)} %get-tuple-element.21), channel_id=1, source_target_pairs={{0,32},{1,33},{2,34},{3,35},{4,36},{5,37},{6,38},{7,39},{8,40},{9,... | collective-permute-start | bytes 479240 | tf_op jit(solution)/shard_map/ppermute | solution.py:221
  12.4 0.1 pad_add_fusion.1.odd
  12.4 0.0 collective-permute-done.first
  12.4 3.1 %collective-permute-done.1.second = f32[104,384]{1,0:T(8,128)S(1)} collective-permute-done((f32[104,384]{1,0:T(8,128)S(1)}, f32[104,384]{1,0:T(8,128)S(1)}, u32[]{:S(2)}, u32[]{:S(2)}) %collective-permute-start.1) | collective-permute-done | bytes 159776 | tf_op jit(solution)/shard_map/ppermute | solution.py:221
  15.5 0.0 copy-start.1
  15.6 0.0 copy-start.3
  15.6 0.0 copy-start.4
  15.6 0.0 copy-start.5
  15.6 0.0 copy-start.6
  15.6 0.0 copy-start.7
  15.6 0.0 copy-start.11
  15.7 2.1 %collective-permute-start.3 = (f32[104,384]{1,0:T(8,128)S(1)}, f32[104,384]{1,0:T(8,128)S(1)}, u32[]{:S(2)}, u32[]{:S(2)}) collective-permute-start(f32[104,384]{1,0:T(8,128)S(1)} %get-tuple-element.38), channel_id=1, source_target_pairs={{0,1},{1,0},{2,3},{3,2},{4,5},{5,4},{6,7},{7,6},{8,9},{9,8},{10,11... | collective-permute-start | bytes 479240 | tf_op jit(solution)/shard_map/ppermute | solution.py:232
  17.7 11.6 %collective-permute-start.2 = (f32[104,384]{1,0:T(8,128)S(1)}, f32[104,384]{1,0:T(8,128)S(1)}, u32[]{:S(2)}, u32[]{:S(2)}) collective-permute-start(f32[104,384]{1,0:T(8,128)S(1)} %get-tuple-element.39), channel_id=1, source_target_pairs={{1,2},{2,1},{3,4},{4,3},{5,6},{6,5},{7,8},{8,7},{9,10},{10,9},{11,... | collective-permute-start | bytes 479240 | tf_op jit(solution)/shard_map/ppermute | solution.py:231
  29.3 0.0 copy-done.1
  29.3 0.0 copy-done.3
  29.3 0.0 copy-done.4
  29.4 0.0 copy-done.5
  29.4 0.0 copy-done.6
  29.4 0.0 copy-done.7
  29.4 0.0 copy-done.11
  29.4 2.3 %own_bonds.2.before = f32[104,512]{1,0:T(8,128)S(1)} custom-call(s32[2]{0:T(128)S(1)} %pad_add_fusion.1.odd, s32[1]{0:T(128)S(6)} %copy.18.owned, f32[32]{0:T(128)S(1)} %copy-done.11, f32[3,32,512]{2,1,0:T(8,128)S(1)} %copy-done.1, f32[3,512]{1,0:T(4,128)S(1)} %copy-done.8, f32[3,32,512]{2,1,0:T(8,128)S(1)} %copy-done.3, f32[12,512]{1,0:T(8,128)S(1)} %copy-done.4, ...), custom_call_target="tpu_custom_call" | custom-call | flops 1308622848 | bytes 1000000 | tf_op jit(solution)/shard_map/own_bonds/pallas_call | solution.py:222
  31.7 0.0 copy-start.2
  31.8 0.0 copy-start.9
  31.8 0.0 copy-start.10
  31.8 2.4 %len_bonds.2.before = f32[104,512]{1,0:T(8,128)S(1)} custom-call(s32[2]{0:T(128)S(1)} %pad_add_fusion.1.odd, s32[1]{0:T(128)S(6)} %copy.18.owned, f32[104,512]{1,0:T(8,128)S(1)} %own_bonds.2.before, f32[104,384]{1,0:T(8,128)S(1)} %collective-permute-done.first, f32[104,384]{1,0:T(8,128)S(1)} %collective-permute-done.1.second, f32[3,32,512]{2,1,0:T(8,128)S(1)} %copy-done.1, ...), custom_call_target="tpu_custom_call" | custom-call | flops 1308622848 | bytes 1000000 | tf_op jit(solution)/shard_map/len_bonds/pallas_call | solution.py:233
  34.2 0.0 collective-permute-done.3.fourth
  34.2 0.0 collective-permute-done.2.third
  34.2 0.0 copy-done.2
  34.2 0.0 copy-done.9
  34.2 0.0 copy-done.10
  34.2 3.5 %height_bonds.2 = (f32[3,32,512]{2,1,0:T(8,128)S(1)}, f32[3,512]{1,0:T(4,128)S(1)}, f32[3,32,512]{2,1,0:T(8,128)S(1)}, f32[3,512]{1,0:T(4,128)S(1)}, f32[104,384...) custom-call(s32[2]{0:T(128)S(1)} %pad_add_fusion.1.odd, ...), custom_call_target="tpu_custom_call" | custom-call | flops 1635778560 | bytes 1500000 | tf_op jit(solution)/shard_map/height_bonds/pallas_call | solution.py:242
  37.7 4.0 %collective-permute-start.4 = (f32[104,384]{1,0:T(8,128)S(1)}, f32[104,384]{1,0:T(8,128)S(1)}, u32[]{:S(2)}, u32[]{:S(2)}) collective-permute-start(f32[104,384]{1,0:T(8,128)S(1)} %get-tuple-element.26), channel_id=1, source_target_pairs={{32,64},{33,65},{34,66},{35,67},{36,68},{37,69},{38,70},{39,71},{4... | collective-permute-start | bytes 479240 | tf_op jit(solution)/shard_map/ppermute | solution.py:220
  41.7 2.0 %collective-permute-start.5 = (f32[104,384]{1,0:T(8,128)S(1)}, f32[104,384]{1,0:T(8,128)S(1)}, u32[]{:S(2)}, u32[]{:S(2)}) collective-permute-start(f32[104,384]{1,0:T(8,128)S(1)} %get-tuple-element.27), channel_id=1, source_target_pairs={{0,32},{1,33},{2,34},{3,35},{4,36},{5,37},{6,38},{7,39},{8,40},{9,... | collective-permute-start | bytes 479240 | tf_op jit(solution)/shard_map/ppermute | solution.py:221
  43.6 1.3 %collective-permute-done.4.first = f32[104,384]{1,0:T(8,128)S(1)} collective-permute-done((f32[104,384]{1,0:T(8,128)S(1)}, f32[104,384]{1,0:T(8,128)S(1)}, u32[]{:S(2)}, u32[]{:S(2)}) %collective-permute-start.4) | collective-permute-done | bytes 159776 | tf_op jit(solution)/shard_map/ppermute | solution.py:220
  44.9 3.9 %collective-permute-done.5.second = f32[104,384]{1,0:T(8,128)S(1)} collective-permute-done((f32[104,384]{1,0:T(8,128)S(1)}, f32[104,384]{1,0:T(8,128)S(1)}, u32[]{:S(2)}, u32[]{:S(2)}) %collective-permute-start.5) | collective-permute-done | bytes 159776 | tf_op jit(solution)/shard_map/ppermute | solution.py:221
  48.9 1.9 %collective-permute-start.7 = (f32[104,384]{1,0:T(8,128)S(1)}, f32[104,384]{1,0:T(8,128)S(1)}, u32[]{:S(2)}, u32[]{:S(2)}) collective-permute-start(f32[104,384]{1,0:T(8,128)S(1)} %get-tuple-element.36), channel_id=1, source_target_pairs={{0,1},{1,0},{2,3},{3,2},{4,5},{5,4},{6,7},{7,6},{8,9},{9,8},{10,11... | collective-permute-start | bytes 479240 | tf_op jit(solution)/shard_map/ppermute | solution.py:232
  50.8 4.1 %collective-permute-start.6 = (f32[104,384]{1,0:T(8,128)S(1)}, f32[104,384]{1,0:T(8,128)S(1)}, u32[]{:S(2)}, u32[]{:S(2)}) collective-permute-start(f32[104,384]{1,0:T(8,128)S(1)} %get-tuple-element.37), channel_id=1, source_target_pairs={{1,2},{2,1},{3,4},{4,3},{5,6},{6,5},{7,8},{8,7},{9,10},{10,9},{11,... | collective-permute-start | bytes 479240 | tf_op jit(solution)/shard_map/ppermute | solution.py:231
  54.9 2.3 %own_bonds.3.before = f32[104,512]{1,0:T(8,128)S(1)} custom-call(s32[2]{0:T(128)S(1)} %pad_add_fusion.1.odd, s32[1]{0:T(128)S(6)} %copy.18.owned, f32[32]{0:T(128)S(1)} %copy-done.11, f32[3,32,512]{2,1,0:T(8,128)S(1)} %get-tuple-element.24.tangent, f32[3,512]{1,0:T(4,128)S(1)} %get-tuple-element.25.position, f32[3,32,512]{2,1,0:T(8,128)S(1)} %copy-done.3, ...), custom_call_target="tpu_custom_call" | custom-call | flops 1308622848 | bytes 1000000 | tf_op jit(solution)/shard_map/own_bonds/pallas_call | solution.py:222
  57.3 2.3 %len_bonds.3.before = f32[104,512]{1,0:T(8,128)S(1)} custom-call(s32[2]{0:T(128)S(1)} %pad_add_fusion.1.odd, s32[1]{0:T(128)S(6)} %copy.18.owned, f32[104,512]{1,0:T(8,128)S(1)} %own_bonds.3.before, f32[104,384]{1,0:T(8,128)S(1)} %collective-permute-done.4.first, f32[104,384]{1,0:T(8,128)S(1)} %collective-permute-done.5.second, ...), custom_call_target="tpu_custom_call" | custom-call | flops 1308622848 | bytes 1000000 | tf_op jit(solution)/shard_map/len_bonds/pallas_call | solution.py:233
  59.6 0.0 collective-permute-done.7.fourth
  59.6 1.4 %collective-permute-done.6.third = f32[104,384]{1,0:T(8,128)S(1)} collective-permute-done((f32[104,384]{1,0:T(8,128)S(1)}, f32[104,384]{1,0:T(8,128)S(1)}, u32[]{:S(2)}, u32[]{:S(2)}) %collective-permute-start.6) | collective-permute-done | bytes 159776 | tf_op jit(solution)/shard_map/ppermute | solution.py:231
  61.0 3.8 %height_bonds.3 = (f32[3,32,512]{2,1,0:T(8,128)}, f32[3,512]{1,0:T(4,128)}, f32[3,32,512]{2,1,0:T(8,128)}, f32[3,512]{1,0:T(4,128)}) custom-call(s32[2]{0:T(128)S(1)} %pad_add_fusion.1.odd, s32[1]{0:T(128)S(6)} %copy.18.owned, f32[104,512]{1,0:T(8,128)S(1)} %len_bonds.3.before, f32[104,384]{1,0:T(8,128)S(1)} %collective-permute-done.6.third, ...), custom_call_target="tpu_custom_call" | custom-call | flops 1635778560 | bytes 1500000 | tf_op jit(solution)/shard_map/height_bonds/pallas_call | solution.py:242
  (15 shorter events, 0.1 us)
Async XLA Ops:
  0.6 0.7 %copy-start.13 = (s32[4,16]{1,0:T(4,128)S(1)}, s32[4,16]{1,0:T(4,128)}, u32[]{:S(2)}) copy-start(s32[4,16]{1,0:T(4,128)} %param.26) | copy-start | bytes 772
  0.7 0.7 %copy-start.12 = (s32[4,256]{1,0:T(4,128)S(1)}, s32[4,256]{1,0:T(4,128)}, u32[]{:S(2)}) copy-start(s32[4,256]{1,0:T(4,128)} %param.25) | copy-start | bytes 12292
  1.6 0.7 %copy-start.8 = (f32[3,512]{1,0:T(4,128)S(1)}, f32[3,512]{1,0:T(4,128)}, u32[]{:S(2)}) copy-start(f32[3,512]{1,0:T(4,128)} %position.7) | copy-start | bytes 18436
  2.3 0.9 %copy-start = (f32[3,32,512]{2,1,0:T(8,128)S(1)}, f32[3,32,512]{2,1,0:T(8,128)}, u32[]{:S(2)}) copy-start(f32[3,32,512]{2,1,0:T(8,128)} %tangent.7) | copy-start | bytes 589828
  3.7 8.7 %collective-permute-start = (f32[104,384]{1,0:T(8,128)S(1)}, f32[104,384]{1,0:T(8,128)S(1)}, u32[]{:S(2)}, u32[]{:S(2)}) collective-permute-start(f32[104,384]{1,0:T(8,128)S(1)} %get-tuple-element.20), channel_id=1, source_target_pairs={{32,64},{33,65},{34,66},{35,67},{36,68},{37,69},{38,70},{39,71},{4... | collective-permute-start | bytes 479240 | tf_op jit(solution)/shard_map/ppermute | solution.py:220
  7.2 8.3 %collective-permute-start.1 = (f32[104,384]{1,0:T(8,128)S(1)}, f32[104,384]{1,0:T(8,128)S(1)}, u32[]{:S(2)}, u32[]{:S(2)}) collective-permute-start(f32[104,384]{1,0:T(8,128)S(1)} %get-tuple-element.21), channel_id=1, source_target_pairs={{0,32},{1,33},{2,34},{3,35},{4,36},{5,37},{6,38},{7,39},{8,40},{9,... | collective-permute-start | bytes 479240 | tf_op jit(solution)/shard_map/ppermute | solution.py:221
  15.5 13.8 %copy-start.1 = (f32[3,32,512]{2,1,0:T(8,128)S(1)}, f32[3,32,512]{2,1,0:T(8,128)}, u32[]{:S(2)}) copy-start(f32[3,32,512]{2,1,0:T(8,128)} %tangent.7) | copy-start | bytes 589828
  15.6 13.8 %copy-start.3 = (f32[3,32,512]{2,1,0:T(8,128)S(1)}, f32[3,32,512]{2,1,0:T(8,128)}, u32[]{:S(2)}) copy-start(f32[3,32,512]{2,1,0:T(8,128)} %basis.3) | copy-start | bytes 589828
  15.6 13.8 %copy-start.4 = (f32[12,512]{1,0:T(8,128)S(1)}, f32[12,512]{1,0:T(8,128)}, u32[]{:S(2)}) copy-start(f32[12,512]{1,0:T(8,128)} %stiffness.11) | copy-start | bytes 73732
  15.6 13.8 %copy-start.5 = (f32[12,512]{1,0:T(8,128)S(1)}, f32[12,512]{1,0:T(8,128)}, u32[]{:S(2)}) copy-start(f32[12,512]{1,0:T(8,128)} %rest_length.11) | copy-start | bytes 73732
  15.6 13.8 %copy-start.6 = (s32[12,512]{1,0:T(8,128)S(1)}, s32[12,512]{1,0:T(8,128)}, u32[]{:S(2)}) copy-start(s32[12,512]{1,0:T(8,128)} %neighbours.11) | copy-start | bytes 73732
  15.6 13.8 %copy-start.7 = (s32[12,512]{1,0:T(8,128)S(1)}, s32[12,512]{1,0:T(8,128)}, u32[]{:S(2)}) copy-start(s32[12,512]{1,0:T(8,128)} %intact.11) | copy-start | bytes 73732
  15.6 13.7 %copy-start.11 = (f32[32]{0:T(128)S(1)}, f32[32]{0:T(128)}, u32[]{:S(2)}) copy-start(f32[32]{0:T(128)} %params.3) | copy-start | bytes 388
  15.7 18.5 %collective-permute-start.3 = (f32[104,384]{1,0:T(8,128)S(1)}, f32[104,384]{1,0:T(8,128)S(1)}, u32[]{:S(2)}, u32[]{:S(2)}) collective-permute-start(f32[104,384]{1,0:T(8,128)S(1)} %get-tuple-element.38), channel_id=1, source_target_pairs={{0,1},{1,0},{2,3},{3,2},{4,5},{5,4},{6,7},{7,6},{8,9},{9,8},{10,11... | collective-permute-start | bytes 479240 | tf_op jit(solution)/shard_map/ppermute | solution.py:232
  17.7 16.5 %collective-permute-start.2 = (f32[104,384]{1,0:T(8,128)S(1)}, f32[104,384]{1,0:T(8,128)S(1)}, u32[]{:S(2)}, u32[]{:S(2)}) collective-permute-start(f32[104,384]{1,0:T(8,128)S(1)} %get-tuple-element.39), channel_id=1, source_target_pairs={{1,2},{2,1},{3,4},{4,3},{5,6},{6,5},{7,8},{8,7},{9,10},{10,9},{11,... | collective-permute-start | bytes 479240 | tf_op jit(solution)/shard_map/ppermute | solution.py:231
  31.7 2.4 %copy-start.2 = (f32[3,32,512]{2,1,0:T(8,128)S(1)}, f32[3,32,512]{2,1,0:T(8,128)}, u32[]{:S(2)}) copy-start(f32[3,32,512]{2,1,0:T(8,128)} %tangent_vel.1) | copy-start | bytes 589828
  31.8 2.4 %copy-start.9 = (f32[3,512]{1,0:T(4,128)S(1)}, f32[3,512]{1,0:T(4,128)}, u32[]{:S(2)}) copy-start(f32[3,512]{1,0:T(4,128)} %velocity.1) | copy-start | bytes 18436
  31.8 2.4 %copy-start.10 = (f32[512]{0:T(512)S(1)}, f32[512]{0:T(512)}, u32[]{:S(2)}) copy-start(f32[512]{0:T(512)} %param.18) | copy-start | bytes 6148
  37.7 7.2 %collective-permute-start.4 = (f32[104,384]{1,0:T(8,128)S(1)}, f32[104,384]{1,0:T(8,128)S(1)}, u32[]{:S(2)}, u32[]{:S(2)}) collective-permute-start(f32[104,384]{1,0:T(8,128)S(1)} %get-tuple-element.26), channel_id=1, source_target_pairs={{32,64},{33,65},{34,66},{35,67},{36,68},{37,69},{38,70},{39,71},{4... | collective-permute-start | bytes 479240 | tf_op jit(solution)/shard_map/ppermute | solution.py:220
  41.7 7.2 %collective-permute-start.5 = (f32[104,384]{1,0:T(8,128)S(1)}, f32[104,384]{1,0:T(8,128)S(1)}, u32[]{:S(2)}, u32[]{:S(2)}) collective-permute-start(f32[104,384]{1,0:T(8,128)S(1)} %get-tuple-element.27), channel_id=1, source_target_pairs={{0,32},{1,33},{2,34},{3,35},{4,36},{5,37},{6,38},{7,39},{8,40},{9,... | collective-permute-start | bytes 479240 | tf_op jit(solution)/shard_map/ppermute | solution.py:221
  48.9 10.7 %collective-permute-start.7 = (f32[104,384]{1,0:T(8,128)S(1)}, f32[104,384]{1,0:T(8,128)S(1)}, u32[]{:S(2)}, u32[]{:S(2)}) collective-permute-start(f32[104,384]{1,0:T(8,128)S(1)} %get-tuple-element.36), channel_id=1, source_target_pairs={{0,1},{1,0},{2,3},{3,2},{4,5},{5,4},{6,7},{7,6},{8,9},{9,8},{10,11... | collective-permute-start | bytes 479240 | tf_op jit(solution)/shard_map/ppermute | solution.py:232
  50.8 10.2 %collective-permute-start.6 = (f32[104,384]{1,0:T(8,128)S(1)}, f32[104,384]{1,0:T(8,128)S(1)}, u32[]{:S(2)}, u32[]{:S(2)}) collective-permute-start(f32[104,384]{1,0:T(8,128)S(1)} %get-tuple-element.37), channel_id=1, source_target_pairs={{1,2},{2,1},{3,4},{4,3},{5,6},{6,5},{7,8},{8,7},{9,10},{10,9},{11,... | collective-permute-start | bytes 479240 | tf_op jit(solution)/shard_map/ppermute | solution.py:231

commit v2 on v1

--- a/solution.py
+++ b/solution.py
@@ -9,8 +9,9 @@
 DT = 0.05
 FACE = 256
 CORNER = 16
-MESSAGE = FACE + 128
 ROWS = 104
+MESSAGE = ROWS + 16
+GROUPS = ROWS // 8
 AXES = ("len", "height")
 PARAMS = pltpu.CompilerParams(vmem_limit_bytes=16 * 2**20)
 
@@ -53,11 +54,36 @@
     return jnp.concatenate([flat, position, jnp.zeros((ROWS - tang - 3, lanes), jnp.float32)], axis=0)
 
 
+def fold(columns):
+    slot = lax.broadcasted_iota(jnp.int32, (8, FACE), 1) >> 5
+    parts = []
+    for first in range(0, GROUPS, 8):
+        part = jnp.zeros((8, FACE), jnp.float32)
+        for group in range(first, min(first + 8, GROUPS)):
+            part = jnp.where(slot == group - first, columns[8 * group : 8 * group + 8, :], part)
+        parts.append(part)
+    return jnp.concatenate(parts, axis=0)
+
+
+def unfold(one, two):
+    lane = lax.broadcasted_iota(jnp.int32, (16, 128), 1)
+    moved = []
+    for slot in range(8):
+        back = (FACE - 32 * slot) % FACE
+        left = one if back == 0 else pltpu.roll(one, back, 1)
+        right = pltpu.roll(two, (back + 32) % FACE, 1) if (back + 32) % FACE else two
+        moved.append(jnp.where(lane < 32, left[:, :128], right[:, :128]))
+    parts = [moved[group % 8][8 * (group // 8) : 8 * (group // 8) + 8, :] for group in range(GROUPS)]
+    return jnp.concatenate(parts, axis=0)
+
+
 def pack(table, sends, first, second, third, fourth):
-    first[...] = pick(table, sends[0:1, :])
-    second[...] = pick(table, sends[1:2, :])
-    third[...] = pick(table, sends[2:3, :FACE])
-    fourth[...] = pick(table, sends[3:4, :FACE])
+    first[:ROWS, :] = pick(table, sends[0:1, :])
+    first[ROWS:, :] = fold(pick(table, sends[4:5, :]))
+    second[:ROWS, :] = pick(table, sends[1:2, :])
+    second[ROWS:, :] = fold(pick(table, sends[5:6, :]))
+    third[...] = pick(table, sends[2:3, :])
+    fourth[...] = pick(table, sends[3:4, :])
 
 
 def bonds_into(total, table, index, inside, tangent, position, stiffness, rest_length, intact, owned):
@@ -95,8 +121,8 @@
     second_l = jnp.where(forward == odd[0], 1, 0)
     second_h = jnp.where(upward == odd[1], 1, 0)
     on_l = (face == 0) | (face == 3)
-    at_face = jnp.where(on_l, 512 + 256 * second_l, 1024 + 256 * second_h) + (index & 255)
-    at_corner = 1536 + 32 * second_h + 16 * second_l + (index & 15)
+    at_face = jnp.where(on_l, 512 + 256 * second_l, 1280 - 256 * second_h) + (index & 255)
+    at_corner = 1536 + 32 * second_h + 16 * (second_l ^ second_h) + (index & 15)
     return jnp.where(own, index, jnp.where(is_corner, at_corner, at_face))
 
 
@@ -121,11 +147,11 @@
     bonds_into(total, table, index, inside, tangent, position, stiffness, rest_length, intact, owned[0])
 
 
-def len_kernel(odd, owned, before, first, second, tangent, position, stiffness, rest_length, neighbours, intact, total):
+def side_kernel(odd, owned, before, first, second, fourth, tangent, position, stiffness, rest_length, neighbours, intact, total):
     total[...] = before[...]
-    table = halves(jnp.concatenate([first[:, :FACE], second[:, :FACE]], axis=1))
+    table = halves(jnp.concatenate([first[:ROWS, :], second[:ROWS, :], fourth[:ROWS, :]], axis=1))
     index = place_of(neighbours[...], odd) - 512
-    inside = (index >= 0) & (index < 512)
+    inside = (index >= 0) & (index < 768)
     bonds_into(total, table, index, inside, tangent, position, stiffness, rest_length, intact, owned[0])
 
 
@@ -135,10 +161,9 @@
         total = outs[-1]
         tang = tangent.shape[1]
         total[...] = before[...]
-        lane = lax.broadcasted_iota(jnp.int32, (ROWS, 128), 1)
-        corners = jnp.where(lane < 32, third[:, FACE:], fourth[:, FACE:])
-        table = halves(jnp.concatenate([third[:, :FACE], fourth[:, :FACE], corners], axis=1))
-        index = place_of(neighbours[...], odd) - 1024
+        corners = unfold(third[ROWS:, :], fourth[ROWS:, :])
+        table = halves(jnp.concatenate([third[:ROWS, :], corners], axis=1))[:, : FACE + 64]
+        index = place_of(neighbours[...], odd) - 1280
         inside = index >= 0
         bonds_into(total, table, index, inside, tangent, position, stiffness, rest_length, intact, owned[0])
         pace = DT / mass[...]
@@ -195,19 +220,20 @@
     def either(flag, yes, no):
         return jnp.where(flag == 1, yes, no)
 
-    blank = jnp.full((CORNER,), -1, jnp.int32)
-    rest_blank = jnp.full((64,), -1, jnp.int32)
     up = [either(odd_h, corner_lists[2 * a + 1], corner_lists[2 * a]) for a in range(2)]
     down = [either(odd_h, corner_lists[2 * a], corner_lists[2 * a + 1]) for a in range(2)]
     sends = jnp.stack(
         [
-            jnp.concatenate([either(odd_l, face_lists[3], face_lists[0]), either(odd_l, up[1], up[0]), blank, either(odd_l, down[1], down[0]), blank, rest_blank]),
-            jnp.concatenate([either(odd_l, face_lists[0], face_lists[3]), blank, either(odd_l, up[0], up[1]), blank, either(odd_l, down[0], down[1]), rest_blank]),
-            jnp.concatenate([either(odd_h, face_lists[2], face_lists[1]), blank, blank, blank, blank, rest_blank]),
-            jnp.concatenate([either(odd_h, face_lists[1], face_lists[2]), blank, blank, blank, blank, rest_blank]),
+            either(odd_l, face_lists[3], face_lists[0]),
+            either(odd_l, face_lists[0], face_lists[3]),
+            either(odd_h, face_lists[2], face_lists[1]),
+            either(odd_h, face_lists[1], face_lists[2]),
+            jnp.tile(jnp.concatenate([either(odd_l, up[1], up[0]), either(odd_l, down[1], down[0])]), 8),
+            jnp.tile(jnp.concatenate([either(odd_l, down[0], down[1]), either(odd_l, up[0], up[1])]), 8),
         ]
     )
-    packed = (f32(ROWS, MESSAGE), f32(ROWS, MESSAGE), f32(ROWS, FACE), f32(ROWS, FACE))
+    low = lax.broadcasted_iota(jnp.int32, (MESSAGE - ROWS, FACE), 1) % 32 < CORNER
+    packed = (f32(MESSAGE, FACE), f32(MESSAGE, FACE), f32(ROWS, FACE), f32(ROWS, FACE))
     messages = pl.pallas_call(
         pack_kernel,
         out_shape=packed,
@@ -227,17 +253,19 @@
             cost_estimate=cost(512, bonds, 1000000),
             name="own_bonds",
         )(odd, owned, params, tangent_pos, position, load_basis, stiffness, rest_length, neighbours, intact)
-        corners = first[:, FACE:] + second[:, FACE:]
-        third = lax.ppermute(jnp.concatenate([messages[2], corners], axis=1), AXES, matching(strips, levels, 1, 1))
-        fourth = lax.ppermute(jnp.concatenate([messages[3], corners], axis=1), AXES, matching(strips, levels, 1, 0))
+        first, second, total = lax.optimization_barrier((first, second, total))
+        mine = jnp.where(low, second[ROWS:], first[ROWS:])
+        fourth = lax.ppermute(jnp.concatenate([messages[3], mine]), AXES, matching(strips, levels, 1, 0))
+        mine = jnp.where(low, first[ROWS:], second[ROWS:])
+        third = lax.ppermute(jnp.concatenate([messages[2], mine]), AXES, matching(strips, levels, 1, 1))
         total = pl.pallas_call(
-            len_kernel,
+            side_kernel,
             out_shape=f32(ROWS, count),
-            in_specs=[SMEM] * 2 + [VMEM] * 9,
+            in_specs=[SMEM] * 2 + [VMEM] * 10,
             compiler_params=PARAMS,
-            cost_estimate=cost(512, bonds, 1000000),
-            name="len_bonds",
-        )(odd, owned, total, first, second, tangent_pos, position, stiffness, rest_length, neighbours, intact)
+            cost_estimate=cost(768, bonds, 1000000),
+            name="side_bonds",
+        )(odd, owned, total, first, second, fourth, tangent_pos, position, stiffness, rest_length, neighbours, intact)
         state = (f32(*tangent_pos.shape), f32(*position.shape), f32(*tangent_pos.shape), f32(*position.shape))
         out = pl.pallas_call(
             height_kernel(last),
@@ -245,7 +273,7 @@
             in_specs=[SMEM] * 2 + [VMEM] * 13,
             scratch_shapes=[pltpu.VMEM((ROWS, count), jnp.float32)],
             compiler_params=PARAMS,
-            cost_estimate=cost(640, bonds, 1500000),
+            cost_estimate=cost(320, bonds, 1500000),
             name="height_bonds",
         )(odd, owned, total, third, fourth, tangent_pos, position, tangent_vel, velocity, mass, stiffness, rest_length, neighbours, intact, sends)
         tangent_pos, position, tangent_vel, velocity = out[:4]

time: 65.2 us -> 60.9 us (0.934)
  waiting for transfers between devices: 9.73 us -> 3.76 us
  starting transfers between devices: 33.6 us -> 35 us
    ppermute x2, waiting for transfers between devices: 7.02 us -> 2.5 us  [on_device(): second = lax.ppermute(messages[1], AXES, matching(strips, levels, 0, 0))]
    pallas_call x2, Pallas kernels: 7.26 us -> 5.68 us  [on_device(): pl.pallas_call(height_kernel(last), out_shape=state if last else state +...]
    ppermute x4, starting transfers between devices: 19.7 us -> 21.1 us  [the longest x2 17.2 us: on_device(): lax.ppermute(jnp.concatenate([messages[2], mine]), AXES, matching(strips,...]
    pallas_call x2, Pallas kernels: 4.68 us -> 6.03 us  [on_device(): pl.pallas_call(side_kernel, out_shape=f32(ROWS, count), in_specs=[SMEM] *...]
    ppermute x2, waiting for transfers between devices: 1.28 us -> 0.01 us  [on_device(): first = lax.ppermute(messages[0], AXES, matching(strips, levels, 0, 1))]
  transfers between devices with their start and end apart: 8 -> 8, of which waited for: 4 -> 2; matrix products, arithmetic and copies ran while one was open for 0% -> 0% of each run, Pallas kernels for 14% -> 18%
where the time goes in v2:
time: 60.9 us; the launch traced here: 60.5 us
  starting transfers between devices  35 us (57%)
  Pallas kernels  16.8 us (28%)
  waiting for transfers between devices  3.76 us (6%)
  local copies, waits for them, and re-layouts  3.05 us (5%)
  between operations  1.63 us (3%)
    ppermute x2, starting transfers between devices, on_device(): lax.ppermute(jnp.concatenate([messages[2], mine]), AXES, matching(strips,...  17.2 us
    ppermute x2, starting transfers between devices, on_device(): first = lax.ppermute(messages[0], AXES, matching(strips, levels, 0, 1))  7.44 us
    ppermute x2, starting transfers between devices, on_device(): second = lax.ppermute(messages[1], AXES, matching(strips, levels, 0, 0))  6.47 us
    pallas_call x2, Pallas kernels, on_device(): pl.pallas_call(side_kernel, out_shape=f32(ROWS, count), in_specs=[SMEM] *...  6.03 us
    pallas_call x2, Pallas kernels, on_device(): pl.pallas_call(height_kernel(last), out_shape=state if last else state +...  5.68 us
    pallas_call x2, Pallas kernels, on_device(): pl.pallas_call(own_kernel, out_shape=f32(ROWS, count), in_specs=[SMEM] *...  4.6 us
    ppermute x2, starting transfers between devices, on_device(): lax.ppermute(jnp.concatenate([messages[3], mine]), AXES, matching(strips,...  3.84 us
    unnamed x28, local copies, waits for them, and re-layouts  2.86 us
  transfers between devices with their start and end apart: 8, of which 2 were waited for; matrix products, arithmetic and copies ran while one was open for 0% of the time, Pallas kernels for 18%

profile of v2, /device:TPU:14, one launch (start us, length us, event | category | flops | bytes accessed | tf_op | source)
XLA Modules:
  0.0 60.5 jit_solution(3236660051680992987)
XLA Ops:
  0.6 0.0 copy-start.13
  0.7 0.0 copy-start.12
  0.7 0.7 %copy-done.13 = s32[4,16]{1,0:T(4,128)S(1)} copy-done((s32[4,16]{1,0:T(4,128)S(1)}, s32[4,16]{1,0:T(4,128)}, u32[]{:S(2)}) %copy-start.13) | copy-done | bytes 280
  1.3 0.0 copy-done.12
  1.4 0.1 pad_add_fusion.1
  1.4 0.1 stack_tile.6
  1.5 0.1 stack_tile.7
  1.6 0.0 copy-start.8
  1.6 0.7 %copy-done.8 = f32[3,512]{1,0:T(4,128)S(1)} copy-done((f32[3,512]{1,0:T(4,128)S(1)}, f32[3,512]{1,0:T(4,128)}, u32[]{:S(2)}) %copy-start.8) | copy-done | bytes 6168
  2.3 0.0 copy-start
  2.3 0.9 %copy-done = f32[3,32,512]{2,1,0:T(8,128)S(1)} copy-done((f32[3,32,512]{2,1,0:T(8,128)S(1)}, f32[3,32,512]{2,1,0:T(8,128)}, u32[]{:S(2)}) %copy-start) | copy-done | bytes 196632
  3.2 0.0 copy-start.1
  3.2 0.0 copy-start.3
  3.2 0.0 copy-start.4
  3.2 0.0 copy-start.5
  3.2 0.0 copy-start.6
  3.3 0.0 copy-start.7
  3.3 0.5 pack.1
  3.8 3.5 %collective-permute-start = (f32[120,256]{1,0:T(8,128)S(1)}, f32[120,256]{1,0:T(8,128)S(1)}, u32[]{:S(2)}, u32[]{:S(2)}) collective-permute-start(f32[120,256]{1,0:T(8,128)S(1)} %get-tuple-element.26), channel_id=1, source_target_pairs={{32,64},{33,65},{34,66},{35,67},{36,68},{37,69},{38,70},{39,71},{4... | collective-permute-start | bytes 368648 | tf_op jit(solution)/shard_map/ppermute | solution.py:246
  7.3 4.5 %collective-permute-start.1 = (f32[120,256]{1,0:T(8,128)S(1)}, f32[120,256]{1,0:T(8,128)S(1)}, u32[]{:S(2)}, u32[]{:S(2)}) collective-permute-start(f32[120,256]{1,0:T(8,128)S(1)} %get-tuple-element.27), channel_id=1, source_target_pairs={{0,32},{1,33},{2,34},{3,35},{4,36},{5,37},{6,38},{7,39},{8,40},{9,... | collective-permute-start | bytes 368648 | tf_op jit(solution)/shard_map/ppermute | solution.py:247
  12.5 0.0 copy-start.11
  12.5 0.1 pad_add_fusion.odd
  12.6 0.0 copy-done.1
  12.6 0.0 copy-done.3
  12.6 0.0 copy-done.4
  12.6 0.0 copy-done.5
  12.6 0.0 copy-done.6
  12.6 0.0 copy-done.7
  12.6 0.5 copy-done.11
  13.1 2.3 %own_bonds.2.before = f32[104,512]{1,0:T(8,128)S(1)} custom-call(s32[2]{0:T(128)S(1)} %pad_add_fusion.odd, s32[1]{0:T(128)S(6)} %copy.18.owned, f32[32]{0:T(128)S(1)} %copy-done.11, f32[3,32,512]{2,1,0:T(8,128)S(1)} %copy-done.1, f32[3,512]{1,0:T(4,128)S(1)} %copy-done.8, f32[3,32,512]{2,1,0:T(8,128)S(1)} %copy-done.3, f32[12,512]{1,0:T(8,128)S(1)} %copy-done.4, ...), custom_call_target="tpu_custom_call" | custom-call | flops 1308622848 | bytes 1000000 | tf_op jit(solution)/shard_map/own_bonds/pallas_call | solution.py:248
  15.4 0.0 collective-permute-done.first
  15.4 0.0 collective-permute-done.1.second
  15.5 1.9 %collective-permute-start.2 = (f32[120,256]{1,0:T(8,128)S(1)}, f32[120,256]{1,0:T(8,128)S(1)}, u32[]{:S(2)}, u32[]{:S(2)}) collective-permute-start(f32[120,256]{1,0:T(8,128)S(1)} %pad_maximum_fusion), channel_id=1, source_target_pairs={{0,1},{1,0},{2,3},{3,2},{4,5},{5,4},{6,7},{7,6},{8,9},{9,8},{10,11... | collective-permute-start | bytes 368648 | tf_op jit(solution)/shard_map/ppermute | solution.py:258
  17.4 0.0 copy-start.2
  17.5 0.0 copy-start.9
  17.5 0.0 copy-start.10
  17.5 11.7 %collective-permute-start.3 = (f32[120,256]{1,0:T(8,128)S(1)}, f32[120,256]{1,0:T(8,128)S(1)}, u32[]{:S(2)}, u32[]{:S(2)}) collective-permute-start(f32[120,256]{1,0:T(8,128)S(1)} %pad_maximum_fusion.1), channel_id=1, source_target_pairs={{1,2},{2,1},{3,4},{4,3},{5,6},{6,5},{7,8},{8,7},{9,10},{10,9},{11,... | collective-permute-start | bytes 368648 | tf_op jit(solution)/shard_map/ppermute | solution.py:260
  29.2 0.0 collective-permute-done.2.fourth
  29.2 3.0 %side_bonds.2.before = f32[104,512]{1,0:T(8,128)S(1)} custom-call(s32[2]{0:T(128)S(1)} %pad_add_fusion.odd, s32[1]{0:T(128)S(6)} %copy.18.owned, f32[104,512]{1,0:T(8,128)S(1)} %own_bonds.2.before, f32[120,256]{1,0:T(8,128)S(1)} %collective-permute-done.first, f32[120,256]{1,0:T(8,128)S(1)} %collective-permute-done.1.second, ...), custom_call_target="tpu_custom_call" | custom-call | flops 1962934272 | bytes 1000000 | tf_op jit(solution)/shard_map/side_bonds/pallas_call | solution.py:261
  32.2 0.0 collective-permute-done.3.third
  32.2 0.0 copy-done.2
  32.2 0.0 copy-done.9
  32.3 0.0 copy-done.10
  32.3 2.7 %height_bonds.2 = (f32[3,32,512]{2,1,0:T(8,128)S(1)}, f32[3,512]{1,0:T(4,128)S(1)}, f32[3,32,512]{2,1,0:T(8,128)S(1)}, f32[3,512]{1,0:T(4,128)S(1)}, f32[120,256...) custom-call(s32[2]{0:T(128)S(1)} %pad_add_fusion.odd, ...), custom_call_target="tpu_custom_call" | custom-call | flops 817889280 | bytes 1500000 | tf_op jit(solution)/shard_map/height_bonds/pallas_call | solution.py:270
  35.0 4.0 %collective-permute-start.4 = (f32[120,256]{1,0:T(8,128)S(1)}, f32[120,256]{1,0:T(8,128)S(1)}, u32[]{:S(2)}, u32[]{:S(2)}) collective-permute-start(f32[120,256]{1,0:T(8,128)S(1)} %get-tuple-element.33), channel_id=1, source_target_pairs={{32,64},{33,65},{34,66},{35,67},{36,68},{37,69},{38,70},{39,71},{4... | collective-permute-start | bytes 368648 | tf_op jit(solution)/shard_map/ppermute | solution.py:246
  38.9 2.0 %collective-permute-start.5 = (f32[120,256]{1,0:T(8,128)S(1)}, f32[120,256]{1,0:T(8,128)S(1)}, u32[]{:S(2)}, u32[]{:S(2)}) collective-permute-start(f32[120,256]{1,0:T(8,128)S(1)} %get-tuple-element.34), channel_id=1, source_target_pairs={{0,32},{1,33},{2,34},{3,35},{4,36},{5,37},{6,38},{7,39},{8,40},{9,... | collective-permute-start | bytes 368648 | tf_op jit(solution)/shard_map/ppermute | solution.py:247
  40.9 2.3 %own_bonds.3.before = f32[104,512]{1,0:T(8,128)S(1)} custom-call(s32[2]{0:T(128)S(1)} %pad_add_fusion.odd, s32[1]{0:T(128)S(6)} %copy.18.owned, f32[32]{0:T(128)S(1)} %copy-done.11, f32[3,32,512]{2,1,0:T(8,128)S(1)} %get-tuple-element.35.tangent, f32[3,512]{1,0:T(4,128)S(1)} %get-tuple-element.36.position, f32[3,32,512]{2,1,0:T(8,128)S(1)} %copy-done.3, ...), custom_call_target="tpu_custom_call" | custom-call | flops 1308622848 | bytes 1000000 | tf_op jit(solution)/shard_map/own_bonds/pallas_call | solution.py:248
  43.2 0.0 collective-permute-done.4.first
  43.2 2.5 %collective-permute-done.5.second = f32[120,256]{1,0:T(8,128)S(1)} collective-permute-done((f32[120,256]{1,0:T(8,128)S(1)}, f32[120,256]{1,0:T(8,128)S(1)}, u32[]{:S(2)}, u32[]{:S(2)}) %collective-permute-start.5) | collective-permute-done | bytes 122912 | tf_op jit(solution)/shard_map/ppermute | solution.py:247
  45.7 1.9 %collective-permute-start.6 = (f32[120,256]{1,0:T(8,128)S(1)}, f32[120,256]{1,0:T(8,128)S(1)}, u32[]{:S(2)}, u32[]{:S(2)}) collective-permute-start(f32[120,256]{1,0:T(8,128)S(1)} %pad_maximum_fusion.2), channel_id=1, source_target_pairs={{0,1},{1,0},{2,3},{3,2},{4,5},{5,4},{6,7},{7,6},{8,9},{9,8},{10,11... | collective-permute-start | bytes 368648 | tf_op jit(solution)/shard_map/ppermute | solution.py:258
  47.7 5.5 %collective-permute-start.7 = (f32[120,256]{1,0:T(8,128)S(1)}, f32[120,256]{1,0:T(8,128)S(1)}, u32[]{:S(2)}, u32[]{:S(2)}) collective-permute-start(f32[120,256]{1,0:T(8,128)S(1)} %pad_maximum_fusion.3), channel_id=1, source_target_pairs={{1,2},{2,1},{3,4},{4,3},{5,6},{6,5},{7,8},{8,7},{9,10},{10,9},{11,... | collective-permute-start | bytes 368648 | tf_op jit(solution)/shard_map/ppermute | solution.py:260
  53.2 0.0 collective-permute-done.6.fourth
  53.2 3.0 %side_bonds.3.before = f32[104,512]{1,0:T(8,128)S(1)} custom-call(s32[2]{0:T(128)S(1)} %pad_add_fusion.odd, s32[1]{0:T(128)S(6)} %copy.18.owned, f32[104,512]{1,0:T(8,128)S(1)} %own_bonds.3.before, f32[120,256]{1,0:T(8,128)S(1)} %collective-permute-done.4.first, f32[120,256]{1,0:T(8,128)S(1)} %collective-permute-done.5.second, ...), custom_call_target="tpu_custom_call" | custom-call | flops 1962934272 | bytes 1000000 | tf_op jit(solution)/shard_map/side_bonds/pallas_call | solution.py:261
  56.2 1.2 %collective-permute-done.7.third = f32[120,256]{1,0:T(8,128)S(1)} collective-permute-done((f32[120,256]{1,0:T(8,128)S(1)}, f32[120,256]{1,0:T(8,128)S(1)}, u32[]{:S(2)}, u32[]{:S(2)}) %collective-permute-start.7) | collective-permute-done | bytes 122912 | tf_op jit(solution)/shard_map/ppermute | solution.py:260
  57.5 3.0 %height_bonds.3 = (f32[3,32,512]{2,1,0:T(8,128)}, f32[3,512]{1,0:T(4,128)}, f32[3,32,512]{2,1,0:T(8,128)}, f32[3,512]{1,0:T(4,128)}) custom-call(s32[2]{0:T(128)S(1)} %pad_add_fusion.odd, s32[1]{0:T(128)S(6)} %copy.18.owned, f32[104,512]{1,0:T(8,128)S(1)} %side_bonds.3.before, f32[120,256]{1,0:T(8,128)S(1)} %collective-permute-done.7.third, ...), custom_call_target="tpu_custom_call" | custom-call | flops 817889280 | bytes 1500000 | tf_op jit(solution)/shard_map/height_bonds/pallas_call | solution.py:270
  (13 shorter events, 0.1 us)
Async XLA Ops:
  0.6 0.7 %copy-start.13 = (s32[4,16]{1,0:T(4,128)S(1)}, s32[4,16]{1,0:T(4,128)}, u32[]{:S(2)}) copy-start(s32[4,16]{1,0:T(4,128)} %param.26) | copy-start | bytes 772
  0.7 0.7 %copy-start.12 = (s32[4,256]{1,0:T(4,128)S(1)}, s32[4,256]{1,0:T(4,128)}, u32[]{:S(2)}) copy-start(s32[4,256]{1,0:T(4,128)} %param.25) | copy-start | bytes 12292
  1.6 0.7 %copy-start.8 = (f32[3,512]{1,0:T(4,128)S(1)}, f32[3,512]{1,0:T(4,128)}, u32[]{:S(2)}) copy-start(f32[3,512]{1,0:T(4,128)} %position.7) | copy-start | bytes 18436
  2.3 0.9 %copy-start = (f32[3,32,512]{2,1,0:T(8,128)S(1)}, f32[3,32,512]{2,1,0:T(8,128)}, u32[]{:S(2)}) copy-start(f32[3,32,512]{2,1,0:T(8,128)} %tangent.7) | copy-start | bytes 589828
  3.2 9.3 %copy-start.1 = (f32[3,32,512]{2,1,0:T(8,128)S(1)}, f32[3,32,512]{2,1,0:T(8,128)}, u32[]{:S(2)}) copy-start(f32[3,32,512]{2,1,0:T(8,128)} %tangent.7) | copy-start | bytes 589828
  3.2 9.3 %copy-start.3 = (f32[3,32,512]{2,1,0:T(8,128)S(1)}, f32[3,32,512]{2,1,0:T(8,128)}, u32[]{:S(2)}) copy-start(f32[3,32,512]{2,1,0:T(8,128)} %basis.3) | copy-start | bytes 589828
  3.2 9.3 %copy-start.4 = (f32[12,512]{1,0:T(8,128)S(1)}, f32[12,512]{1,0:T(8,128)}, u32[]{:S(2)}) copy-start(f32[12,512]{1,0:T(8,128)} %stiffness.11) | copy-start | bytes 73732
  3.2 9.3 %copy-start.5 = (f32[12,512]{1,0:T(8,128)S(1)}, f32[12,512]{1,0:T(8,128)}, u32[]{:S(2)}) copy-start(f32[12,512]{1,0:T(8,128)} %rest_length.11) | copy-start | bytes 73732
  3.2 9.3 %copy-start.6 = (s32[12,512]{1,0:T(8,128)S(1)}, s32[12,512]{1,0:T(8,128)}, u32[]{:S(2)}) copy-start(s32[12,512]{1,0:T(8,128)} %neighbours.11) | copy-start | bytes 73732
  3.3 9.3 %copy-start.7 = (s32[12,512]{1,0:T(8,128)S(1)}, s32[12,512]{1,0:T(8,128)}, u32[]{:S(2)}) copy-start(s32[12,512]{1,0:T(8,128)} %intact.11) | copy-start | bytes 73732
  3.8 11.7 %collective-permute-start = (f32[120,256]{1,0:T(8,128)S(1)}, f32[120,256]{1,0:T(8,128)S(1)}, u32[]{:S(2)}, u32[]{:S(2)}) collective-permute-start(f32[120,256]{1,0:T(8,128)S(1)} %get-tuple-element.26), channel_id=1, source_target_pairs={{32,64},{33,65},{34,66},{35,67},{36,68},{37,69},{38,70},{39,71},{4... | collective-permute-start | bytes 368648 | tf_op jit(solution)/shard_map/ppermute | solution.py:246
  7.3 8.2 %collective-permute-start.1 = (f32[120,256]{1,0:T(8,128)S(1)}, f32[120,256]{1,0:T(8,128)S(1)}, u32[]{:S(2)}, u32[]{:S(2)}) collective-permute-start(f32[120,256]{1,0:T(8,128)S(1)} %get-tuple-element.27), channel_id=1, source_target_pairs={{0,32},{1,33},{2,34},{3,35},{4,36},{5,37},{6,38},{7,39},{8,40},{9,... | collective-permute-start | bytes 368648 | tf_op jit(solution)/shard_map/ppermute | solution.py:247
  12.5 0.7 %copy-start.11 = (f32[32]{0:T(128)S(1)}, f32[32]{0:T(128)}, u32[]{:S(2)}) copy-start(f32[32]{0:T(128)} %params.3) | copy-start | bytes 388
  15.5 13.7 %collective-permute-start.2 = (f32[120,256]{1,0:T(8,128)S(1)}, f32[120,256]{1,0:T(8,128)S(1)}, u32[]{:S(2)}, u32[]{:S(2)}) collective-permute-start(f32[120,256]{1,0:T(8,128)S(1)} %pad_maximum_fusion), channel_id=1, source_target_pairs={{0,1},{1,0},{2,3},{3,2},{4,5},{5,4},{6,7},{7,6},{8,9},{9,8},{10,11... | collective-permute-start | bytes 368648 | tf_op jit(solution)/shard_map/ppermute | solution.py:258
  17.4 14.8 %copy-start.2 = (f32[3,32,512]{2,1,0:T(8,128)S(1)}, f32[3,32,512]{2,1,0:T(8,128)}, u32[]{:S(2)}) copy-start(f32[3,32,512]{2,1,0:T(8,128)} %tangent_vel.1) | copy-start | bytes 589828
  17.5 14.8 %copy-start.9 = (f32[3,512]{1,0:T(4,128)S(1)}, f32[3,512]{1,0:T(4,128)}, u32[]{:S(2)}) copy-start(f32[3,512]{1,0:T(4,128)} %velocity.1) | copy-start | bytes 18436
  17.5 14.8 %copy-start.10 = (f32[512]{0:T(512)S(1)}, f32[512]{0:T(512)}, u32[]{:S(2)}) copy-start(f32[512]{0:T(512)} %param.18) | copy-start | bytes 6148
  17.5 14.8 %collective-permute-start.3 = (f32[120,256]{1,0:T(8,128)S(1)}, f32[120,256]{1,0:T(8,128)S(1)}, u32[]{:S(2)}, u32[]{:S(2)}) collective-permute-start(f32[120,256]{1,0:T(8,128)S(1)} %pad_maximum_fusion.1), channel_id=1, source_target_pairs={{1,2},{2,1},{3,4},{4,3},{5,6},{6,5},{7,8},{8,7},{9,10},{10,9},{11,... | collective-permute-start | bytes 368648 | tf_op jit(solution)/shard_map/ppermute | solution.py:260
  35.0 8.2 %collective-permute-start.4 = (f32[120,256]{1,0:T(8,128)S(1)}, f32[120,256]{1,0:T(8,128)S(1)}, u32[]{:S(2)}, u32[]{:S(2)}) collective-permute-start(f32[120,256]{1,0:T(8,128)S(1)} %get-tuple-element.33), channel_id=1, source_target_pairs={{32,64},{33,65},{34,66},{35,67},{36,68},{37,69},{38,70},{39,71},{4... | collective-permute-start | bytes 368648 | tf_op jit(solution)/shard_map/ppermute | solution.py:246
  38.9 6.8 %collective-permute-start.5 = (f32[120,256]{1,0:T(8,128)S(1)}, f32[120,256]{1,0:T(8,128)S(1)}, u32[]{:S(2)}, u32[]{:S(2)}) collective-permute-start(f32[120,256]{1,0:T(8,128)S(1)} %get-tuple-element.34), channel_id=1, source_target_pairs={{0,32},{1,33},{2,34},{3,35},{4,36},{5,37},{6,38},{7,39},{8,40},{9,... | collective-permute-start | bytes 368648 | tf_op jit(solution)/shard_map/ppermute | solution.py:247
  45.7 7.5 %collective-permute-start.6 = (f32[120,256]{1,0:T(8,128)S(1)}, f32[120,256]{1,0:T(8,128)S(1)}, u32[]{:S(2)}, u32[]{:S(2)}) collective-permute-start(f32[120,256]{1,0:T(8,128)S(1)} %pad_maximum_fusion.2), channel_id=1, source_target_pairs={{0,1},{1,0},{2,3},{3,2},{4,5},{5,4},{6,7},{7,6},{8,9},{9,8},{10,11... | collective-permute-start | bytes 368648 | tf_op jit(solution)/shard_map/ppermute | solution.py:258
  47.7 9.8 %collective-permute-start.7 = (f32[120,256]{1,0:T(8,128)S(1)}, f32[120,256]{1,0:T(8,128)S(1)}, u32[]{:S(2)}, u32[]{:S(2)}) collective-permute-start(f32[120,256]{1,0:T(8,128)S(1)} %pad_maximum_fusion.3), channel_id=1, source_target_pairs={{1,2},{2,1},{3,4},{4,3},{5,6},{6,5},{7,8},{8,7},{9,10},{10,9},{11,... | collective-permute-start | bytes 368648 | tf_op jit(solution)/shard_map/ppermute | solution.py:260

commit v3 on v2

--- a/solution.py
+++ b/solution.py
@@ -25,6 +25,10 @@
             if 0 <= other < size:
                 pairs.append((l * levels + h, other * levels + h if along == 0 else l * levels + other))
     return pairs
+
+
+def couples(strips, levels):
+    return [[l * levels + h, l * levels + h + 1] for l in range(strips) for h in range(0, levels, 2)]
 
 
 def halves(table):
@@ -147,8 +151,9 @@
     bonds_into(total, table, index, inside, tangent, position, stiffness, rest_length, intact, owned[0])
 
 
-def side_kernel(odd, owned, before, first, second, fourth, tangent, position, stiffness, rest_length, neighbours, intact, total):
+def side_kernel(odd, owned, before, first, second, both, tangent, position, stiffness, rest_length, neighbours, intact, total):
     total[...] = before[...]
+    fourth = both.at[1 - odd[1]]
     table = halves(jnp.concatenate([first[:ROWS, :], second[:ROWS, :], fourth[:ROWS, :]], axis=1))
     index = place_of(neighbours[...], odd) - 512
     inside = (index >= 0) & (index < 768)
@@ -156,11 +161,12 @@
 
 
 def height_kernel(last):
-    def body(odd, owned, before, third, fourth, tangent, position, tangent_vel, velocity, mass, stiffness, rest_length, neighbours, intact, sends, *outs):
+    def body(odd, owned, before, third, both, tangent, position, tangent_vel, velocity, mass, stiffness, rest_length, neighbours, intact, sends, *outs):
         new_tangent, new_position, new_tangent_vel, new_velocity = outs[:4]
         total = outs[-1]
         tang = tangent.shape[1]
         total[...] = before[...]
+        fourth = both.at[1 - odd[1]]
         corners = unfold(third[ROWS:, :], fourth[ROWS:, :])
         table = halves(jnp.concatenate([third[:ROWS, :], corners], axis=1))[:, : FACE + 64]
         index = place_of(neighbours[...], odd) - 1280
@@ -255,17 +261,18 @@
         )(odd, owned, params, tangent_pos, position, load_basis, stiffness, rest_length, neighbours, intact)
         first, second, total = lax.optimization_barrier((first, second, total))
         mine = jnp.where(low, second[ROWS:], first[ROWS:])
-        fourth = lax.ppermute(jnp.concatenate([messages[3], mine]), AXES, matching(strips, levels, 1, 0))
+        beside = jnp.concatenate([messages[3], mine])
         mine = jnp.where(low, first[ROWS:], second[ROWS:])
         third = lax.ppermute(jnp.concatenate([messages[2], mine]), AXES, matching(strips, levels, 1, 1))
+        both = lax.all_gather(beside, AXES, axis_index_groups=couples(strips, levels))
         total = pl.pallas_call(
             side_kernel,
             out_shape=f32(ROWS, count),
             in_specs=[SMEM] * 2 + [VMEM] * 10,
             compiler_params=PARAMS,
-            cost_estimate=cost(768, bonds, 1000000),
+            cost_estimate=cost(1, bonds, 1000),
             name="side_bonds",
-        )(odd, owned, total, first, second, fourth, tangent_pos, position, stiffness, rest_length, neighbours, intact)
+        )(odd, owned, total, first, second, both, tangent_pos, position, stiffness, rest_length, neighbours, intact)
         state = (f32(*tangent_pos.shape), f32(*position.shape), f32(*tangent_pos.shape), f32(*position.shape))
         out = pl.pallas_call(
             height_kernel(last),
@@ -275,7 +282,7 @@
             compiler_params=PARAMS,
             cost_estimate=cost(320, bonds, 1500000),
             name="height_bonds",
-        )(odd, owned, total, third, fourth, tangent_pos, position, tangent_vel, velocity, mass, stiffness, rest_length, neighbours, intact, sends)
+        )(odd, owned, total, third, both, tangent_pos, position, tangent_vel, velocity, mass, stiffness, rest_length, neighbours, intact, sends)
         tangent_pos, position, tangent_vel, velocity = out[:4]
         messages = out[4:]
     return (position, velocity, tangent_pos, tangent_vel)

time: 60.9 us -> 57.9 us (0.951)
  starting transfers between devices: 35 us -> 27.9 us
  blocking collectives: 0 us -> 4.14 us
    all_gather x0 -> x2, blocking collectives: none -> 4.14 us  [on_device(): lax.all_gather(beside, AXES, axis_index_groups=couples(strips, levels))]
    ppermute x2 -> x0, starting transfers between devices: 3.84 us -> none  [on_device(): lax.ppermute(jnp.concatenate([messages[3], mine]), AXES, matching(strips,...]
    ppermute x2, starting transfers between devices: 17.2 us -> 13.9 us  [on_device(): lax.ppermute(jnp.concatenate([messages[2], mine]), AXES, matching(strips,...]
  transfers between devices with their start and end apart: 8 -> 6, of which waited for: 2 -> 2; matrix products, arithmetic and copies ran while one was open for 0% -> 0% of each run, Pallas kernels for 18% -> 19%
where the time goes in v3:
time: 57.9 us; the launch traced here: 57.5 us
  starting transfers between devices  27.9 us (48%)
  Pallas kernels  16.9 us (29%)
  blocking collectives  4.14 us (7%)
  waiting for transfers between devices  3.71 us (6%)
  local copies, waits for them, and re-layouts  3.04 us (5%)
  between operations  1.58 us (3%)
    ppermute x2, starting transfers between devices, on_device(): lax.ppermute(jnp.concatenate([messages[2], mine]), AXES, matching(strips,...  13.9 us
    ppermute x2, starting transfers between devices, on_device(): first = lax.ppermute(messages[0], AXES, matching(strips, levels, 0, 1))  7.44 us
    ppermute x2, starting transfers between devices, on_device(): second = lax.ppermute(messages[1], AXES, matching(strips, levels, 0, 0))  6.47 us
    pallas_call x2, Pallas kernels, on_device(): pl.pallas_call(side_kernel, out_shape=f32(ROWS, count), in_specs=[SMEM] *...  6.06 us
    pallas_call x2, Pallas kernels, on_device(): pl.pallas_call(height_kernel(last), out_shape=state if last else state +...  5.68 us
    pallas_call x2, Pallas kernels, on_device(): pl.pallas_call(own_kernel, out_shape=f32(ROWS, count), in_specs=[SMEM] *...  4.68 us
    all_gather x2, blocking collectives, on_device(): lax.all_gather(beside, AXES, axis_index_groups=couples(strips, levels))  4.14 us
    unnamed x28, local copies, waits for them, and re-layouts  2.85 us
  transfers between devices with their start and end apart: 6, of which 2 were waited for; matrix products, arithmetic and copies ran while one was open for 0% of the time, Pallas kernels for 19%

profile of v3, /device:TPU:14, one launch (start us, length us, event | category | flops | bytes accessed | tf_op | source)
XLA Modules:
  0.0 57.5 jit_solution(11480270179916860493)
XLA Ops:
  0.6 0.0 copy-start.13
  0.7 0.0 copy-start.12
  0.7 0.7 %copy-done.13 = s32[4,16]{1,0:T(4,128)S(1)} copy-done((s32[4,16]{1,0:T(4,128)S(1)}, s32[4,16]{1,0:T(4,128)}, u32[]{:S(2)}) %copy-start.13) | copy-done | bytes 280
  1.3 0.0 copy-done.12
  1.4 0.1 pad_add_fusion.1
  1.4 0.1 stack_tile.6
  1.5 0.1 stack_tile.7
  1.6 0.0 copy-start.6
  1.6 0.7 %copy-done.6 = f32[3,512]{1,0:T(4,128)S(1)} copy-done((f32[3,512]{1,0:T(4,128)S(1)}, f32[3,512]{1,0:T(4,128)}, u32[]{:S(2)}) %copy-start.6) | copy-done | bytes 6168
  2.3 0.0 copy-start
  2.3 0.9 %copy-done = f32[3,32,512]{2,1,0:T(8,128)S(1)} copy-done((f32[3,32,512]{2,1,0:T(8,128)S(1)}, f32[3,32,512]{2,1,0:T(8,128)}, u32[]{:S(2)}) %copy-start) | copy-done | bytes 196632
  3.2 0.0 copy-start.1
  3.2 0.0 copy-start.2
  3.2 0.0 copy-start.3
  3.2 0.0 copy-start.4
  3.2 0.0 copy-start.5
  3.3 0.0 copy-start.8
  3.3 0.5 pack.1
  3.8 3.5 %collective-permute-start = (f32[120,256]{1,0:T(8,128)S(1)}, f32[120,256]{1,0:T(8,128)S(1)}, u32[]{:S(2)}, u32[]{:S(2)}) collective-permute-start(f32[120,256]{1,0:T(8,128)S(1)} %get-tuple-element.26), channel_id=1, source_target_pairs={{32,64},{33,65},{34,66},{35,67},{36,68},{37,69},{38,70},{39,71},{4... | collective-permute-start | bytes 368648 | tf_op jit(solution)/shard_map/ppermute | solution.py:252
  7.3 4.5 %collective-permute-start.1 = (f32[120,256]{1,0:T(8,128)S(1)}, f32[120,256]{1,0:T(8,128)S(1)}, u32[]{:S(2)}, u32[]{:S(2)}) collective-permute-start(f32[120,256]{1,0:T(8,128)S(1)} %get-tuple-element.27), channel_id=1, source_target_pairs={{0,32},{1,33},{2,34},{3,35},{4,36},{5,37},{6,38},{7,39},{8,40},{9,... | collective-permute-start | bytes 368648 | tf_op jit(solution)/shard_map/ppermute | solution.py:253
  12.5 0.0 copy-start.11
  12.5 0.1 pad_add_fusion.odd
  12.6 0.0 copy-done.1
  12.6 0.0 copy-done.2
  12.6 0.0 copy-done.3
  12.6 0.0 copy-done.4
  12.6 0.0 copy-done.5
  12.6 0.0 copy-done.8
  12.6 0.5 copy-done.11
  13.1 2.3 %own_bonds.2.before = f32[104,512]{1,0:T(8,128)S(1)} custom-call(s32[2]{0:T(128)S(1)} %pad_add_fusion.odd, s32[1]{0:T(128)S(6)} %copy.18.owned, f32[32]{0:T(128)S(1)} %copy-done.11, f32[3,32,512]{2,1,0:T(8,128)S(1)} %copy-done.1, f32[3,512]{1,0:T(4,128)S(1)} %copy-done.6, f32[3,32,512]{2,1,0:T(8,128)S(1)} %copy-done.8, f32[12,512]{1,0:T(8,128)S(1)} %copy-done.2, ...), custom_call_target="tpu_custom_call" | custom-call | flops 1308622848 | bytes 1000000 | tf_op jit(solution)/shard_map/own_bonds/pallas_call | solution.py:254
  15.5 0.0 collective-permute-done.first
  15.5 0.0 collective-permute-done.1.second
  15.5 10.4 %collective-permute-start.2 = (f32[120,256]{1,0:T(8,128)S(1)}, f32[120,256]{1,0:T(8,128)S(1)}, u32[]{:S(2)}, u32[]{:S(2)}) collective-permute-start(f32[120,256]{1,0:T(8,128)S(1)} %pad_maximum_fusion.1), channel_id=1, source_target_pairs={{1,2},{2,1},{3,4},{4,3},{5,6},{6,5},{7,8},{8,7},{9,10},{10,9},{11,... | collective-permute-start | bytes 368648 | tf_op jit(solution)/shard_map/ppermute | solution.py:266
  25.9 2.0 %all-gather = f32[240,256]{1,0:T(8,128)S(1)} all-gather(f32[120,256]{1,0:T(8,128)S(1)} %pad_maximum_fusion), channel_id=2, replica_groups={{0,1},{2,3},{4,5},{6,7},{8,9},{10,11},{12,13},{14,15},{16,17},{18,19},{..., dimensions={0}, use_global_device_ids=true | all-gather | bytes 368640 | tf_op jit(solution)/shard_map/all_gather | solution.py:267
  27.9 0.0 copy-start.7
  27.9 0.0 copy-start.9
  27.9 0.0 copy-start.10
  27.9 3.0 %side_bonds.2.before = f32[104,512]{1,0:T(8,128)S(1)} custom-call(s32[2]{0:T(128)S(1)} %pad_add_fusion.odd, s32[1]{0:T(128)S(6)} %copy.18.owned, f32[104,512]{1,0:T(8,128)S(1)} %own_bonds.2.before, f32[120,256]{1,0:T(8,128)S(1)} %collective-permute-done.first, f32[120,256]{1,0:T(8,128)S(1)} %collective-permute-done.1.second, f32[2,120,256]{2,1,0:T(8,128)S(1)} %bitcast.15, ...), custom_call_target="tpu_custom_call" | custom-call | flops 2555904 | bytes 1000 | tf_op jit(solution)/shard_map/side_bonds/pallas_call | solution.py:268
  31.0 0.0 collective-permute-done.2.third
  31.0 0.0 copy-done.7
  31.0 0.0 copy-done.9
  31.0 0.0 copy-done.10
  31.0 2.7 %height_bonds.2 = (f32[3,32,512]{2,1,0:T(8,128)S(1)}, f32[3,512]{1,0:T(4,128)S(1)}, f32[3,32,512]{2,1,0:T(8,128)S(1)}, f32[3,512]{1,0:T(4,128)S(1)}, f32[120,256...) custom-call(s32[2]{0:T(128)S(1)} %pad_add_fusion.odd, ...), custom_call_target="tpu_custom_call" | custom-call | flops 817889280 | bytes 1500000 | tf_op jit(solution)/shard_map/height_bonds/pallas_call | solution.py:277
  33.7 4.0 %collective-permute-start.3 = (f32[120,256]{1,0:T(8,128)S(1)}, f32[120,256]{1,0:T(8,128)S(1)}, u32[]{:S(2)}, u32[]{:S(2)}) collective-permute-start(f32[120,256]{1,0:T(8,128)S(1)} %get-tuple-element.33), channel_id=1, source_target_pairs={{32,64},{33,65},{34,66},{35,67},{36,68},{37,69},{38,70},{39,71},{4... | collective-permute-start | bytes 368648 | tf_op jit(solution)/shard_map/ppermute | solution.py:252
  37.7 2.0 %collective-permute-start.4 = (f32[120,256]{1,0:T(8,128)S(1)}, f32[120,256]{1,0:T(8,128)S(1)}, u32[]{:S(2)}, u32[]{:S(2)}) collective-permute-start(f32[120,256]{1,0:T(8,128)S(1)} %get-tuple-element.34), channel_id=1, source_target_pairs={{0,32},{1,33},{2,34},{3,35},{4,36},{5,37},{6,38},{7,39},{8,40},{9,... | collective-permute-start | bytes 368648 | tf_op jit(solution)/shard_map/ppermute | solution.py:253
  39.6 2.3 %own_bonds.3.before = f32[104,512]{1,0:T(8,128)S(1)} custom-call(s32[2]{0:T(128)S(1)} %pad_add_fusion.odd, s32[1]{0:T(128)S(6)} %copy.18.owned, f32[32]{0:T(128)S(1)} %copy-done.11, f32[3,32,512]{2,1,0:T(8,128)S(1)} %get-tuple-element.35.tangent, f32[3,512]{1,0:T(4,128)S(1)} %get-tuple-element.36.position, f32[3,32,512]{2,1,0:T(8,128)S(1)} %copy-done.8, ...), custom_call_target="tpu_custom_call" | custom-call | flops 1308622848 | bytes 1000000 | tf_op jit(solution)/shard_map/own_bonds/pallas_call | solution.py:254
  42.0 0.0 collective-permute-done.3.first
  42.0 2.7 %collective-permute-done.4.second = f32[120,256]{1,0:T(8,128)S(1)} collective-permute-done((f32[120,256]{1,0:T(8,128)S(1)}, f32[120,256]{1,0:T(8,128)S(1)}, u32[]{:S(2)}, u32[]{:S(2)}) %collective-permute-start.4) | collective-permute-done | bytes 122912 | tf_op jit(solution)/shard_map/ppermute | solution.py:253
  44.7 3.6 %collective-permute-start.5 = (f32[120,256]{1,0:T(8,128)S(1)}, f32[120,256]{1,0:T(8,128)S(1)}, u32[]{:S(2)}, u32[]{:S(2)}) collective-permute-start(f32[120,256]{1,0:T(8,128)S(1)} %pad_maximum_fusion.3), channel_id=1, source_target_pairs={{1,2},{2,1},{3,4},{4,3},{5,6},{6,5},{7,8},{8,7},{9,10},{10,9},{11,... | collective-permute-start | bytes 368648 | tf_op jit(solution)/shard_map/ppermute | solution.py:266
  48.3 2.2 %all-gather.1 = f32[240,256]{1,0:T(8,128)S(1)} all-gather(f32[120,256]{1,0:T(8,128)S(1)} %pad_maximum_fusion.2), channel_id=3, replica_groups={{0,1},{2,3},{4,5},{6,7},{8,9},{10,11},{12,13},{14,15},{16,17},{18,19},{..., dimensions={0}, use_global_device_ids=true | all-gather | bytes 368640 | tf_op jit(solution)/shard_map/all_gather | solution.py:267
  50.5 3.0 %side_bonds.3.before = f32[104,512]{1,0:T(8,128)S(1)} custom-call(s32[2]{0:T(128)S(1)} %pad_add_fusion.odd, s32[1]{0:T(128)S(6)} %copy.18.owned, f32[104,512]{1,0:T(8,128)S(1)} %own_bonds.3.before, f32[120,256]{1,0:T(8,128)S(1)} %collective-permute-done.3.first, f32[120,256]{1,0:T(8,128)S(1)} %collective-permute-done.4.second, f32[2,120,256]{2,1,0:T(8,128)S(1)} %bitcast.13, ...), custom_call_target="tpu_custom_call" | custom-call | flops 2555904 | bytes 1000 | tf_op jit(solution)/shard_map/side_bonds/pallas_call | solution.py:268
  53.5 1.0 %collective-permute-done.5.third = f32[120,256]{1,0:T(8,128)S(1)} collective-permute-done((f32[120,256]{1,0:T(8,128)S(1)}, f32[120,256]{1,0:T(8,128)S(1)}, u32[]{:S(2)}, u32[]{:S(2)}) %collective-permute-start.5) | collective-permute-done | bytes 122912 | tf_op jit(solution)/shard_map/ppermute | solution.py:266
  54.5 3.0 %height_bonds.3 = (f32[3,32,512]{2,1,0:T(8,128)}, f32[3,512]{1,0:T(4,128)}, f32[3,32,512]{2,1,0:T(8,128)}, f32[3,512]{1,0:T(4,128)}) custom-call(s32[2]{0:T(128)S(1)} %pad_add_fusion.odd, s32[1]{0:T(128)S(6)} %copy.18.owned, f32[104,512]{1,0:T(8,128)S(1)} %side_bonds.3.before, f32[120,256]{1,0:T(8,128)S(1)} %collective-permute-done.5.third, ...), custom_call_target="tpu_custom_call" | custom-call | flops 817889280 | bytes 1500000 | tf_op jit(solution)/shard_map/height_bonds/pallas_call | solution.py:277
  (13 shorter events, 0.1 us)
Async XLA Ops:
  0.6 0.7 %copy-start.13 = (s32[4,16]{1,0:T(4,128)S(1)}, s32[4,16]{1,0:T(4,128)}, u32[]{:S(2)}) copy-start(s32[4,16]{1,0:T(4,128)} %param.26) | copy-start | bytes 772
  0.7 0.7 %copy-start.12 = (s32[4,256]{1,0:T(4,128)S(1)}, s32[4,256]{1,0:T(4,128)}, u32[]{:S(2)}) copy-start(s32[4,256]{1,0:T(4,128)} %param.25) | copy-start | bytes 12292
  1.6 0.7 %copy-start.6 = (f32[3,512]{1,0:T(4,128)S(1)}, f32[3,512]{1,0:T(4,128)}, u32[]{:S(2)}) copy-start(f32[3,512]{1,0:T(4,128)} %position.7) | copy-start | bytes 18436
  2.3 0.9 %copy-start = (f32[3,32,512]{2,1,0:T(8,128)S(1)}, f32[3,32,512]{2,1,0:T(8,128)}, u32[]{:S(2)}) copy-start(f32[3,32,512]{2,1,0:T(8,128)} %tangent.7) | copy-start | bytes 589828
  3.2 9.3 %copy-start.1 = (f32[3,32,512]{2,1,0:T(8,128)S(1)}, f32[3,32,512]{2,1,0:T(8,128)}, u32[]{:S(2)}) copy-start(f32[3,32,512]{2,1,0:T(8,128)} %tangent.7) | copy-start | bytes 589828
  3.2 9.3 %copy-start.2 = (f32[12,512]{1,0:T(8,128)S(1)}, f32[12,512]{1,0:T(8,128)}, u32[]{:S(2)}) copy-start(f32[12,512]{1,0:T(8,128)} %stiffness.11) | copy-start | bytes 73732
  3.2 9.3 %copy-start.3 = (f32[12,512]{1,0:T(8,128)S(1)}, f32[12,512]{1,0:T(8,128)}, u32[]{:S(2)}) copy-start(f32[12,512]{1,0:T(8,128)} %rest_length.11) | copy-start | bytes 73732
  3.2 9.3 %copy-start.4 = (s32[12,512]{1,0:T(8,128)S(1)}, s32[12,512]{1,0:T(8,128)}, u32[]{:S(2)}) copy-start(s32[12,512]{1,0:T(8,128)} %neighbours.11) | copy-start | bytes 73732
  3.2 9.3 %copy-start.5 = (s32[12,512]{1,0:T(8,128)S(1)}, s32[12,512]{1,0:T(8,128)}, u32[]{:S(2)}) copy-start(s32[12,512]{1,0:T(8,128)} %intact.11) | copy-start | bytes 73732
  3.3 9.3 %copy-start.8 = (f32[3,32,512]{2,1,0:T(8,128)S(1)}, f32[3,32,512]{2,1,0:T(8,128)}, u32[]{:S(2)}) copy-start(f32[3,32,512]{2,1,0:T(8,128)} %basis.3) | copy-start | bytes 589828
  3.8 11.7 %collective-permute-start = (f32[120,256]{1,0:T(8,128)S(1)}, f32[120,256]{1,0:T(8,128)S(1)}, u32[]{:S(2)}, u32[]{:S(2)}) collective-permute-start(f32[120,256]{1,0:T(8,128)S(1)} %get-tuple-element.26), channel_id=1, source_target_pairs={{32,64},{33,65},{34,66},{35,67},{36,68},{37,69},{38,70},{39,71},{4... | collective-permute-start | bytes 368648 | tf_op jit(solution)/shard_map/ppermute | solution.py:252
  7.3 8.2 %collective-permute-start.1 = (f32[120,256]{1,0:T(8,128)S(1)}, f32[120,256]{1,0:T(8,128)S(1)}, u32[]{:S(2)}, u32[]{:S(2)}) collective-permute-start(f32[120,256]{1,0:T(8,128)S(1)} %get-tuple-element.27), channel_id=1, source_target_pairs={{0,32},{1,33},{2,34},{3,35},{4,36},{5,37},{6,38},{7,39},{8,40},{9,... | collective-permute-start | bytes 368648 | tf_op jit(solution)/shard_map/ppermute | solution.py:253
  12.5 0.7 %copy-start.11 = (f32[32]{0:T(128)S(1)}, f32[32]{0:T(128)}, u32[]{:S(2)}) copy-start(f32[32]{0:T(128)} %params.3) | copy-start | bytes 388
  15.5 15.4 %collective-permute-start.2 = (f32[120,256]{1,0:T(8,128)S(1)}, f32[120,256]{1,0:T(8,128)S(1)}, u32[]{:S(2)}, u32[]{:S(2)}) collective-permute-start(f32[120,256]{1,0:T(8,128)S(1)} %pad_maximum_fusion.1), channel_id=1, source_target_pairs={{1,2},{2,1},{3,4},{4,3},{5,6},{6,5},{7,8},{8,7},{9,10},{10,9},{11,... | collective-permute-start | bytes 368648 | tf_op jit(solution)/shard_map/ppermute | solution.py:266
  27.9 3.1 %copy-start.7 = (f32[3,32,512]{2,1,0:T(8,128)S(1)}, f32[3,32,512]{2,1,0:T(8,128)}, u32[]{:S(2)}) copy-start(f32[3,32,512]{2,1,0:T(8,128)} %tangent_vel.1) | copy-start | bytes 589828
  27.9 3.1 %copy-start.9 = (f32[3,512]{1,0:T(4,128)S(1)}, f32[3,512]{1,0:T(4,128)}, u32[]{:S(2)}) copy-start(f32[3,512]{1,0:T(4,128)} %velocity.1) | copy-start | bytes 18436
  27.9 3.1 %copy-start.10 = (f32[512]{0:T(512)S(1)}, f32[512]{0:T(512)}, u32[]{:S(2)}) copy-start(f32[512]{0:T(512)} %param.18) | copy-start | bytes 6148
  33.7 8.3 %collective-permute-start.3 = (f32[120,256]{1,0:T(8,128)S(1)}, f32[120,256]{1,0:T(8,128)S(1)}, u32[]{:S(2)}, u32[]{:S(2)}) collective-permute-start(f32[120,256]{1,0:T(8,128)S(1)} %get-tuple-element.33), channel_id=1, source_target_pairs={{32,64},{33,65},{34,66},{35,67},{36,68},{37,69},{38,70},{39,71},{4... | collective-permute-start | bytes 368648 | tf_op jit(solution)/shard_map/ppermute | solution.py:252
  37.7 7.0 %collective-permute-start.4 = (f32[120,256]{1,0:T(8,128)S(1)}, f32[120,256]{1,0:T(8,128)S(1)}, u32[]{:S(2)}, u32[]{:S(2)}) collective-permute-start(f32[120,256]{1,0:T(8,128)S(1)} %get-tuple-element.34), channel_id=1, source_target_pairs={{0,32},{1,33},{2,34},{3,35},{4,36},{5,37},{6,38},{7,39},{8,40},{9,... | collective-permute-start | bytes 368648 | tf_op jit(solution)/shard_map/ppermute | solution.py:253
  44.7 9.8 %collective-permute-start.5 = (f32[120,256]{1,0:T(8,128)S(1)}, f32[120,256]{1,0:T(8,128)S(1)}, u32[]{:S(2)}, u32[]{:S(2)}) collective-permute-start(f32[120,256]{1,0:T(8,128)S(1)} %pad_maximum_fusion.3), channel_id=1, source_target_pairs={{1,2},{2,1},{3,4},{4,3},{5,6},{6,5},{7,8},{8,7},{9,10},{10,9},{11,... | collective-permute-start | bytes 368648 | tf_op jit(solution)/shard_map/ppermute | solution.py:266

commit v4 on v3

--- a/solution.py
+++ b/solution.py
@@ -81,25 +81,20 @@
     return jnp.concatenate(parts, axis=0)
 
 
-def pack(table, sends, first, second, third, fourth):
+def pack_len(table, sends, first, second):
     first[:ROWS, :] = pick(table, sends[0:1, :])
     first[ROWS:, :] = fold(pick(table, sends[4:5, :]))
     second[:ROWS, :] = pick(table, sends[1:2, :])
     second[ROWS:, :] = fold(pick(table, sends[5:6, :]))
-    third[...] = pick(table, sends[2:3, :])
-    fourth[...] = pick(table, sends[3:4, :])
-
-
-def bonds_into(total, table, index, inside, tangent, position, stiffness, rest_length, intact, owned):
-    count = position.shape[1]
+
+
+def bonds_into(total, table, index, inside, tangent, position, stiffness, rest_length, weights):
     tang = tangent.shape[1]
-    slot = lax.broadcasted_iota(jnp.int32, (1, count), 1)
-    live = slot < owned
     own = [tangent[c] for c in range(3)]
     force = [total[3 * tang + c : 3 * tang + c + 1, :] for c in range(3)]
     for bond in range(index.shape[0]):
         rows = pick(table, index[bond : bond + 1, :])
-        weight = jnp.where(live & inside[bond : bond + 1, :], intact[bond : bond + 1, :].astype(jnp.float32), 0.0)
+        weight = jnp.where(inside[bond : bond + 1, :], weights[bond : bond + 1, :], 0.0)
         stiff = stiffness[bond : bond + 1, :] * weight
         rest = rest_length[bond : bond + 1, :]
         delta = [rows[3 * tang + c : 3 * tang + c + 1, :] - position[c : c + 1, :] for c in range(3)]
@@ -115,63 +110,95 @@
         total[3 * tang + c : 3 * tang + c + 1, :] = force[c]
 
 
-def place_of(index, odd):
+def place_of(index, odd_l, odd_h):
     own = index < 512
     face = (index - 512) >> 8
     is_corner = index >= 1536
     corner = (index - 1536) >> 4
     upward = jnp.where(is_corner, corner & 1, (face >> 1) & 1)
     forward = jnp.where(is_corner, corner >> 1, (face >> 1) & 1)
-    second_l = jnp.where(forward == odd[0], 1, 0)
-    second_h = jnp.where(upward == odd[1], 1, 0)
+    second_l = jnp.where(forward == odd_l, 1, 0)
+    second_h = jnp.where(upward == odd_h, 1, 0)
     on_l = (face == 0) | (face == 3)
     at_face = jnp.where(on_l, 512 + 256 * second_l, 1280 - 256 * second_h) + (index & 255)
     at_corner = 1536 + 32 * second_h + 16 * (second_l ^ second_h) + (index & 15)
     return jnp.where(own, index, jnp.where(is_corner, at_corner, at_face))
 
 
-def pack_kernel(tangent, position, sends, first, second, third, fourth):
-    table = halves(stacked(tangent[...], position[...]))
-    pack(table, sends, first, second, third, fourth)
-
-
-def own_kernel(odd, owned, params, tangent, position, basis, stiffness, rest_length, neighbours, intact, total):
+def first_kernel(odd, tangent, position, faces, corners, params, first, second, sends, rates, line):
+    rates[...] = params[...]
+    odd_l = odd[0:1, :FACE]
+    odd_h = odd[1:2, :FACE]
+    near_l = odd[0:1, :128]
+    near_h = odd[1:2, :128]
+    line[...] = jnp.zeros(line.shape, jnp.int32)
+    line[0:4, 0:CORNER] = corners[...]
+    lane = lax.broadcasted_iota(jnp.int32, (8, 128), 1)
+    spread = jnp.take_along_axis(line[...], lane & (CORNER - 1), axis=1, mode="promise_in_bounds")
+    low = (lane[0:1, :] & (2 * CORNER - 1)) < CORNER
+    rows = [spread[c : c + 1, :] for c in range(4)]
+    up = [jnp.where(near_h == 1, rows[2 * a + 1], rows[2 * a]) for a in range(2)]
+    down = [jnp.where(near_h == 1, rows[2 * a], rows[2 * a + 1]) for a in range(2)]
+    one = jnp.where(low, jnp.where(near_l == 1, up[1], up[0]), jnp.where(near_l == 1, down[1], down[0]))
+    two = jnp.where(low, jnp.where(near_l == 1, down[0], down[1]), jnp.where(near_l == 1, up[0], up[1]))
+    sends[0:1, :] = jnp.where(odd_l == 1, faces[3:4, :], faces[0:1, :])
+    sends[1:2, :] = jnp.where(odd_l == 1, faces[0:1, :], faces[3:4, :])
+    sends[2:3, :] = jnp.where(odd_h == 1, faces[2:3, :], faces[1:2, :])
+    sends[3:4, :] = jnp.where(odd_h == 1, faces[1:2, :], faces[2:3, :])
+    sends[4:5, :] = jnp.concatenate([one, one], axis=1)
+    sends[5:6, :] = jnp.concatenate([two, two], axis=1)
+    sends[6:8, :] = jnp.zeros((2, FACE), jnp.int32)
+    pack_len(halves(stacked(tangent[...], position[...])), sends, first, second)
+
+
+def own_bonds(params, tangent, position, basis, stiffness, rest_length, index, weights, sends, total, third, fourth):
     tang = tangent.shape[1]
     count = position.shape[1]
+    table = halves(stacked(tangent[...], position[...]))
+    third[...] = pick(table, sends[2:3, :])
+    fourth[...] = pick(table, sends[3:4, :])
     for c in range(3):
         total[c * tang : (c + 1) * tang, :] = basis[c]
-        outer = jnp.zeros((1, count), jnp.float32)
-        for p in range(tang):
-            outer = outer + params[p] * basis[c, p : p + 1, :]
-        total[3 * tang + c : 3 * tang + c + 1, :] = outer
+        total[3 * tang + c : 3 * tang + c + 1, :] = jnp.dot(params[...], basis[c], precision=lax.Precision.HIGHEST, preferred_element_type=jnp.float32)
     total[3 * tang + 3 : ROWS, :] = jnp.zeros((ROWS - 3 * tang - 3, count), jnp.float32)
-    table = halves(stacked(tangent[...], position[...]))
+    bonds_into(total, table, index, index < 512, tangent, position, stiffness, rest_length, weights)
+
+
+def own_kernel(odd, owned, params, tangent, position, basis, stiffness, rest_length, neighbours, intact, sends, total, third, fourth, placed, weights):
     index = neighbours[...]
-    inside = index < 512
-    bonds_into(total, table, index, inside, tangent, position, stiffness, rest_length, intact, owned[0])
-
-
-def side_kernel(odd, owned, before, first, second, both, tangent, position, stiffness, rest_length, neighbours, intact, total):
+    placed[...] = place_of(index, odd[0:1, :], odd[1:2, :])
+    slot = lax.broadcasted_iota(jnp.int32, index.shape, 1)
+    weights[...] = jnp.where(slot < owned[...], intact[...].astype(jnp.float32), 0.0)
+    own_bonds(params, tangent, position, basis, stiffness, rest_length, index, weights, sends, total, third, fourth)
+
+
+def own_again_kernel(params, tangent, position, basis, stiffness, rest_length, placed, weights, sends, total, third, fourth):
+    own_bonds(params, tangent, position, basis, stiffness, rest_length, placed[...], weights, sends, total, third, fourth)
+
+
+def partner(both, odd):
+    return jnp.where(odd[1:2, :FACE] == 1, both[0], both[1])
+
+
+def side_kernel(odd, before, first, second, both, tangent, position, stiffness, rest_length, placed, weights, total):
     total[...] = before[...]
-    fourth = both.at[1 - odd[1]]
-    table = halves(jnp.concatenate([first[:ROWS, :], second[:ROWS, :], fourth[:ROWS, :]], axis=1))
-    index = place_of(neighbours[...], odd) - 512
+    table = halves(jnp.concatenate([first[:ROWS, :], second[:ROWS, :], partner(both, odd)[:ROWS, :]], axis=1))
+    index = placed[...] - 512
     inside = (index >= 0) & (index < 768)
-    bonds_into(total, table, index, inside, tangent, position, stiffness, rest_length, intact, owned[0])
+    bonds_into(total, table, index, inside, tangent, position, stiffness, rest_length, weights)
 
 
 def height_kernel(last):
-    def body(odd, owned, before, third, both, tangent, position, tangent_vel, velocity, mass, stiffness, rest_length, neighbours, intact, sends, *outs):
+    def body(odd, before, third, both, tangent, position, tangent_vel, velocity, mass, stiffness, rest_length, placed, weights, sends, *outs):
         new_tangent, new_position, new_tangent_vel, new_velocity = outs[:4]
         total = outs[-1]
         tang = tangent.shape[1]
         total[...] = before[...]
-        fourth = both.at[1 - odd[1]]
-        corners = unfold(third[ROWS:, :], fourth[ROWS:, :])
+        corners = unfold(third[ROWS:, :], partner(both, odd)[ROWS:, :])
         table = halves(jnp.concatenate([third[:ROWS, :], corners], axis=1))[:, : FACE + 64]
-        index = place_of(neighbours[...], odd) - 1280
+        index = placed[...] - 1280
         inside = index >= 0
-        bonds_into(total, table, index, inside, tangent, position, stiffness, rest_length, intact, owned[0])
+        bonds_into(total, table, index, inside, tangent, position, stiffness, rest_length, weights)
         pace = DT / mass[...]
         for c in range(3):
             speed = tangent_vel[c] + pace * total[c * tang : (c + 1) * tang, :]
@@ -182,7 +209,7 @@
         new_position[...] = position[...] + DT * speed
         if not last:
             table = halves(stacked(new_tangent[...], new_position[...]))
-            pack(table, sends, *outs[4:8])
+            pack_len(table, sends, *outs[4:6])
 
     return body
 
@@ -191,12 +218,12 @@
     return pl.CostEstimate(flops=2 * 2 * ROWS * columns * bonds * 512, bytes_accessed=moved, transcendentals=0)
 
 
+def i32(*shape):
+    return jax.ShapeDtypeStruct(shape, jnp.int32)
+
+
 def f32(*shape):
     return jax.ShapeDtypeStruct(shape, jnp.float32)
-
-
-VMEM = pl.BlockSpec(memory_space=pltpu.VMEM)
-SMEM = pl.BlockSpec(memory_space=pltpu.SMEM)
 
 
 def on_device(
@@ -220,69 +247,62 @@
     strips, levels = lax.axis_size("len"), lax.axis_size("height")
     odd_l = lax.axis_index("len") % 2
     odd_h = lax.axis_index("height") % 2
-    odd = jnp.stack([odd_l, odd_h]).astype(jnp.int32)
+    odd = jnp.stack([jnp.full((count,), odd_l, jnp.int32), jnp.full((count,), odd_h, jnp.int32)])
     mass = mass.reshape(1, count)
 
-    def either(flag, yes, no):
-        return jnp.where(flag == 1, yes, no)
-
-    up = [either(odd_h, corner_lists[2 * a + 1], corner_lists[2 * a]) for a in range(2)]
-    down = [either(odd_h, corner_lists[2 * a], corner_lists[2 * a + 1]) for a in range(2)]
-    sends = jnp.stack(
-        [
-            either(odd_l, face_lists[3], face_lists[0]),
-            either(odd_l, face_lists[0], face_lists[3]),
-            either(odd_h, face_lists[2], face_lists[1]),
-            either(odd_h, face_lists[1], face_lists[2]),
-            jnp.tile(jnp.concatenate([either(odd_l, up[1], up[0]), either(odd_l, down[1], down[0])]), 8),
-            jnp.tile(jnp.concatenate([either(odd_l, down[0], down[1]), either(odd_l, up[0], up[1])]), 8),
-        ]
-    )
     low = lax.broadcasted_iota(jnp.int32, (MESSAGE - ROWS, FACE), 1) % 32 < CORNER
-    packed = (f32(MESSAGE, FACE), f32(MESSAGE, FACE), f32(ROWS, FACE), f32(ROWS, FACE))
-    messages = pl.pallas_call(
-        pack_kernel,
-        out_shape=packed,
+    packed = (f32(MESSAGE, FACE), f32(MESSAGE, FACE))
+    *messages, sends, rates = pl.pallas_call(
+        first_kernel,
+        out_shape=packed + (i32(8, FACE), f32(1, params.shape[0])),
+        scratch_shapes=[pltpu.VMEM((8, 128), jnp.int32)],
         compiler_params=PARAMS,
         cost_estimate=cost(512, 3, 700000),
-        name="pack",
-    )(tangent_pos, position, sends)
+        name="first_messages",
+    )(odd, tangent_pos, position, face_lists, corner_lists, params.reshape(1, -1))
     for step in range(STEPS):
         last = step == STEPS - 1
         first = lax.ppermute(messages[0], AXES, matching(strips, levels, 0, 1))
         second = lax.ppermute(messages[1], AXES, matching(strips, levels, 0, 0))
-        total = pl.pallas_call(
-            own_kernel,
-            out_shape=f32(ROWS, count),
-            in_specs=[SMEM] * 3 + [VMEM] * 7,
-            compiler_params=PARAMS,
-            cost_estimate=cost(512, bonds, 1000000),
-            name="own_bonds",
-        )(odd, owned, params, tangent_pos, position, load_basis, stiffness, rest_length, neighbours, intact)
+        made = (f32(ROWS, count), f32(ROWS, FACE), f32(ROWS, FACE))
+        if step == 0:
+            total, faces_z, faces_core, placed, weights = pl.pallas_call(
+                own_kernel,
+                out_shape=made + (i32(bonds, count), f32(bonds, count)),
+                compiler_params=PARAMS,
+                cost_estimate=cost(512, bonds, 1000000),
+                name="own_bonds",
+            )(odd, owned.reshape(1, 1), rates, tangent_pos, position, load_basis, stiffness, rest_length, neighbours, intact, sends)
+        else:
+            total, faces_z, faces_core = pl.pallas_call(
+                own_again_kernel,
+                out_shape=made,
+                compiler_params=PARAMS,
+                cost_estimate=cost(512, bonds, 1000000),
+                name="own_bonds_again",
+            )(rates, tangent_pos, position, load_basis, stiffness, rest_length, placed, weights, sends)
         first, second, total = lax.optimization_barrier((first, second, total))
         mine = jnp.where(low, second[ROWS:], first[ROWS:])
-        beside = jnp.concatenate([messages[3], mine])
+        beside = jnp.concatenate([faces_core, mine])
         mine = jnp.where(low, first[ROWS:], second[ROWS:])
-        third = lax.ppermute(jnp.concatenate([messages[2], mine]), AXES, matching(strips, levels, 1, 1))
+        third = lax.ppermute(jnp.concatenate([faces_z, mine]), AXES, matching(strips, levels, 1, 1))
         both = lax.all_gather(beside, AXES, axis_index_groups=couples(strips, levels))
         total = pl.pallas_call(
             side_kernel,
             out_shape=f32(ROWS, count),
-            in_specs=[SMEM] * 2 + [VMEM] * 10,
             compiler_params=PARAMS,
             cost_estimate=cost(1, bonds, 1000),
             name="side_bonds",
-        )(odd, owned, total, first, second, both, tangent_pos, position, stiffness, rest_length, neighbours, intact)
+        )(odd, total, first, second, both, tangent_pos, position, stiffness, rest_length, placed, weights)
         state = (f32(*tangent_pos.shape), f32(*position.shape), f32(*tangent_pos.shape), f32(*position.shape))
         out = pl.pallas_call(
             height_kernel(last),
             out_shape=state if last else state + packed,
-            in_specs=[SMEM] * 2 + [VMEM] * 13,
             scratch_shapes=[pltpu.VMEM((ROWS, count), jnp.float32)],
             compiler_params=PARAMS,
             cost_estimate=cost(320, bonds, 1500000),
             name="height_bonds",
-        )(odd, owned, total, third, both, tangent_pos, position, tangent_vel, velocity, mass, stiffness, rest_length, neighbours, intact, sends)
+        )(odd, total, third, both, tangent_pos, position, tangent_vel, velocity, mass, stiffness, rest_length, placed, weights, sends)
         tangent_pos, position, tangent_vel, velocity = out[:4]
         messages = out[4:]
     return (position, velocity, tangent_pos, tangent_vel)

time: 57.9 us -> 54.2 us (0.936)
  Pallas kernels: 16.9 us -> 14 us
  local copies, waits for them, and re-layouts: 3.04 us -> 1.64 us
  waiting for transfers between devices: 3.71 us -> 4.56 us
    pallas_call x5, Pallas kernels: 11.3 us -> 9.56 us  [the longest x2 4.91 us: on_device(): pl.pallas_call(side_kernel, out_shape=f32(ROWS, count), compiler_params=P...]
    unnamed x28 -> x26, local copies, waits for them, and re-layouts: 2.85 us -> 1.56 us
    pallas_call x2, Pallas kernels: 5.68 us -> 4.48 us  [on_device(): pl.pallas_call(height_kernel(last), out_shape=state if last else state +...]
  transfers between devices with their start and end apart: 6 -> 6, of which waited for: 2 -> 3; matrix products, arithmetic and copies ran while one was open for 0% -> 0% of each run, Pallas kernels for 19% -> 17%
where the time goes in v4:
time: 54.2 us; the launch traced here: 53.9 us
  starting transfers between devices  27.9 us (51%)
  Pallas kernels  14 us (26%)
  waiting for transfers between devices  4.56 us (8%)
  blocking collectives  4.14 us (8%)
  local copies, waits for them, and re-layouts  1.64 us (3%)
  between operations  1.57 us (3%)
    ppermute x2, starting transfers between devices, on_device(): lax.ppermute(jnp.concatenate([faces_z, mine]), AXES, matching(strips, lev...  13.9 us
    ppermute x2, starting transfers between devices, on_device(): first = lax.ppermute(messages[0], AXES, matching(strips, levels, 0, 1))  7.44 us
    ppermute x2, starting transfers between devices, on_device(): second = lax.ppermute(messages[1], AXES, matching(strips, levels, 0, 0))  6.47 us
    pallas_call x2, Pallas kernels, on_device(): pl.pallas_call(side_kernel, out_shape=f32(ROWS, count), compiler_params=P...  4.91 us
    pallas_call x2, Pallas kernels, on_device(): pl.pallas_call(height_kernel(last), out_shape=state if last else state +...  4.48 us
    all_gather x2, blocking collectives, on_device(): lax.all_gather(beside, AXES, axis_index_groups=couples(strips, levels))  4.14 us
    ppermute x2, waiting for transfers between devices, on_device(): second = lax.ppermute(messages[1], AXES, matching(strips, levels, 0, 0))  3.11 us
    pallas_call x1, Pallas kernels, on_device(): pl.pallas_call(own_kernel, out_shape=made + (i32(bonds, count), f32(bonds...  2.13 us
  transfers between devices with their start and end apart: 6, of which 3 were waited for; matrix products, arithmetic and copies ran while one was open for 0% of the time, Pallas kernels for 17%

profile of v4, /device:TPU:14, one launch (start us, length us, event | category | flops | bytes accessed | tf_op | source)
XLA Modules:
  0.0 53.9 jit_solution(2827220301391017000)
XLA Ops:
  0.6 0.0 copy-start.3
  0.7 0.0 copy-start.9
  0.7 0.0 copy-start.10
  0.7 0.0 copy-start.12
  0.7 0.1 stack.6.odd
  0.8 0.6 %copy-done.3 = f32[3,512]{1,0:T(4,128)S(1)} copy-done((f32[3,512]{1,0:T(4,128)S(1)}, f32[3,512]{1,0:T(4,128)}, u32[]{:S(2)}) %copy-start.3) | copy-done | bytes 6168
  1.3 0.0 copy-done.9
  1.3 0.0 copy-done.10
  1.4 0.0 copy-done.12
  1.4 0.0 copy-start
  1.4 0.9 %copy-done = f32[3,32,512]{2,1,0:T(8,128)S(1)} copy-done((f32[3,32,512]{2,1,0:T(8,128)S(1)}, f32[3,32,512]{2,1,0:T(8,128)}, u32[]{:S(2)}) %copy-start) | copy-done | bytes 196632
  2.3 0.0 copy-start.1
  2.3 0.0 copy-start.2
  2.3 0.0 copy-start.5
  2.3 0.0 copy-start.6
  2.3 0.0 copy-start.7
  2.3 0.5 first_messages.1
  2.8 3.5 %collective-permute-start = (f32[120,256]{1,0:T(8,128)S(1)}, f32[120,256]{1,0:T(8,128)S(1)}, u32[]{:S(2)}, u32[]{:S(2)}) collective-permute-start(f32[120,256]{1,0:T(8,128)S(1)} %get-tuple-element.32), channel_id=1, source_target_pairs={{32,64},{33,65},{34,66},{35,67},{36,68},{37,69},{38,70},{39,71},{4... | collective-permute-start | bytes 368648 | tf_op jit(solution)/shard_map/ppermute | solution.py:265
  6.3 4.5 %collective-permute-start.1 = (f32[120,256]{1,0:T(8,128)S(1)}, f32[120,256]{1,0:T(8,128)S(1)}, u32[]{:S(2)}, u32[]{:S(2)}) collective-permute-start(f32[120,256]{1,0:T(8,128)S(1)} %get-tuple-element.33), channel_id=1, source_target_pairs={{0,32},{1,33},{2,34},{3,35},{4,36},{5,37},{6,38},{7,39},{8,40},{9,... | collective-permute-start | bytes 368648 | tf_op jit(solution)/shard_map/ppermute | solution.py:266
  11.5 0.0 copy-done.1
  11.5 0.0 copy-done.2
  11.5 0.0 copy-done.5
  11.5 0.0 copy-done.6
  11.5 0.0 copy-done.7
  11.5 2.1 %own_bonds.1 = (f32[104,512]{1,0:T(8,128)S(1)}, f32[104,256]{1,0:T(8,128)S(1)}, f32[104,256]{1,0:T(8,128)S(1)}, s32[12,512]{1,0:T(8,128)S(1)}, f32[12,512]{1,0:T(8,128)S(1)}) custom-call(s32[2,512]{1,0:T(2,128)S(1)} %stack.6.odd, s32[1,1]{1,0:T(1,128)} %bitcast.6.owned, f32[1,32]{1,0:T(1,128)S(1)} %get-tuple-element.34.params, f32[3,32,512]{2,1,0:T(8,128)S(1)} %copy-done, ...), custom_call_target="tpu_custom_call" | custom-call | flops 1308622848 | bytes 1000000 | tf_op jit(solution)/shard_map/own_bonds/pallas_call | solution.py:269
  13.7 0.0 collective-permute-done.first
  13.7 0.2 collective-permute-done.1.second
  13.9 10.2 %collective-permute-start.2 = (f32[120,256]{1,0:T(8,128)S(1)}, f32[120,256]{1,0:T(8,128)S(1)}, u32[]{:S(2)}, u32[]{:S(2)}) collective-permute-start(f32[120,256]{1,0:T(8,128)S(1)} %pad_maximum_fusion.1), channel_id=1, source_target_pairs={{1,2},{2,1},{3,4},{4,3},{5,6},{6,5},{7,8},{8,7},{9,10},{10,9},{11,... | collective-permute-start | bytes 368648 | tf_op jit(solution)/shard_map/ppermute | solution.py:288
  24.1 2.0 %all-gather = f32[240,256]{1,0:T(8,128)S(1)} all-gather(f32[120,256]{1,0:T(8,128)S(1)} %pad_maximum_fusion), channel_id=2, replica_groups={{0,1},{2,3},{4,5},{6,7},{8,9},{10,11},{12,13},{14,15},{16,17},{18,19},{..., dimensions={0}, use_global_device_ids=true | all-gather | bytes 368640 | tf_op jit(solution)/shard_map/all_gather | solution.py:289
  26.1 0.0 copy-start.4
  26.1 0.0 copy-start.8
  26.1 0.0 copy-start.11
  26.1 2.4 %side_bonds.2.before = f32[104,512]{1,0:T(8,128)S(1)} custom-call(s32[2,512]{1,0:T(2,128)S(1)} %stack.6.odd, f32[104,512]{1,0:T(8,128)S(1)} %get-tuple-element.37.before, f32[120,256]{1,0:T(8,128)S(1)} %collective-permute-done.first, f32[120,256]{1,0:T(8,128)S(1)} %collective-permute-done.1.second, f32[2,120,256]{2,1,0:T(8,128)S(1)} %bitcast.9, ...), custom_call_target="tpu_custom_call" | custom-call | flops 2555904 | bytes 1000 | tf_op jit(solution)/shard_map/side_bonds/pallas_call | solution.py:290
  28.6 0.0 collective-permute-done.2.third
  28.6 0.0 copy-done.4
  28.6 0.0 copy-done.8
  28.6 0.0 copy-done.11
  28.6 2.0 %height_bonds.2 = (f32[3,32,512]{2,1,0:T(8,128)S(1)}, f32[3,512]{1,0:T(4,128)S(1)}, f32[3,32,512]{2,1,0:T(8,128)S(1)}, f32[3,512]{1,0:T(4,128)S(1)}, f32[120,256]{1,0:T(8,128)S(1)}, /*index=5*/f32[120,256]{1,0:T(8,128)S(1)}) custom-call(s32[2,512]{1,0:T(2,128)S(1)} %stack.6.odd, f32[104,512]{1,0:T(8,128)S(1)} %side_bonds.2.before, ...), custom_call_target="tpu_custom_call" | custom-call | flops 817889280 | bytes 1500000 | tf_op jit(solution)/shard_map/height_bonds/pallas_call | solution.py:298
  30.6 4.0 %collective-permute-start.3 = (f32[120,256]{1,0:T(8,128)S(1)}, f32[120,256]{1,0:T(8,128)S(1)}, u32[]{:S(2)}, u32[]{:S(2)}) collective-permute-start(f32[120,256]{1,0:T(8,128)S(1)} %get-tuple-element.44), channel_id=1, source_target_pairs={{32,64},{33,65},{34,66},{35,67},{36,68},{37,69},{38,70},{39,71},{4... | collective-permute-start | bytes 368648 | tf_op jit(solution)/shard_map/ppermute | solution.py:265
  34.6 2.0 %collective-permute-start.4 = (f32[120,256]{1,0:T(8,128)S(1)}, f32[120,256]{1,0:T(8,128)S(1)}, u32[]{:S(2)}, u32[]{:S(2)}) collective-permute-start(f32[120,256]{1,0:T(8,128)S(1)} %get-tuple-element.45), channel_id=1, source_target_pairs={{0,32},{1,33},{2,34},{3,35},{4,36},{5,37},{6,38},{7,39},{8,40},{9,... | collective-permute-start | bytes 368648 | tf_op jit(solution)/shard_map/ppermute | solution.py:266
  36.6 2.1 %own_bonds_again.1 = (f32[104,512]{1,0:T(8,128)S(1)}, f32[104,256]{1,0:T(8,128)S(1)}, f32[104,256]{1,0:T(8,128)S(1)}) custom-call(f32[1,32]{1,0:T(1,128)S(1)} %get-tuple-element.34.params, f32[3,32,512]{2,1,0:T(8,128)S(1)} %get-tuple-element.46.tangent, f32[3,512]{1,0:T(4,128)S(1)} %get-tuple-element.47.position, f32[3,32,512]{2,1,0:T(8,128)S(1)} %copy-done.5, ...), custom_call_target="tpu_custom_call" | custom-call | flops 1308622848 | bytes 1000000 | tf_op jit(solution)/shard_map/own_bonds_again/pallas_call | solution.py:277
  38.6 0.0 collective-permute-done.3.first
  38.6 3.0 %collective-permute-done.4.second = f32[120,256]{1,0:T(8,128)S(1)} collective-permute-done((f32[120,256]{1,0:T(8,128)S(1)}, f32[120,256]{1,0:T(8,128)S(1)}, u32[]{:S(2)}, u32[]{:S(2)}) %collective-permute-start.4) | collective-permute-done | bytes 122912 | tf_op jit(solution)/shard_map/ppermute | solution.py:266
  41.6 3.7 %collective-permute-start.5 = (f32[120,256]{1,0:T(8,128)S(1)}, f32[120,256]{1,0:T(8,128)S(1)}, u32[]{:S(2)}, u32[]{:S(2)}) collective-permute-start(f32[120,256]{1,0:T(8,128)S(1)} %pad_maximum_fusion.3), channel_id=1, source_target_pairs={{1,2},{2,1},{3,4},{4,3},{5,6},{6,5},{7,8},{8,7},{9,10},{10,9},{11,... | collective-permute-start | bytes 368648 | tf_op jit(solution)/shard_map/ppermute | solution.py:288
  45.3 2.2 %all-gather.1 = f32[240,256]{1,0:T(8,128)S(1)} all-gather(f32[120,256]{1,0:T(8,128)S(1)} %pad_maximum_fusion.2), channel_id=3, replica_groups={{0,1},{2,3},{4,5},{6,7},{8,9},{10,11},{12,13},{14,15},{16,17},{18,19},{..., dimensions={0}, use_global_device_ids=true | all-gather | bytes 368640 | tf_op jit(solution)/shard_map/all_gather | solution.py:289
  47.5 2.5 %side_bonds.3.before = f32[104,512]{1,0:T(8,128)S(1)} custom-call(s32[2,512]{1,0:T(2,128)S(1)} %stack.6.odd, f32[104,512]{1,0:T(8,128)S(1)} %get-tuple-element.49.before, f32[120,256]{1,0:T(8,128)S(1)} %collective-permute-done.3.first, f32[120,256]{1,0:T(8,128)S(1)} %collective-permute-done.4.second, f32[2,120,256]{2,1,0:T(8,128)S(1)} %bitcast.7, ...), custom_call_target="tpu_custom_call" | custom-call | flops 2555904 | bytes 1000 | tf_op jit(solution)/shard_map/side_bonds/pallas_call | solution.py:290
  50.0 1.4 %collective-permute-done.5.third = f32[120,256]{1,0:T(8,128)S(1)} collective-permute-done((f32[120,256]{1,0:T(8,128)S(1)}, f32[120,256]{1,0:T(8,128)S(1)}, u32[]{:S(2)}, u32[]{:S(2)}) %collective-permute-start.5) | collective-permute-done | bytes 122912 | tf_op jit(solution)/shard_map/ppermute | solution.py:288
  51.4 2.5 %height_bonds.3 = (f32[3,32,512]{2,1,0:T(8,128)}, f32[3,512]{1,0:T(4,128)}, f32[3,32,512]{2,1,0:T(8,128)}, f32[3,512]{1,0:T(4,128)}) custom-call(s32[2,512]{1,0:T(2,128)S(1)} %stack.6.odd, f32[104,512]{1,0:T(8,128)S(1)} %side_bonds.3.before, f32[120,256]{1,0:T(8,128)S(1)} %collective-permute-done.5.third, f32[2,120,256]{2,1,0:T(8,128)S(1)} %bitcast.8, ...), custom_call_target="tpu_custom_call" | custom-call | flops 817889280 | bytes 1500000 | tf_op jit(solution)/shard_map/height_bonds/pallas_call | solution.py:298
  (9 shorter events, 0.1 us)
Async XLA Ops:
  0.6 0.7 %copy-start.3 = (f32[3,512]{1,0:T(4,128)S(1)}, f32[3,512]{1,0:T(4,128)}, u32[]{:S(2)}) copy-start(f32[3,512]{1,0:T(4,128)} %position.7) | copy-start | bytes 18436
  0.7 0.7 %copy-start.9 = (s32[4,256]{1,0:T(4,128)S(1)}, s32[4,256]{1,0:T(4,128)}, u32[]{:S(2)}) copy-start(s32[4,256]{1,0:T(4,128)} %faces.1) | copy-start | bytes 12292
  0.7 0.7 %copy-start.10 = (s32[4,16]{1,0:T(4,128)S(1)}, s32[4,16]{1,0:T(4,128)}, u32[]{:S(2)}) copy-start(s32[4,16]{1,0:T(4,128)} %corners.1) | copy-start | bytes 772
  0.7 0.7 %copy-start.12 = (f32[32]{0:T(128)S(1)}, f32[32]{0:T(128)}, u32[]{:S(2)}) copy-start(f32[32]{0:T(128)} %param.20) | copy-start | bytes 388
  1.4 0.9 %copy-start = (f32[3,32,512]{2,1,0:T(8,128)S(1)}, f32[3,32,512]{2,1,0:T(8,128)}, u32[]{:S(2)}) copy-start(f32[3,32,512]{2,1,0:T(8,128)} %tangent.7) | copy-start | bytes 589828
  2.3 9.2 %copy-start.1 = (f32[12,512]{1,0:T(8,128)S(1)}, f32[12,512]{1,0:T(8,128)}, u32[]{:S(2)}) copy-start(f32[12,512]{1,0:T(8,128)} %stiffness.11) | copy-start | bytes 73732
  2.3 9.2 %copy-start.2 = (f32[12,512]{1,0:T(8,128)S(1)}, f32[12,512]{1,0:T(8,128)}, u32[]{:S(2)}) copy-start(f32[12,512]{1,0:T(8,128)} %rest_length.11) | copy-start | bytes 73732
  2.3 9.2 %copy-start.5 = (f32[3,32,512]{2,1,0:T(8,128)S(1)}, f32[3,32,512]{2,1,0:T(8,128)}, u32[]{:S(2)}) copy-start(f32[3,32,512]{2,1,0:T(8,128)} %basis.3) | copy-start | bytes 589828
  2.3 9.2 %copy-start.6 = (s32[12,512]{1,0:T(8,128)S(1)}, s32[12,512]{1,0:T(8,128)}, u32[]{:S(2)}) copy-start(s32[12,512]{1,0:T(8,128)} %neighbours.1) | copy-start | bytes 73732
  2.3 9.2 %copy-start.7 = (s32[12,512]{1,0:T(8,128)S(1)}, s32[12,512]{1,0:T(8,128)}, u32[]{:S(2)}) copy-start(s32[12,512]{1,0:T(8,128)} %intact.1) | copy-start | bytes 73732
  2.8 10.9 %collective-permute-start = (f32[120,256]{1,0:T(8,128)S(1)}, f32[120,256]{1,0:T(8,128)S(1)}, u32[]{:S(2)}, u32[]{:S(2)}) collective-permute-start(f32[120,256]{1,0:T(8,128)S(1)} %get-tuple-element.32), channel_id=1, source_target_pairs={{32,64},{33,65},{34,66},{35,67},{36,68},{37,69},{38,70},{39,71},{4... | collective-permute-start | bytes 368648 | tf_op jit(solution)/shard_map/ppermute | solution.py:265
  6.3 7.5 %collective-permute-start.1 = (f32[120,256]{1,0:T(8,128)S(1)}, f32[120,256]{1,0:T(8,128)S(1)}, u32[]{:S(2)}, u32[]{:S(2)}) collective-permute-start(f32[120,256]{1,0:T(8,128)S(1)} %get-tuple-element.33), channel_id=1, source_target_pairs={{0,32},{1,33},{2,34},{3,35},{4,36},{5,37},{6,38},{7,39},{8,40},{9,... | collective-permute-start | bytes 368648 | tf_op jit(solution)/shard_map/ppermute | solution.py:266
  13.9 14.7 %collective-permute-start.2 = (f32[120,256]{1,0:T(8,128)S(1)}, f32[120,256]{1,0:T(8,128)S(1)}, u32[]{:S(2)}, u32[]{:S(2)}) collective-permute-start(f32[120,256]{1,0:T(8,128)S(1)} %pad_maximum_fusion.1), channel_id=1, source_target_pairs={{1,2},{2,1},{3,4},{4,3},{5,6},{6,5},{7,8},{8,7},{9,10},{10,9},{11,... | collective-permute-start | bytes 368648 | tf_op jit(solution)/shard_map/ppermute | solution.py:288
  26.1 2.5 %copy-start.4 = (f32[3,32,512]{2,1,0:T(8,128)S(1)}, f32[3,32,512]{2,1,0:T(8,128)}, u32[]{:S(2)}) copy-start(f32[3,32,512]{2,1,0:T(8,128)} %tangent_vel.1) | copy-start | bytes 589828
  26.1 2.5 %copy-start.8 = (f32[3,512]{1,0:T(4,128)S(1)}, f32[3,512]{1,0:T(4,128)}, u32[]{:S(2)}) copy-start(f32[3,512]{1,0:T(4,128)} %velocity.1) | copy-start | bytes 18436
  26.1 2.5 %copy-start.11 = (f32[512]{0:T(512)S(1)}, f32[512]{0:T(512)}, u32[]{:S(2)}) copy-start(f32[512]{0:T(512)} %param.18) | copy-start | bytes 6148
  30.6 8.0 %collective-permute-start.3 = (f32[120,256]{1,0:T(8,128)S(1)}, f32[120,256]{1,0:T(8,128)S(1)}, u32[]{:S(2)}, u32[]{:S(2)}) collective-permute-start(f32[120,256]{1,0:T(8,128)S(1)} %get-tuple-element.44), channel_id=1, source_target_pairs={{32,64},{33,65},{34,66},{35,67},{36,68},{37,69},{38,70},{39,71},{4... | collective-permute-start | bytes 368648 | tf_op jit(solution)/shard_map/ppermute | solution.py:265
  34.6 7.0 %collective-permute-start.4 = (f32[120,256]{1,0:T(8,128)S(1)}, f32[120,256]{1,0:T(8,128)S(1)}, u32[]{:S(2)}, u32[]{:S(2)}) collective-permute-start(f32[120,256]{1,0:T(8,128)S(1)} %get-tuple-element.45), channel_id=1, source_target_pairs={{0,32},{1,33},{2,34},{3,35},{4,36},{5,37},{6,38},{7,39},{8,40},{9,... | collective-permute-start | bytes 368648 | tf_op jit(solution)/shard_map/ppermute | solution.py:266
  41.6 9.8 %collective-permute-start.5 = (f32[120,256]{1,0:T(8,128)S(1)}, f32[120,256]{1,0:T(8,128)S(1)}, u32[]{:S(2)}, u32[]{:S(2)}) collective-permute-start(f32[120,256]{1,0:T(8,128)S(1)} %pad_maximum_fusion.3), channel_id=1, source_target_pairs={{1,2},{2,1},{3,4},{4,3},{5,6},{6,5},{7,8},{8,7},{9,10},{10,9},{11,... | collective-permute-start | bytes 368648 | tf_op jit(solution)/shard_map/ppermute | solution.py:288

commit v5 on v4

--- a/solution.py
+++ b/solution.py
@@ -10,7 +10,8 @@
 FACE = 256
 CORNER = 16
 ROWS = 104
-MESSAGE = ROWS + 16
+USED = 99
+MESSAGE = ROWS + 8
 GROUPS = ROWS // 8
 AXES = ("len", "height")
 PARAMS = pltpu.CompilerParams(vmem_limit_bytes=16 * 2**20)
@@ -58,34 +59,53 @@
     return jnp.concatenate([flat, position, jnp.zeros((ROWS - tang - 3, lanes), jnp.float32)], axis=0)
 
 
-def fold(columns):
+def fold(columns, message):
     slot = lax.broadcasted_iota(jnp.int32, (8, FACE), 1) >> 5
+    level = lax.broadcasted_iota(jnp.int32, (8, FACE), 0)
+    part = jnp.zeros((8, FACE), jnp.float32)
+    for group in range(GROUPS):
+        block = columns[8 * group : 8 * group + 8, :]
+        block = jnp.concatenate([block, block], axis=1)
+        if group < 8:
+            part = jnp.where(slot == group, block, part)
+        else:
+            line = jnp.sum(jnp.where(slot == level, block, 0.0), axis=0, keepdims=True)
+            message[USED + group - 8 : USED + group - 7, :] = line
+    message[ROWS:, :] = part
+
+
+def raised(line):
+    level = lax.broadcasted_iota(jnp.int32, (8, 128), 0)
+    wide = jnp.broadcast_to(line, (8, FACE))
+    near = jnp.where(level < 4, wide[:, :128], wide[:, 128:])
+    rows = near
+    for run in range(1, 4):
+        rows = jnp.where((level & 3) == run, pltpu.roll(near, 128 - 32 * run, 1), rows)
+    return rows
+
+
+def unfold(one, two):
+    lane = lax.broadcasted_iota(jnp.int32, (8, 128), 1)
     parts = []
-    for first in range(0, GROUPS, 8):
-        part = jnp.zeros((8, FACE), jnp.float32)
-        for group in range(first, min(first + 8, GROUPS)):
-            part = jnp.where(slot == group - first, columns[8 * group : 8 * group + 8, :], part)
-        parts.append(part)
+    for group in range(GROUPS):
+        if group < 8:
+            back = (FACE - 32 * group) % FACE
+            left, right = one[ROWS:, :], two[ROWS:, :]
+            left = pltpu.roll(left, back, 1) if back else left
+            right = pltpu.roll(right, (back + 32) % FACE, 1) if (back + 32) % FACE else right
+        else:
+            left, right = [raised(message[USED + group - 8 : USED + group - 7, :]) for message in (one, two)]
+            right = pltpu.roll(right, 32, 1)
+        parts.append(jnp.where(lane < 32, left[:, :128], right[:, :128]))
     return jnp.concatenate(parts, axis=0)
 
 
-def unfold(one, two):
-    lane = lax.broadcasted_iota(jnp.int32, (16, 128), 1)
-    moved = []
-    for slot in range(8):
-        back = (FACE - 32 * slot) % FACE
-        left = one if back == 0 else pltpu.roll(one, back, 1)
-        right = pltpu.roll(two, (back + 32) % FACE, 1) if (back + 32) % FACE else two
-        moved.append(jnp.where(lane < 32, left[:, :128], right[:, :128]))
-    parts = [moved[group % 8][8 * (group // 8) : 8 * (group // 8) + 8, :] for group in range(GROUPS)]
-    return jnp.concatenate(parts, axis=0)
-
-
 def pack_len(table, sends, first, second):
+    corners = pick(table, jnp.concatenate([sends[4:5, :128], sends[5:6, :128]], axis=1))
     first[:ROWS, :] = pick(table, sends[0:1, :])
-    first[ROWS:, :] = fold(pick(table, sends[4:5, :]))
+    fold(corners[:, :128], first)
     second[:ROWS, :] = pick(table, sends[1:2, :])
-    second[ROWS:, :] = fold(pick(table, sends[5:6, :]))
+    fold(corners[:, 128:], second)
 
 
 def bonds_into(total, table, index, inside, tangent, position, stiffness, rest_length, weights):
@@ -194,7 +214,7 @@
         total = outs[-1]
         tang = tangent.shape[1]
         total[...] = before[...]
-        corners = unfold(third[ROWS:, :], partner(both, odd)[ROWS:, :])
+        corners = unfold(third[...], partner(both, odd))
         table = halves(jnp.concatenate([third[:ROWS, :], corners], axis=1))[:, : FACE + 64]
         index = placed[...] - 1280
         inside = index >= 0
@@ -250,7 +270,7 @@
     odd = jnp.stack([jnp.full((count,), odd_l, jnp.int32), jnp.full((count,), odd_h, jnp.int32)])
     mass = mass.reshape(1, count)
 
-    low = lax.broadcasted_iota(jnp.int32, (MESSAGE - ROWS, FACE), 1) % 32 < CORNER
+    low = lax.broadcasted_iota(jnp.int32, (MESSAGE - USED, FACE), 1) % 32 < CORNER
     packed = (f32(MESSAGE, FACE), f32(MESSAGE, FACE))
     *messages, sends, rates = pl.pallas_call(
         first_kernel,
@@ -282,10 +302,10 @@
                 name="own_bonds_again",
             )(rates, tangent_pos, position, load_basis, stiffness, rest_length, placed, weights, sends)
         first, second, total = lax.optimization_barrier((first, second, total))
-        mine = jnp.where(low, second[ROWS:], first[ROWS:])
-        beside = jnp.concatenate([faces_core, mine])
-        mine = jnp.where(low, first[ROWS:], second[ROWS:])
-        third = lax.ppermute(jnp.concatenate([faces_z, mine]), AXES, matching(strips, levels, 1, 1))
+        mine = jnp.where(low, second[USED:], first[USED:])
+        beside = jnp.concatenate([faces_core[:USED], mine])
+        mine = jnp.where(low, first[USED:], second[USED:])
+        third = lax.ppermute(jnp.concatenate([faces_z[:USED], mine]), AXES, matching(strips, levels, 1, 1))
         both = lax.all_gather(beside, AXES, axis_index_groups=couples(strips, levels))
         total = pl.pallas_call(
             side_kernel,

time: 54.2 us -> 54 us (level)
  transfers between devices with their start and end apart: 6 -> 6, of which waited for: 3 -> 2; matrix products, arithmetic and copies ran while one was open for 0% -> 0% of each run, Pallas kernels for 17% -> 17%
where the time goes in v5:
time: 54 us; the launch traced here: 53.6 us
  starting transfers between devices  28 us (52%)
  Pallas kernels  14 us (26%)
  waiting for transfers between devices  4.22 us (8%)
  blocking collectives  4.12 us (8%)
  local copies, waits for them, and re-layouts  1.64 us (3%)
  between operations  1.6 us (3%)
    ppermute x2, starting transfers between devices, on_device(): lax.ppermute(jnp.concatenate([faces_z[:USED], mine]), AXES, matching(stri...  14.1 us
    ppermute x2, starting transfers between devices, on_device(): first = lax.ppermute(messages[0], AXES, matching(strips, levels, 0, 1))  7.46 us
    ppermute x2, starting transfers between devices, on_device(): second = lax.ppermute(messages[1], AXES, matching(strips, levels, 0, 0))  6.47 us
    pallas_call x2, Pallas kernels, on_device(): pl.pallas_call(side_kernel, out_shape=f32(ROWS, count), compiler_params=P...  4.85 us
    pallas_call x2, Pallas kernels, on_device(): pl.pallas_call(height_kernel(last), out_shape=state if last else state +...  4.53 us
    all_gather x2, blocking collectives, on_device(): lax.all_gather(beside, AXES, axis_index_groups=couples(strips, levels))  4.12 us
    ppermute x2, waiting for transfers between devices, on_device(): second = lax.ppermute(messages[1], AXES, matching(strips, levels, 0, 0))  2.82 us
    pallas_call x1, Pallas kernels, on_device(): pl.pallas_call(own_kernel, out_shape=made + (i32(bonds, count), f32(bonds...  2.13 us
  transfers between devices with their start and end apart: 6, of which 2 were waited for; matrix products, arithmetic and copies ran while one was open for 0% of the time, Pallas kernels for 17%

profile of v5, /device:TPU:14, one launch (start us, length us, event | category | flops | bytes accessed | tf_op | source)
XLA Modules:
  0.0 53.6 jit_solution(2224578829273639498)
XLA Ops:
  0.6 0.0 copy-start.3
  0.7 0.0 copy-start.9
  0.7 0.0 copy-start.10
  0.7 0.0 copy-start.12
  0.7 0.1 stack.6.odd
  0.8 0.6 %copy-done.3 = f32[3,512]{1,0:T(4,128)S(1)} copy-done((f32[3,512]{1,0:T(4,128)S(1)}, f32[3,512]{1,0:T(4,128)}, u32[]{:S(2)}) %copy-start.3) | copy-done | bytes 6168
  1.3 0.0 copy-done.9
  1.3 0.0 copy-done.10
  1.4 0.0 copy-done.12
  1.4 0.0 copy-start
  1.4 0.9 %copy-done = f32[3,32,512]{2,1,0:T(8,128)S(1)} copy-done((f32[3,32,512]{2,1,0:T(8,128)S(1)}, f32[3,32,512]{2,1,0:T(8,128)}, u32[]{:S(2)}) %copy-start) | copy-done | bytes 196632
  2.3 0.0 copy-start.1
  2.3 0.0 copy-start.2
  2.3 0.0 copy-start.5
  2.3 0.0 copy-start.6
  2.3 0.0 copy-start.7
  2.3 0.4 first_messages.1
  2.8 3.5 %collective-permute-start = (f32[112,256]{1,0:T(8,128)S(1)}, f32[112,256]{1,0:T(8,128)S(1)}, u32[]{:S(2)}, u32[]{:S(2)}) collective-permute-start(f32[112,256]{1,0:T(8,128)S(1)} %get-tuple-element.32), channel_id=1, source_target_pairs={{32,64},{33,65},{34,66},{35,67},{36,68},{37,69},{38,70},{39,71},{4... | collective-permute-start | bytes 344072 | tf_op jit(solution)/shard_map/ppermute | solution.py:285
  6.3 4.5 %collective-permute-start.1 = (f32[112,256]{1,0:T(8,128)S(1)}, f32[112,256]{1,0:T(8,128)S(1)}, u32[]{:S(2)}, u32[]{:S(2)}) collective-permute-start(f32[112,256]{1,0:T(8,128)S(1)} %get-tuple-element.33), channel_id=1, source_target_pairs={{0,32},{1,33},{2,34},{3,35},{4,36},{5,37},{6,38},{7,39},{8,40},{9,... | collective-permute-start | bytes 344072 | tf_op jit(solution)/shard_map/ppermute | solution.py:286
  11.4 0.0 copy-done.1
  11.4 0.0 copy-done.2
  11.4 0.0 copy-done.5
  11.5 0.0 copy-done.6
  11.5 0.0 copy-done.7
  11.5 2.1 %own_bonds.1 = (f32[104,512]{1,0:T(8,128)S(1)}, f32[104,256]{1,0:T(8,128)S(1)}, f32[104,256]{1,0:T(8,128)S(1)}, s32[12,512]{1,0:T(8,128)S(1)}, f32[12,512]{1,0:T(8,128)S(1)}) custom-call(s32[2,512]{1,0:T(2,128)S(1)} %stack.6.odd, s32[1,1]{1,0:T(1,128)} %bitcast.10.owned, f32[1,32]{1,0:T(1,128)S(1)} %get-tuple-element.34.params, f32[3,32,512]{2,1,0:T(8,128)S(1)} %copy-done, ...), custom_call_target="tpu_custom_call" | custom-call | flops 1308622848 | bytes 1000000 | tf_op jit(solution)/shard_map/own_bonds/pallas_call | solution.py:289
  13.6 0.0 collective-permute-done.first
  13.7 0.0 collective-permute-done.1.second
  13.7 10.4 %collective-permute-start.2 = (f32[112,256]{1,0:T(8,128)S(1)}, f32[112,256]{1,0:T(8,128)S(1)}, u32[]{:S(2)}, u32[]{:S(2)}) collective-permute-start(f32[112,256]{1,0:T(8,128)S(1)} %pad_maximum_fusion.1), channel_id=1, source_target_pairs={{1,2},{2,1},{3,4},{4,3},{5,6},{6,5},{7,8},{8,7},{9,10},{10,9},{11,... | collective-permute-start | bytes 344072 | tf_op jit(solution)/shard_map/ppermute | solution.py:308
  24.1 2.0 %all-gather = f32[224,256]{1,0:T(8,128)S(1)} all-gather(f32[112,256]{1,0:T(8,128)S(1)} %pad_maximum_fusion), channel_id=2, replica_groups={{0,1},{2,3},{4,5},{6,7},{8,9},{10,11},{12,13},{14,15},{16,17},{18,19},{..., dimensions={0}, use_global_device_ids=true | all-gather | bytes 344064 | tf_op jit(solution)/shard_map/all_gather | solution.py:309
  26.1 0.0 copy-start.4
  26.1 0.0 copy-start.8
  26.1 0.0 copy-start.11
  26.1 2.4 %side_bonds.2.before = f32[104,512]{1,0:T(8,128)S(1)} custom-call(s32[2,512]{1,0:T(2,128)S(1)} %stack.6.odd, f32[104,512]{1,0:T(8,128)S(1)} %get-tuple-element.37.before, f32[112,256]{1,0:T(8,128)S(1)} %collective-permute-done.first, f32[112,256]{1,0:T(8,128)S(1)} %collective-permute-done.1.second, f32[2,112,256]{2,1,0:T(8,128)S(1)} %bitcast.13, ...), custom_call_target="tpu_custom_call" | custom-call | flops 2555904 | bytes 1000 | tf_op jit(solution)/shard_map/side_bonds/pallas_call | solution.py:310
  28.5 0.0 collective-permute-done.2.third
  28.5 0.0 copy-done.4
  28.5 0.0 copy-done.8
  28.5 0.0 copy-done.11
  28.5 2.1 %height_bonds.2 = (f32[3,32,512]{2,1,0:T(8,128)S(1)}, f32[3,512]{1,0:T(4,128)S(1)}, f32[3,32,512]{2,1,0:T(8,128)S(1)}, f32[3,512]{1,0:T(4,128)S(1)}, f32[112,256]{1,0:T(8,128)S(1)}, /*index=5*/f32[112,256]{1,0:T(8,128)S(1)}) custom-call(s32[2,512]{1,0:T(2,128)S(1)} %stack.6.odd, f32[104,512]{1,0:T(8,128)S(1)} %side_bonds.2.before, ...), custom_call_target="tpu_custom_call" | custom-call | flops 817889280 | bytes 1500000 | tf_op jit(solution)/shard_map/height_bonds/pallas_call | solution.py:318
  30.6 4.0 %collective-permute-start.3 = (f32[112,256]{1,0:T(8,128)S(1)}, f32[112,256]{1,0:T(8,128)S(1)}, u32[]{:S(2)}, u32[]{:S(2)}) collective-permute-start(f32[112,256]{1,0:T(8,128)S(1)} %get-tuple-element.44), channel_id=1, source_target_pairs={{32,64},{33,65},{34,66},{35,67},{36,68},{37,69},{38,70},{39,71},{4... | collective-permute-start | bytes 344072 | tf_op jit(solution)/shard_map/ppermute | solution.py:285
  34.6 2.0 %collective-permute-start.4 = (f32[112,256]{1,0:T(8,128)S(1)}, f32[112,256]{1,0:T(8,128)S(1)}, u32[]{:S(2)}, u32[]{:S(2)}) collective-permute-start(f32[112,256]{1,0:T(8,128)S(1)} %get-tuple-element.45), channel_id=1, source_target_pairs={{0,32},{1,33},{2,34},{3,35},{4,36},{5,37},{6,38},{7,39},{8,40},{9,... | collective-permute-start | bytes 344072 | tf_op jit(solution)/shard_map/ppermute | solution.py:286
  36.5 2.0 %own_bonds_again.1 = (f32[104,512]{1,0:T(8,128)S(1)}, f32[104,256]{1,0:T(8,128)S(1)}, f32[104,256]{1,0:T(8,128)S(1)}) custom-call(f32[1,32]{1,0:T(1,128)S(1)} %get-tuple-element.34.params, f32[3,32,512]{2,1,0:T(8,128)S(1)} %get-tuple-element.46.tangent, f32[3,512]{1,0:T(4,128)S(1)} %get-tuple-element.47.position, f32[3,32,512]{2,1,0:T(8,128)S(1)} %copy-done.5, ...), custom_call_target="tpu_custom_call" | custom-call | flops 1308622848 | bytes 1000000 | tf_op jit(solution)/shard_map/own_bonds_again/pallas_call | solution.py:297
  38.6 0.0 collective-permute-done.3.first
  38.6 2.8 %collective-permute-done.4.second = f32[112,256]{1,0:T(8,128)S(1)} collective-permute-done((f32[112,256]{1,0:T(8,128)S(1)}, f32[112,256]{1,0:T(8,128)S(1)}, u32[]{:S(2)}, u32[]{:S(2)}) %collective-permute-start.4) | collective-permute-done | bytes 114720 | tf_op jit(solution)/shard_map/ppermute | solution.py:286
  41.4 3.7 %collective-permute-start.5 = (f32[112,256]{1,0:T(8,128)S(1)}, f32[112,256]{1,0:T(8,128)S(1)}, u32[]{:S(2)}, u32[]{:S(2)}) collective-permute-start(f32[112,256]{1,0:T(8,128)S(1)} %pad_maximum_fusion.3), channel_id=1, source_target_pairs={{1,2},{2,1},{3,4},{4,3},{5,6},{6,5},{7,8},{8,7},{9,10},{10,9},{11,... | collective-permute-start | bytes 344072 | tf_op jit(solution)/shard_map/ppermute | solution.py:308
  45.2 2.2 %all-gather.1 = f32[224,256]{1,0:T(8,128)S(1)} all-gather(f32[112,256]{1,0:T(8,128)S(1)} %pad_maximum_fusion.2), channel_id=3, replica_groups={{0,1},{2,3},{4,5},{6,7},{8,9},{10,11},{12,13},{14,15},{16,17},{18,19},{..., dimensions={0}, use_global_device_ids=true | all-gather | bytes 344064 | tf_op jit(solution)/shard_map/all_gather | solution.py:309
  47.3 2.4 %side_bonds.3.before = f32[104,512]{1,0:T(8,128)S(1)} custom-call(s32[2,512]{1,0:T(2,128)S(1)} %stack.6.odd, f32[104,512]{1,0:T(8,128)S(1)} %get-tuple-element.49.before, f32[112,256]{1,0:T(8,128)S(1)} %collective-permute-done.3.first, f32[112,256]{1,0:T(8,128)S(1)} %collective-permute-done.4.second, f32[2,112,256]{2,1,0:T(8,128)S(1)} %bitcast.11, ...), custom_call_target="tpu_custom_call" | custom-call | flops 2555904 | bytes 1000 | tf_op jit(solution)/shard_map/side_bonds/pallas_call | solution.py:310
  49.8 1.4 %collective-permute-done.5.third = f32[112,256]{1,0:T(8,128)S(1)} collective-permute-done((f32[112,256]{1,0:T(8,128)S(1)}, f32[112,256]{1,0:T(8,128)S(1)}, u32[]{:S(2)}, u32[]{:S(2)}) %collective-permute-start.5) | collective-permute-done | bytes 114720 | tf_op jit(solution)/shard_map/ppermute | solution.py:308
  51.1 2.5 %height_bonds.3 = (f32[3,32,512]{2,1,0:T(8,128)}, f32[3,512]{1,0:T(4,128)}, f32[3,32,512]{2,1,0:T(8,128)}, f32[3,512]{1,0:T(4,128)}) custom-call(s32[2,512]{1,0:T(2,128)S(1)} %stack.6.odd, f32[104,512]{1,0:T(8,128)S(1)} %side_bonds.3.before, f32[112,256]{1,0:T(8,128)S(1)} %collective-permute-done.5.third, f32[2,112,256]{2,1,0:T(8,128)S(1)} %bitcast.12, ...), custom_call_target="tpu_custom_call" | custom-call | flops 817889280 | bytes 1500000 | tf_op jit(solution)/shard_map/height_bonds/pallas_call | solution.py:318
  (9 shorter events, 0.1 us)
Async XLA Ops:
  0.6 0.7 %copy-start.3 = (f32[3,512]{1,0:T(4,128)S(1)}, f32[3,512]{1,0:T(4,128)}, u32[]{:S(2)}) copy-start(f32[3,512]{1,0:T(4,128)} %position.7) | copy-start | bytes 18436
  0.7 0.7 %copy-start.9 = (s32[4,256]{1,0:T(4,128)S(1)}, s32[4,256]{1,0:T(4,128)}, u32[]{:S(2)}) copy-start(s32[4,256]{1,0:T(4,128)} %faces.1) | copy-start | bytes 12292
  0.7 0.7 %copy-start.10 = (s32[4,16]{1,0:T(4,128)S(1)}, s32[4,16]{1,0:T(4,128)}, u32[]{:S(2)}) copy-start(s32[4,16]{1,0:T(4,128)} %corners.1) | copy-start | bytes 772
  0.7 0.7 %copy-start.12 = (f32[32]{0:T(128)S(1)}, f32[32]{0:T(128)}, u32[]{:S(2)}) copy-start(f32[32]{0:T(128)} %param.20) | copy-start | bytes 388
  1.4 0.9 %copy-start = (f32[3,32,512]{2,1,0:T(8,128)S(1)}, f32[3,32,512]{2,1,0:T(8,128)}, u32[]{:S(2)}) copy-start(f32[3,32,512]{2,1,0:T(8,128)} %tangent.7) | copy-start | bytes 589828
  2.3 9.1 %copy-start.1 = (f32[12,512]{1,0:T(8,128)S(1)}, f32[12,512]{1,0:T(8,128)}, u32[]{:S(2)}) copy-start(f32[12,512]{1,0:T(8,128)} %stiffness.11) | copy-start | bytes 73732
  2.3 9.1 %copy-start.2 = (f32[12,512]{1,0:T(8,128)S(1)}, f32[12,512]{1,0:T(8,128)}, u32[]{:S(2)}) copy-start(f32[12,512]{1,0:T(8,128)} %rest_length.11) | copy-start | bytes 73732
  2.3 9.2 %copy-start.5 = (f32[3,32,512]{2,1,0:T(8,128)S(1)}, f32[3,32,512]{2,1,0:T(8,128)}, u32[]{:S(2)}) copy-start(f32[3,32,512]{2,1,0:T(8,128)} %basis.3) | copy-start | bytes 589828
  2.3 9.2 %copy-start.6 = (s32[12,512]{1,0:T(8,128)S(1)}, s32[12,512]{1,0:T(8,128)}, u32[]{:S(2)}) copy-start(s32[12,512]{1,0:T(8,128)} %neighbours.1) | copy-start | bytes 73732
  2.3 9.2 %copy-start.7 = (s32[12,512]{1,0:T(8,128)S(1)}, s32[12,512]{1,0:T(8,128)}, u32[]{:S(2)}) copy-start(s32[12,512]{1,0:T(8,128)} %intact.1) | copy-start | bytes 73732
  2.8 10.9 %collective-permute-start = (f32[112,256]{1,0:T(8,128)S(1)}, f32[112,256]{1,0:T(8,128)S(1)}, u32[]{:S(2)}, u32[]{:S(2)}) collective-permute-start(f32[112,256]{1,0:T(8,128)S(1)} %get-tuple-element.32), channel_id=1, source_target_pairs={{32,64},{33,65},{34,66},{35,67},{36,68},{37,69},{38,70},{39,71},{4... | collective-permute-start | bytes 344072 | tf_op jit(solution)/shard_map/ppermute | solution.py:285
  6.3 7.4 %collective-permute-start.1 = (f32[112,256]{1,0:T(8,128)S(1)}, f32[112,256]{1,0:T(8,128)S(1)}, u32[]{:S(2)}, u32[]{:S(2)}) collective-permute-start(f32[112,256]{1,0:T(8,128)S(1)} %get-tuple-element.33), channel_id=1, source_target_pairs={{0,32},{1,33},{2,34},{3,35},{4,36},{5,37},{6,38},{7,39},{8,40},{9,... | collective-permute-start | bytes 344072 | tf_op jit(solution)/shard_map/ppermute | solution.py:286
  13.7 14.8 %collective-permute-start.2 = (f32[112,256]{1,0:T(8,128)S(1)}, f32[112,256]{1,0:T(8,128)S(1)}, u32[]{:S(2)}, u32[]{:S(2)}) collective-permute-start(f32[112,256]{1,0:T(8,128)S(1)} %pad_maximum_fusion.1), channel_id=1, source_target_pairs={{1,2},{2,1},{3,4},{4,3},{5,6},{6,5},{7,8},{8,7},{9,10},{10,9},{11,... | collective-permute-start | bytes 344072 | tf_op jit(solution)/shard_map/ppermute | solution.py:308
  26.1 2.4 %copy-start.4 = (f32[3,32,512]{2,1,0:T(8,128)S(1)}, f32[3,32,512]{2,1,0:T(8,128)}, u32[]{:S(2)}) copy-start(f32[3,32,512]{2,1,0:T(8,128)} %tangent_vel.1) | copy-start | bytes 589828
  26.1 2.4 %copy-start.8 = (f32[3,512]{1,0:T(4,128)S(1)}, f32[3,512]{1,0:T(4,128)}, u32[]{:S(2)}) copy-start(f32[3,512]{1,0:T(4,128)} %velocity.1) | copy-start | bytes 18436
  26.1 2.5 %copy-start.11 = (f32[512]{0:T(512)S(1)}, f32[512]{0:T(512)}, u32[]{:S(2)}) copy-start(f32[512]{0:T(512)} %param.18) | copy-start | bytes 6148
  30.6 8.0 %collective-permute-start.3 = (f32[112,256]{1,0:T(8,128)S(1)}, f32[112,256]{1,0:T(8,128)S(1)}, u32[]{:S(2)}, u32[]{:S(2)}) collective-permute-start(f32[112,256]{1,0:T(8,128)S(1)} %get-tuple-element.44), channel_id=1, source_target_pairs={{32,64},{33,65},{34,66},{35,67},{36,68},{37,69},{38,70},{39,71},{4... | collective-permute-start | bytes 344072 | tf_op jit(solution)/shard_map/ppermute | solution.py:285
  34.6 6.8 %collective-permute-start.4 = (f32[112,256]{1,0:T(8,128)S(1)}, f32[112,256]{1,0:T(8,128)S(1)}, u32[]{:S(2)}, u32[]{:S(2)}) collective-permute-start(f32[112,256]{1,0:T(8,128)S(1)} %get-tuple-element.45), channel_id=1, source_target_pairs={{0,32},{1,33},{2,34},{3,35},{4,36},{5,37},{6,38},{7,39},{8,40},{9,... | collective-permute-start | bytes 344072 | tf_op jit(solution)/shard_map/ppermute | solution.py:286
  41.4 9.7 %collective-permute-start.5 = (f32[112,256]{1,0:T(8,128)S(1)}, f32[112,256]{1,0:T(8,128)S(1)}, u32[]{:S(2)}, u32[]{:S(2)}) collective-permute-start(f32[112,256]{1,0:T(8,128)S(1)} %pad_maximum_fusion.3), channel_id=1, source_target_pairs={{1,2},{2,1},{3,4},{4,3},{5,6},{6,5},{7,8},{8,7},{9,10},{10,9},{11,... | collective-permute-start | bytes 344072 | tf_op jit(solution)/shard_map/ppermute | solution.py:308

commit v6 on v5

--- a/solution.py
+++ b/solution.py
@@ -210,8 +210,19 @@
 
 def height_kernel(last):
     def body(odd, before, third, both, tangent, position, tangent_vel, velocity, mass, stiffness, rest_length, placed, weights, sends, *outs):
-        new_tangent, new_position, new_tangent_vel, new_velocity = outs[:4]
-        total = outs[-1]
+        if last:
+            far, near = outs[:4], outs[4:8]
+            total, sems = outs[8:]
+        else:
+            near, total = outs[:4], outs[-1]
+        new_tangent, new_position, new_tangent_vel, new_velocity = near
+        copies = []
+
+        def send(which, *part):
+            if last:
+                copies.append(pltpu.make_async_copy(near[which].at[part] if part else near[which], far[which].at[part] if part else far[which], sems.at[len(copies)]))
+                copies[-1].start()
+
         tang = tangent.shape[1]
         total[...] = before[...]
         corners = unfold(third[...], partner(both, odd))
@@ -223,10 +234,16 @@
         for c in range(3):
             speed = tangent_vel[c] + pace * total[c * tang : (c + 1) * tang, :]
             new_tangent_vel[c] = speed
+            send(2, c)
             new_tangent[c] = tangent[c] + DT * speed
+            send(0, c)
         speed = velocity[...] + pace * total[3 * tang : 3 * tang + 3, :]
         new_velocity[...] = speed
+        send(3)
         new_position[...] = position[...] + DT * speed
+        send(1)
+        for copy in copies:
+            copy.wait()
         if not last:
             table = halves(stacked(new_tangent[...], new_position[...]))
             pack_len(table, sends, *outs[4:6])
@@ -318,7 +335,10 @@
         out = pl.pallas_call(
             height_kernel(last),
             out_shape=state if last else state + packed,
-            scratch_shapes=[pltpu.VMEM((ROWS, count), jnp.float32)],
+            **({"out_specs": [pl.BlockSpec(memory_space=pl.ANY)] * 4} if last else {}),
+            scratch_shapes=[pltpu.VMEM(one.shape, one.dtype) for one in state if last]
+            + [pltpu.VMEM((ROWS, count), jnp.float32)]
+            + [pltpu.SemaphoreType.DMA((8,)) for _ in range(last)],
             compiler_params=PARAMS,
             cost_estimate=cost(320, bonds, 1500000),
             name="height_bonds",

time: 54 us -> 54.2 us (level)
  no operation moved by 1% of the time
where the time goes in v6:
time: 54.2 us; the launch traced here: 53.8 us
  starting transfers between devices  28 us (52%)
  Pallas kernels  14 us (26%)
  waiting for transfers between devices  4.22 us (8%)
  blocking collectives  4.12 us (8%)
  between operations  1.76 us (3%)
  local copies, waits for them, and re-layouts  1.64 us (3%)
    ppermute x2, starting transfers between devices, on_device(): lax.ppermute(jnp.concatenate([faces_z[:USED], mine]), AXES, matching(stri...  14.1 us
    ppermute x2, starting transfers between devices, on_device(): first = lax.ppermute(messages[0], AXES, matching(strips, levels, 0, 1))  7.46 us
    ppermute x2, starting transfers between devices, on_device(): second = lax.ppermute(messages[1], AXES, matching(strips, levels, 0, 0))  6.47 us
    pallas_call x2, Pallas kernels, on_device(): pl.pallas_call(side_kernel, out_shape=f32(ROWS, count), compiler_params=P...  4.85 us
    pallas_call x2, Pallas kernels, on_device(): pl.pallas_call(height_kernel(last), out_shape=state if last else state +...  4.56 us
    all_gather x2, blocking collectives, on_device(): lax.all_gather(beside, AXES, axis_index_groups=couples(strips, levels))  4.12 us
    ppermute x2, waiting for transfers between devices, on_device(): second = lax.ppermute(messages[1], AXES, matching(strips, levels, 0, 0))  2.82 us
    pallas_call x1, Pallas kernels, on_device(): pl.pallas_call(own_kernel, out_shape=made + (i32(bonds, count), f32(bonds...  2.13 us
  transfers between devices with their start and end apart: 6, of which 2 were waited for; matrix products, arithmetic and copies ran while one was open for 0% of the time, Pallas kernels for 17%

profile of v6, /device:TPU:14, one launch (start us, length us, event | category | flops | bytes accessed | tf_op | source)
XLA Modules:
  0.0 53.8 jit_solution(13384385742665912517)
XLA Ops:
  0.6 0.0 copy-start.3
  0.7 0.0 copy-start.9
  0.7 0.0 copy-start.10
  0.7 0.0 copy-start.12
  0.7 0.1 stack.6.odd
  0.8 0.6 %copy-done.3 = f32[3,512]{1,0:T(4,128)S(1)} copy-done((f32[3,512]{1,0:T(4,128)S(1)}, f32[3,512]{1,0:T(4,128)}, u32[]{:S(2)}) %copy-start.3) | copy-done | bytes 6168
  1.3 0.0 copy-done.9
  1.3 0.0 copy-done.10
  1.4 0.0 copy-done.12
  1.4 0.0 copy-start
  1.4 0.9 %copy-done = f32[3,32,512]{2,1,0:T(8,128)S(1)} copy-done((f32[3,32,512]{2,1,0:T(8,128)S(1)}, f32[3,32,512]{2,1,0:T(8,128)}, u32[]{:S(2)}) %copy-start) | copy-done | bytes 196632
  2.3 0.0 copy-start.1
  2.3 0.0 copy-start.2
  2.3 0.0 copy-start.5
  2.3 0.0 copy-start.6
  2.3 0.0 copy-start.7
  2.3 0.4 first_messages.1
  2.8 3.5 %collective-permute-start = (f32[112,256]{1,0:T(8,128)S(1)}, f32[112,256]{1,0:T(8,128)S(1)}, u32[]{:S(2)}, u32[]{:S(2)}) collective-permute-start(f32[112,256]{1,0:T(8,128)S(1)} %get-tuple-element.32), channel_id=1, source_target_pairs={{32,64},{33,65},{34,66},{35,67},{36,68},{37,69},{38,70},{39,71},{4... | collective-permute-start | bytes 344072 | tf_op jit(solution)/shard_map/ppermute | solution.py:302
  6.3 4.5 %collective-permute-start.1 = (f32[112,256]{1,0:T(8,128)S(1)}, f32[112,256]{1,0:T(8,128)S(1)}, u32[]{:S(2)}, u32[]{:S(2)}) collective-permute-start(f32[112,256]{1,0:T(8,128)S(1)} %get-tuple-element.33), channel_id=1, source_target_pairs={{0,32},{1,33},{2,34},{3,35},{4,36},{5,37},{6,38},{7,39},{8,40},{9,... | collective-permute-start | bytes 344072 | tf_op jit(solution)/shard_map/ppermute | solution.py:303
  11.4 0.0 copy-done.1
  11.4 0.0 copy-done.2
  11.4 0.0 copy-done.5
  11.5 0.0 copy-done.6
  11.5 0.0 copy-done.7
  11.5 2.1 %own_bonds.1 = (f32[104,512]{1,0:T(8,128)S(1)}, f32[104,256]{1,0:T(8,128)S(1)}, f32[104,256]{1,0:T(8,128)S(1)}, s32[12,512]{1,0:T(8,128)S(1)}, f32[12,512]{1,0:T(8,128)S(1)}) custom-call(s32[2,512]{1,0:T(2,128)S(1)} %stack.6.odd, s32[1,1]{1,0:T(1,128)} %bitcast.10.owned, f32[1,32]{1,0:T(1,128)S(1)} %get-tuple-element.34.params, f32[3,32,512]{2,1,0:T(8,128)S(1)} %copy-done, ...), custom_call_target="tpu_custom_call" | custom-call | flops 1308622848 | bytes 1000000 | tf_op jit(solution)/shard_map/own_bonds/pallas_call | solution.py:306
  13.6 0.0 collective-permute-done.first
  13.7 0.0 collective-permute-done.1.second
  13.7 10.4 %collective-permute-start.2 = (f32[112,256]{1,0:T(8,128)S(1)}, f32[112,256]{1,0:T(8,128)S(1)}, u32[]{:S(2)}, u32[]{:S(2)}) collective-permute-start(f32[112,256]{1,0:T(8,128)S(1)} %pad_maximum_fusion.1), channel_id=1, source_target_pairs={{1,2},{2,1},{3,4},{4,3},{5,6},{6,5},{7,8},{8,7},{9,10},{10,9},{11,... | collective-permute-start | bytes 344072 | tf_op jit(solution)/shard_map/ppermute | solution.py:325
  24.1 2.0 %all-gather = f32[224,256]{1,0:T(8,128)S(1)} all-gather(f32[112,256]{1,0:T(8,128)S(1)} %pad_maximum_fusion), channel_id=2, replica_groups={{0,1},{2,3},{4,5},{6,7},{8,9},{10,11},{12,13},{14,15},{16,17},{18,19},{..., dimensions={0}, use_global_device_ids=true | all-gather | bytes 344064 | tf_op jit(solution)/shard_map/all_gather | solution.py:326
  26.1 0.0 copy-start.4
  26.1 0.0 copy-start.8
  26.1 0.0 copy-start.11
  26.1 2.4 %side_bonds.2.before = f32[104,512]{1,0:T(8,128)S(1)} custom-call(s32[2,512]{1,0:T(2,128)S(1)} %stack.6.odd, f32[104,512]{1,0:T(8,128)S(1)} %get-tuple-element.37.before, f32[112,256]{1,0:T(8,128)S(1)} %collective-permute-done.first, f32[112,256]{1,0:T(8,128)S(1)} %collective-permute-done.1.second, f32[2,112,256]{2,1,0:T(8,128)S(1)} %bitcast.13, ...), custom_call_target="tpu_custom_call" | custom-call | flops 2555904 | bytes 1000 | tf_op jit(solution)/shard_map/side_bonds/pallas_call | solution.py:327
  28.5 0.0 collective-permute-done.2.third
  28.5 0.0 copy-done.4
  28.5 0.0 copy-done.8
  28.5 0.0 copy-done.11
  28.5 2.1 %height_bonds.2 = (f32[3,32,512]{2,1,0:T(8,128)S(1)}, f32[3,512]{1,0:T(4,128)S(1)}, f32[3,32,512]{2,1,0:T(8,128)S(1)}, f32[3,512]{1,0:T(4,128)S(1)}, f32[112,256]{1,0:T(8,128)S(1)}, /*index=5*/f32[112,256]{1,0:T(8,128)S(1)}) custom-call(s32[2,512]{1,0:T(2,128)S(1)} %stack.6.odd, f32[104,512]{1,0:T(8,128)S(1)} %side_bonds.2.before, ...), custom_call_target="tpu_custom_call" | custom-call | flops 817889280 | bytes 1500000 | tf_op jit(solution)/shard_map/height_bonds/pallas_call | solution.py:335
  30.6 4.0 %collective-permute-start.3 = (f32[112,256]{1,0:T(8,128)S(1)}, f32[112,256]{1,0:T(8,128)S(1)}, u32[]{:S(2)}, u32[]{:S(2)}) collective-permute-start(f32[112,256]{1,0:T(8,128)S(1)} %get-tuple-element.44), channel_id=1, source_target_pairs={{32,64},{33,65},{34,66},{35,67},{36,68},{37,69},{38,70},{39,71},{4... | collective-permute-start | bytes 344072 | tf_op jit(solution)/shard_map/ppermute | solution.py:302
  34.6 2.0 %collective-permute-start.4 = (f32[112,256]{1,0:T(8,128)S(1)}, f32[112,256]{1,0:T(8,128)S(1)}, u32[]{:S(2)}, u32[]{:S(2)}) collective-permute-start(f32[112,256]{1,0:T(8,128)S(1)} %get-tuple-element.45), channel_id=1, source_target_pairs={{0,32},{1,33},{2,34},{3,35},{4,36},{5,37},{6,38},{7,39},{8,40},{9,... | collective-permute-start | bytes 344072 | tf_op jit(solution)/shard_map/ppermute | solution.py:303
  36.5 2.0 %own_bonds_again.1 = (f32[104,512]{1,0:T(8,128)S(1)}, f32[104,256]{1,0:T(8,128)S(1)}, f32[104,256]{1,0:T(8,128)S(1)}) custom-call(f32[1,32]{1,0:T(1,128)S(1)} %get-tuple-element.34.params, f32[3,32,512]{2,1,0:T(8,128)S(1)} %get-tuple-element.46.tangent, f32[3,512]{1,0:T(4,128)S(1)} %get-tuple-element.47.position, f32[3,32,512]{2,1,0:T(8,128)S(1)} %copy-done.5, ...), custom_call_target="tpu_custom_call" | custom-call | flops 1308622848 | bytes 1000000 | tf_op jit(solution)/shard_map/own_bonds_again/pallas_call | solution.py:314
  38.6 0.0 collective-permute-done.3.first
  38.6 2.8 %collective-permute-done.4.second = f32[112,256]{1,0:T(8,128)S(1)} collective-permute-done((f32[112,256]{1,0:T(8,128)S(1)}, f32[112,256]{1,0:T(8,128)S(1)}, u32[]{:S(2)}, u32[]{:S(2)}) %collective-permute-start.4) | collective-permute-done | bytes 114720 | tf_op jit(solution)/shard_map/ppermute | solution.py:303
  41.4 3.7 %collective-permute-start.5 = (f32[112,256]{1,0:T(8,128)S(1)}, f32[112,256]{1,0:T(8,128)S(1)}, u32[]{:S(2)}, u32[]{:S(2)}) collective-permute-start(f32[112,256]{1,0:T(8,128)S(1)} %pad_maximum_fusion.3), channel_id=1, source_target_pairs={{1,2},{2,1},{3,4},{4,3},{5,6},{6,5},{7,8},{8,7},{9,10},{10,9},{11,... | collective-permute-start | bytes 344072 | tf_op jit(solution)/shard_map/ppermute | solution.py:325
  45.2 2.2 %all-gather.1 = f32[224,256]{1,0:T(8,128)S(1)} all-gather(f32[112,256]{1,0:T(8,128)S(1)} %pad_maximum_fusion.2), channel_id=3, replica_groups={{0,1},{2,3},{4,5},{6,7},{8,9},{10,11},{12,13},{14,15},{16,17},{18,19},{..., dimensions={0}, use_global_device_ids=true | all-gather | bytes 344064 | tf_op jit(solution)/shard_map/all_gather | solution.py:326
  47.3 2.4 %side_bonds.3.before = f32[104,512]{1,0:T(8,128)S(1)} custom-call(s32[2,512]{1,0:T(2,128)S(1)} %stack.6.odd, f32[104,512]{1,0:T(8,128)S(1)} %get-tuple-element.49.before, f32[112,256]{1,0:T(8,128)S(1)} %collective-permute-done.3.first, f32[112,256]{1,0:T(8,128)S(1)} %collective-permute-done.4.second, f32[2,112,256]{2,1,0:T(8,128)S(1)} %bitcast.11, ...), custom_call_target="tpu_custom_call" | custom-call | flops 2555904 | bytes 1000 | tf_op jit(solution)/shard_map/side_bonds/pallas_call | solution.py:327
  49.8 1.4 %collective-permute-done.5.third = f32[112,256]{1,0:T(8,128)S(1)} collective-permute-done((f32[112,256]{1,0:T(8,128)S(1)}, f32[112,256]{1,0:T(8,128)S(1)}, u32[]{:S(2)}, u32[]{:S(2)}) %collective-permute-start.5) | collective-permute-done | bytes 114720 | tf_op jit(solution)/shard_map/ppermute | solution.py:325
  51.1 2.5 %height_bonds.3 = (f32[3,32,512]{2,1,0:T(8,128)}, f32[3,512]{1,0:T(4,128)}, f32[3,32,512]{2,1,0:T(8,128)}, f32[3,512]{1,0:T(4,128)}) custom-call(s32[2,512]{1,0:T(2,128)S(1)} %stack.6.odd, f32[104,512]{1,0:T(8,128)S(1)} %side_bonds.3.before, f32[112,256]{1,0:T(8,128)S(1)} %collective-permute-done.5.third, f32[2,112,256]{2,1,0:T(8,128)S(1)} %bitcast.12, ...), custom_call_target="tpu_custom_call" | custom-call | flops 817889280 | bytes 1500000 | tf_op jit(solution)/shard_map/height_bonds/pallas_call | solution.py:335
  (9 shorter events, 0.1 us)
Async XLA Ops:
  0.6 0.7 %copy-start.3 = (f32[3,512]{1,0:T(4,128)S(1)}, f32[3,512]{1,0:T(4,128)}, u32[]{:S(2)}) copy-start(f32[3,512]{1,0:T(4,128)} %position.7) | copy-start | bytes 18436
  0.7 0.7 %copy-start.9 = (s32[4,256]{1,0:T(4,128)S(1)}, s32[4,256]{1,0:T(4,128)}, u32[]{:S(2)}) copy-start(s32[4,256]{1,0:T(4,128)} %faces.1) | copy-start | bytes 12292
  0.7 0.7 %copy-start.10 = (s32[4,16]{1,0:T(4,128)S(1)}, s32[4,16]{1,0:T(4,128)}, u32[]{:S(2)}) copy-start(s32[4,16]{1,0:T(4,128)} %corners.1) | copy-start | bytes 772
  0.7 0.7 %copy-start.12 = (f32[32]{0:T(128)S(1)}, f32[32]{0:T(128)}, u32[]{:S(2)}) copy-start(f32[32]{0:T(128)} %param.20) | copy-start | bytes 388
  1.4 0.9 %copy-start = (f32[3,32,512]{2,1,0:T(8,128)S(1)}, f32[3,32,512]{2,1,0:T(8,128)}, u32[]{:S(2)}) copy-start(f32[3,32,512]{2,1,0:T(8,128)} %tangent.7) | copy-start | bytes 589828
  2.3 9.1 %copy-start.1 = (f32[12,512]{1,0:T(8,128)S(1)}, f32[12,512]{1,0:T(8,128)}, u32[]{:S(2)}) copy-start(f32[12,512]{1,0:T(8,128)} %stiffness.11) | copy-start | bytes 73732
  2.3 9.1 %copy-start.2 = (f32[12,512]{1,0:T(8,128)S(1)}, f32[12,512]{1,0:T(8,128)}, u32[]{:S(2)}) copy-start(f32[12,512]{1,0:T(8,128)} %rest_length.11) | copy-start | bytes 73732
  2.3 9.2 %copy-start.5 = (f32[3,32,512]{2,1,0:T(8,128)S(1)}, f32[3,32,512]{2,1,0:T(8,128)}, u32[]{:S(2)}) copy-start(f32[3,32,512]{2,1,0:T(8,128)} %basis.3) | copy-start | bytes 589828
  2.3 9.2 %copy-start.6 = (s32[12,512]{1,0:T(8,128)S(1)}, s32[12,512]{1,0:T(8,128)}, u32[]{:S(2)}) copy-start(s32[12,512]{1,0:T(8,128)} %neighbours.1) | copy-start | bytes 73732
  2.3 9.2 %copy-start.7 = (s32[12,512]{1,0:T(8,128)S(1)}, s32[12,512]{1,0:T(8,128)}, u32[]{:S(2)}) copy-start(s32[12,512]{1,0:T(8,128)} %intact.1) | copy-start | bytes 73732
  2.8 10.9 %collective-permute-start = (f32[112,256]{1,0:T(8,128)S(1)}, f32[112,256]{1,0:T(8,128)S(1)}, u32[]{:S(2)}, u32[]{:S(2)}) collective-permute-start(f32[112,256]{1,0:T(8,128)S(1)} %get-tuple-element.32), channel_id=1, source_target_pairs={{32,64},{33,65},{34,66},{35,67},{36,68},{37,69},{38,70},{39,71},{4... | collective-permute-start | bytes 344072 | tf_op jit(solution)/shard_map/ppermute | solution.py:302
  6.3 7.4 %collective-permute-start.1 = (f32[112,256]{1,0:T(8,128)S(1)}, f32[112,256]{1,0:T(8,128)S(1)}, u32[]{:S(2)}, u32[]{:S(2)}) collective-permute-start(f32[112,256]{1,0:T(8,128)S(1)} %get-tuple-element.33), channel_id=1, source_target_pairs={{0,32},{1,33},{2,34},{3,35},{4,36},{5,37},{6,38},{7,39},{8,40},{9,... | collective-permute-start | bytes 344072 | tf_op jit(solution)/shard_map/ppermute | solution.py:303
  13.7 14.8 %collective-permute-start.2 = (f32[112,256]{1,0:T(8,128)S(1)}, f32[112,256]{1,0:T(8,128)S(1)}, u32[]{:S(2)}, u32[]{:S(2)}) collective-permute-start(f32[112,256]{1,0:T(8,128)S(1)} %pad_maximum_fusion.1), channel_id=1, source_target_pairs={{1,2},{2,1},{3,4},{4,3},{5,6},{6,5},{7,8},{8,7},{9,10},{10,9},{11,... | collective-permute-start | bytes 344072 | tf_op jit(solution)/shard_map/ppermute | solution.py:325
  26.1 2.4 %copy-start.4 = (f32[3,32,512]{2,1,0:T(8,128)S(1)}, f32[3,32,512]{2,1,0:T(8,128)}, u32[]{:S(2)}) copy-start(f32[3,32,512]{2,1,0:T(8,128)} %tangent_vel.1) | copy-start | bytes 589828
  26.1 2.4 %copy-start.8 = (f32[3,512]{1,0:T(4,128)S(1)}, f32[3,512]{1,0:T(4,128)}, u32[]{:S(2)}) copy-start(f32[3,512]{1,0:T(4,128)} %velocity.1) | copy-start | bytes 18436
  26.1 2.5 %copy-start.11 = (f32[512]{0:T(512)S(1)}, f32[512]{0:T(512)}, u32[]{:S(2)}) copy-start(f32[512]{0:T(512)} %param.18) | copy-start | bytes 6148
  30.6 8.0 %collective-permute-start.3 = (f32[112,256]{1,0:T(8,128)S(1)}, f32[112,256]{1,0:T(8,128)S(1)}, u32[]{:S(2)}, u32[]{:S(2)}) collective-permute-start(f32[112,256]{1,0:T(8,128)S(1)} %get-tuple-element.44), channel_id=1, source_target_pairs={{32,64},{33,65},{34,66},{35,67},{36,68},{37,69},{38,70},{39,71},{4... | collective-permute-start | bytes 344072 | tf_op jit(solution)/shard_map/ppermute | solution.py:302
  34.6 6.8 %collective-permute-start.4 = (f32[112,256]{1,0:T(8,128)S(1)}, f32[112,256]{1,0:T(8,128)S(1)}, u32[]{:S(2)}, u32[]{:S(2)}) collective-permute-start(f32[112,256]{1,0:T(8,128)S(1)} %get-tuple-element.45), channel_id=1, source_target_pairs={{0,32},{1,33},{2,34},{3,35},{4,36},{5,37},{6,38},{7,39},{8,40},{9,... | collective-permute-start | bytes 344072 | tf_op jit(solution)/shard_map/ppermute | solution.py:303
  41.4 9.7 %collective-permute-start.5 = (f32[112,256]{1,0:T(8,128)S(1)}, f32[112,256]{1,0:T(8,128)S(1)}, u32[]{:S(2)}, u32[]{:S(2)}) collective-permute-start(f32[112,256]{1,0:T(8,128)S(1)} %pad_maximum_fusion.3), channel_id=1, source_target_pairs={{1,2},{2,1},{3,4},{4,3},{5,6},{6,5},{7,8},{8,7},{9,10},{10,9},{11,... | collective-permute-start | bytes 344072 | tf_op jit(solution)/shard_map/ppermute | solution.py:325
